TPU v7x, 128 devices: a whole 4x4x4 slice. The times are simulated.
128 devices in a mesh: dp: 16 (over z, y), ctx: 8 (over x, core).
Axes of the slice: x: 4, y: 4, z: 4, core: 2. Of those that a mesh axis runs over, the one named last changes fastest.
Arguments:
- history: bfloat16 [16384, 1024], P(('dp', 'ctx')), may hold values from -6 to 6
- grad_output: bfloat16 [16384, 1024], P(('dp', 'ctx')), may hold values from -6 to 6
- lengths: int32 [16, 4], P('dp'), may hold values from 0 to 1024, as said below
- send_order: int32 [16384], P(('dp', 'ctx')), may hold values from 0 to 127, as said below
- place_order: int32 [16384], P(('dp', 'ctx')), may hold values from 0 to 127, as said below
- w_project: bfloat16 [1024, 4096], replicated, may hold values from -0.1875 to 0.1875
- w_out: bfloat16 [1024, 1024], replicated, may hold values from -0.1875 to 0.1875
Outputs:
- output: bfloat16 [16384, 1024], P(('dp', 'ctx'))
- input_grad: bfloat16 [16384, 1024], P(('dp', 'ctx'))
- project_grad: float32 [1024, 4096], P(('dp', 'ctx'))
- mixing_grad: float32 [1024, 1024], P(('dp', 'ctx'))
Inputs may be any that keep to these rules, and one draw needn't show every extreme that they name: For each group, the lengths padded up to multiples of 128 sum to 1024; a zero entry occupies no rows. `send_order`: each device's 128 entries name each of its rows once; entries p * 8 to (p + 1) * 8 - 1 are sent to dp index p. `place_order`: each device's 128 entries are a permutation of 0 to 127.
All inputs are finite; a program needn't handle non-finite values.
Results may differ from a plain program's by a relative error of at most 0.014.
Values may be sent and summed in bfloat16 or wider, within the bound.
No kernel may reach another device: no remote copies, remote signals or barrier semaphores. Data moves between devices by JAX's collectives and lax.ppermute only.
A program may use at most 128 MiB of HBM per device.

v0:
```python
import jax
import jax.numpy as jnp
from jax import lax
from jax.sharding import PartitionSpec as P

HEADS = 16


epsilon = 1e-06
padding_unit = 128


def silu_slope(values):
    sigma = jax.nn.sigmoid(values)
    return sigma * (1.0 + values * (1.0 - sigma))


def layer_norm(values):
    middle = jnp.mean(values, axis=-1, keepdims=True)
    centred = values - middle
    inverse = lax.rsqrt(jnp.mean(centred * centred, axis=-1, keepdims=True) + epsilon)
    return (centred * inverse, inverse)


def norm_back(gradient, normed, inverse):
    first = jnp.mean(gradient, axis=-1, keepdims=True)
    second = jnp.mean(gradient * normed, axis=-1, keepdims=True)
    return inverse * (gradient - first - normed * second)


def row_layout(group_lengths, row_ids):
    blocks = (group_lengths + (padding_unit - 1)) // padding_unit
    ends = jnp.cumsum(blocks * padding_unit)
    starts = ends - blocks * padding_unit
    segment = jnp.sum((ends[None, :] <= row_ids[:, None]).astype(jnp.int32), axis=1)
    onehot = (
        segment[:, None] == jnp.arange(group_lengths.shape[0], dtype=jnp.int32)[None, :]
    ).astype(jnp.int32)
    position = row_ids - jnp.sum(onehot * starts[None, :], axis=1)
    live = position < jnp.sum(onehot * group_lengths[None, :], axis=1)
    return (segment, position, live)


def attend_rows(query_rows, key_rows, value_rows, visible, score_scale):
    scores = (
        jnp.einsum("rhd,lhd->hrl", query_rows, key_rows, preferred_element_type=jnp.float32)
        * score_scale
    )
    weights = jnp.where(visible[None], jax.nn.silu(scores), 0.0).astype(jnp.bfloat16)
    return jnp.einsum("hrl,lhd->rhd", weights, value_rows, preferred_element_type=jnp.float32)


def attend_back(query_rows, key_rows, value_rows, visible, score_scale, grad_att):
    scores = (
        jnp.einsum("rhd,lhd->hrl", query_rows, key_rows, preferred_element_type=jnp.float32)
        * score_scale
    )
    weights = jnp.where(visible[None], jax.nn.silu(scores), 0.0).astype(jnp.bfloat16)
    grad_weights = jnp.einsum(
        "rhd,lhd->hrl", grad_att, value_rows, preferred_element_type=jnp.float32
    )
    grad_scores = (
        jnp.where(visible[None], grad_weights * silu_slope(scores), 0.0) * score_scale
    ).astype(jnp.bfloat16)
    grad_query = jnp.einsum(
        "hrl,lhd->rhd", grad_scores, key_rows, preferred_element_type=jnp.float32
    )
    grad_key = jnp.einsum(
        "hrl,rhd->lhd", grad_scores, query_rows, preferred_element_type=jnp.float32
    )
    grad_value = jnp.einsum("hrl,rhd->lhd", weights, grad_att, preferred_element_type=jnp.float32)
    return (grad_query, grad_key, grad_value)


def local(history, grad_output, lengths, send_order, place_order, w_project, w_out):
    rows_dev = history.shape[0]
    model_width = history.shape[1]
    ctx_count = lax.axis_size("ctx")
    group_rows = ctx_count * rows_dev
    head_width = model_width // HEADS
    score_scale = head_width ** (-0.5)
    arrived = (
        lax.all_to_all(history[send_order], "dp", split_axis=0, concat_axis=0, tiled=True),
        lax.all_to_all(grad_output[send_order], "dp", split_axis=0, concat_axis=0, tiled=True),
    )
    inputs = arrived[0][place_order]
    upstream = arrived[1][place_order]
    row_ids = jnp.arange(group_rows, dtype=jnp.int32)
    segment, position, live = row_layout(lengths[0], row_ids)
    ctx_index = lax.axis_index("ctx")
    offset = ctx_index * rows_dev
    own_segment = lax.dynamic_slice_in_dim(segment, offset, rows_dev)
    own_position = lax.dynamic_slice_in_dim(position, offset, rows_dev)
    own_live = lax.dynamic_slice_in_dim(live, offset, rows_dev)
    visible = (
        (own_segment[:, None] == segment[None, :])
        & (position[None, :] <= own_position[:, None])
        & own_live[:, None]
    )
    normed, inverse = layer_norm(inputs.astype(jnp.float32))
    normed_bf = normed.astype(jnp.bfloat16)
    pre = jnp.dot(normed_bf, w_project, preferred_element_type=jnp.float32)
    proj = jax.nn.silu(pre).astype(jnp.bfloat16)
    gate_rows = proj[:, :model_width]
    query_rows = proj[:, 2 * model_width : 3 * model_width].reshape(rows_dev, HEADS, head_width)
    empty_query = jnp.zeros((rows_dev, HEADS, head_width), jnp.float32)
    gathered = (
        lax.all_gather(proj[:, model_width : 2 * model_width], "ctx", axis=0, tiled=True),
        lax.all_gather(proj[:, 3 * model_width :], "ctx", axis=0, tiled=True),
    )
    value_all = gathered[0].reshape(group_rows, HEADS, head_width)
    key_all = gathered[1].reshape(group_rows, HEADS, head_width)

    def gather_piece(step_index):
        start = step_index * rows_dev
        key_piece = lax.dynamic_slice_in_dim(key_all, start, rows_dev, 0)
        value_piece = lax.dynamic_slice_in_dim(value_all, start, rows_dev, 0)
        mask_piece = lax.dynamic_slice_in_dim(visible, start, rows_dev, 1)
        return (key_piece, value_piece, mask_piece)

    def forward_gathered(step_index, carried):
        key_piece, value_piece, mask_piece = gather_piece(step_index)
        return carried + attend_rows(query_rows, key_piece, value_piece, mask_piece, score_scale)

    attended = lax.fori_loop(0, ctx_count, forward_gathered, empty_query)
    attended = attended.reshape(rows_dev, model_width)
    zvalue, zinverse = layer_norm(attended)
    hidden = (zvalue * gate_rows.astype(jnp.float32)).astype(jnp.bfloat16)
    packed_out = (
        jnp.dot(hidden, w_out, preferred_element_type=jnp.float32) + inputs.astype(jnp.float32)
    ).astype(jnp.bfloat16)
    grad_hidden = lax.dot_general(
        upstream, w_out, (((1,), (1,)), ((), ())), preferred_element_type=jnp.float32
    )
    mixing_part = lax.dot_general(
        hidden, upstream, (((0,), (0,)), ((), ())), preferred_element_type=jnp.float32
    )
    grad_z = grad_hidden * gate_rows.astype(jnp.float32)
    grad_gate = grad_hidden * zvalue
    grad_att = (
        norm_back(grad_z, zvalue, zinverse)
        .astype(jnp.bfloat16)
        .reshape(rows_dev, HEADS, head_width)
    )

    def back_gathered(step_index, carried):
        key_piece, value_piece, mask_piece = gather_piece(step_index)
        start = step_index * rows_dev
        piece_query, piece_key, piece_value = attend_back(
            query_rows, key_piece, value_piece, mask_piece, score_scale, grad_att
        )
        return (
            carried[0] + piece_query,
            lax.dynamic_update_slice_in_dim(carried[1], piece_key, start, 0),
            lax.dynamic_update_slice_in_dim(carried[2], piece_value, start, 0),
        )

    empty_rows = jnp.zeros((group_rows, HEADS, head_width), jnp.float32)
    grad_query, grad_key_all, grad_value_all = lax.fori_loop(
        0, ctx_count, back_gathered, (empty_query, empty_rows, empty_rows)
    )
    key_terms = jnp.concatenate(
        [
            grad_key_all.reshape(group_rows, model_width),
            grad_value_all.reshape(group_rows, model_width),
        ],
        axis=1,
    )
    own_terms = lax.psum_scatter(
        key_terms.astype(jnp.bfloat16), "ctx", scatter_dimension=0, tiled=True
    ).astype(jnp.float32)
    grad_key = own_terms[:, :model_width]
    grad_value = own_terms[:, model_width:]
    grad_pre = (
        jnp.concatenate(
            [grad_gate, grad_value, grad_query.reshape(rows_dev, model_width), grad_key], axis=1
        )
        * silu_slope(pre)
    ).astype(jnp.bfloat16)
    project_part = lax.dot_general(
        normed_bf, grad_pre, (((0,), (0,)), ((), ())), preferred_element_type=jnp.float32
    )
    grad_normed = lax.dot_general(
        grad_pre, w_project, (((1,), (1,)), ((), ())), preferred_element_type=jnp.float32
    )
    packed_grad = (norm_back(grad_normed, normed, inverse) + upstream.astype(jnp.float32)).astype(
        jnp.bfloat16
    )
    project_grad, mixing_grad = (
        lax.psum_scatter(project_part, ("dp", "ctx"), scatter_dimension=0, tiled=True),
        lax.psum_scatter(mixing_part, ("dp", "ctx"), scatter_dimension=0, tiled=True),
    )
    back_out = jnp.zeros_like(packed_out).at[place_order].set(packed_out)
    back_grad = jnp.zeros_like(packed_grad).at[place_order].set(packed_grad)
    returned = (
        lax.all_to_all(back_out, "dp", split_axis=0, concat_axis=0, tiled=True),
        lax.all_to_all(back_grad, "dp", split_axis=0, concat_axis=0, tiled=True),
    )
    output = jnp.zeros_like(history).at[send_order].set(returned[0])
    input_grad = jnp.zeros_like(history).at[send_order].set(returned[1])
    return (output, input_grad, project_grad, mixing_grad)


def solution(mesh):
    placed = (
        P(("dp", "ctx"), None),
        P(("dp", "ctx"), None),
        P("dp", None),
        P(("dp", "ctx")),
        P(("dp", "ctx")),
        P(),
        P(),
    )
    return jax.shard_map(
        local,
        mesh=mesh,
        in_specs=placed,
        out_specs=(
            P(("dp", "ctx"), None),
            P(("dp", "ctx"), None),
            P(("dp", "ctx"), None),
            P(("dp", "ctx"), None),
        ),
        check_vma=False,
    )
```

profile of v0, /device:TPU:6, one launch (start us, length us, event | category | flops | bytes accessed | tf_op | source)
XLA Modules:
  0.0 1549.0 jit_solution(4699199210324219441)
XLA Ops:
  8.0 2.7 gather_fusion
  10.7 8.0 all-to-all-start
  18.9 8.6 all-to-all-done
  28.7 6.1 multiply_convert_fusion
  37.6 1.6 gather_fusion.2
  39.1 3.5 all-to-all-start.2
  44.3 7.1 all-to-all-done.2
  53.4 4.8 all-gather.5.cloned.1.call-done
  58.2 4.0 copy.54
  62.1 23.6 %all-gather.3.cloned.1.call-done = bf16[1024,1024]{1,0:T(8,128)(2,1)} async-done(((bf16[128,1024]{1,0:T(8,128)(2,1)}), bf16[1024,1024]{1,0:T(8,128)(2,1)}) %all-gather.3.cloned.1.call-update) | async-done | bytes 2097168 | tf_op jit(solution)/shard_map/all_gather | solution.py:108
  85.7 4.0 copy.53
  89.7 21.7 %while.32 = (s32[]{:T(128)}, f32[128,16,64]{0,2,1:T(8,128)S(1)}, bf16[1024,16,64]{0,2,1:T(8,128)(2,1)}, pred[128,1024]{1,0:T(8,128)(4,1)}, bf16[1024,16,64]{0,2,...) while((s32[]{:T(128)}, f32[128,16,64]{0,2,1:T(8,128)S(1)}, ...), condition=%wide.region_7.8_spmd.clone, body=%wide.region_6.7_spmd.clone.sunk | while | flops 69206024 | bytes 1918632 | solution.py:125
  90.5 1.8 fusion.111
  93.2 1.8 fusion.111
  95.9 1.8 fusion.111
  98.6 1.8 fusion.111
  101.4 1.8 fusion.111
  104.1 1.8 fusion.111
  106.8 1.8 fusion.111
  109.5 1.8 fusion.111
  112.7 2.1 fusion.58
  114.8 2.1 multiply_convert_fusion.1
  117.8 1.7 broadcast_in_dim.94.clone
  119.4 1.6 broadcast_in_dim.94
  121.1 84.3 %while.33 = (s32[]{:T(128)}, f32[128,16,64]{0,2,1:T(8,128)}, bf16[1024,16,64]{0,2,1:T(8,128)(2,1)}, bf16[1024,16,64]{0,2,1:T(8,128)(2,1)}, bf16[1024,16,64]{0,2,...) while((s32[]{:T(128)}, f32[128,16,64]{0,2,1:T(8,128)}, ...), condition=%wide.region_15.16_spmd.clone, body=%wide.region_14.15_spmd.clone.sunk | while | flops 172752896 | bytes 23429500 | solution.py:159
  121.9 2.8 add_multiply_fusion.2
  124.7 1.6 copy.72
  126.3 1.5 fusion.120
  132.4 2.8 add_multiply_fusion.2
  135.3 1.6 copy.72
  143.0 2.8 add_multiply_fusion.2
  145.8 1.6 copy.72
  147.4 1.5 fusion.120
  153.5 2.8 add_multiply_fusion.2
  156.3 1.6 copy.72
  157.9 1.5 fusion.120
  164.1 2.8 add_multiply_fusion.2
  166.9 1.6 copy.72
  168.5 1.5 fusion.120
  174.6 2.8 add_multiply_fusion.2
  177.4 1.6 copy.72
  179.0 1.5 fusion.120
  185.1 2.8 add_multiply_fusion.2
  188.0 1.6 copy.72
  195.7 2.8 add_multiply_fusion.2
  198.5 1.6 copy.72
  205.3 3.9 copy.60
  209.3 3.9 copy.59
  213.2 4.7 pad_maximum_fusion
  218.9 2.7 fusion.74
  223.7 29.9 %reduce-scatter.4.cloned.1.call-done = bf16[128,2048]{1,0:T(8,128)(2,1)} async-done(((bf16[1024,2048]{1,0:T(8,128)(2,1)}), bf16[128,2048]{1,0:T(8,128)(2,1)}) %reduce-scatter.4.cloned.1.call-update) | async-done | bytes 524304 | tf_op jit(solution)/shard_map/reduce_scatter | solution.py:169
  254.8 2.5 fusion.33
  257.2 8.2 fusion.67
  265.4 2.1 fusion.34
  267.5 2.2 scatter_custom_fusion
  269.8 7.2 all-to-all-start.1
  276.9 7.1 fusion.71
  284.0 2.6 scatter_custom_fusion.2
  286.6 7.2 all-to-all-start.3
  293.8 2.2 scatter_custom_fusion.1
  296.0 7.9 all-to-all-done.3
  303.9 1.8 scatter_custom_fusion.3
  305.7 575.1 %reduce-scatter.8.cloned.1.call-done = f32[8,1024]{1,0:T(8,128)} async-done(((f32[1024,1024]{1,0:T(8,128)}), f32[8,1024]{1,0:T(8,128)}) %reduce-scatter.8.cloned.1.call-update) | async-done | bytes 32784 | tf_op jit(solution)/shard_map/reduce_scatter | solution.py:191
  880.8 661.6 %reduce-scatter.6.cloned.1.call-done = f32[8,4096]{1,0:T(8,128)} async-done(((f32[1024,4096]{1,0:T(8,128)}), f32[8,4096]{1,0:T(8,128)}) %reduce-scatter.6.cloned.1.call-update) | async-done | bytes 131088 | tf_op jit(solution)/shard_map/reduce_scatter | solution.py:190
  (224 shorter events, 62.4 us)
Async XLA Ops:
  7.2 105.5 %copy-start = (bf16[1024,1024]{1,0:T(8,128)(2,1)S(1)}, bf16[1024,1024]{1,0:T(8,128)(2,1)}, u32[]{:S(2)}) copy-start(bf16[1024,1024]{1,0:T(8,128)(2,1)} %param.17) | copy-start | bytes 6291460
  7.2 11.7 copy-start.15
  10.7 16.7 %all-to-all-start = ((bf16[16,8,1024]{2,1,0:T(8,128)(2,1)}), bf16[16,8,1024]{2,1,0:T(8,128)(2,1)S(1)}, u32[]{:S(2)}, u32[]{:S(2)}) async-start(bf16[16,8,1024]{2,1,0:T(8,128)(2,1)} %bitcast), calls=%async_computation | async-start | bytes 524288 | tf_op jit(solution)/shard_map/all_to_all | solution.py:83
  18.8 39.4 %all-gather.5.cloned.1.call-start = ((), (), s32[]{:S(2)}) async-start(), calls=%async_computation.8 | async-start | bytes 2359296 | tf_op jit(solution)/shard_map/all_gather | solution.py:109
  34.8 2.7 copy-start.4
  36.8 5.9 copy-start.14
  36.8 48.9 %all-gather.3.cloned.1.call-start = ((), (), s32[]{:S(2)}) async-start(), calls=%async_computation.7 | async-start | bytes 2359296 | tf_op jit(solution)/shard_map/all_gather | solution.py:108
  39.1 12.2 all-to-all-start.2
  42.7 210.9 %reduce-scatter.4.cloned.1.call-start = ((), (), s32[]{:S(2)}) async-start(), calls=%async_computation.9 | async-start | bytes 4718592 | tf_op jit(solution)/shard_map/reduce_scatter | solution.py:169
  52.2 60.5 %copy-start.9 = (bf16[128,1024]{1,0:T(8,128)(2,1)}, bf16[128,1024]{1,0:T(8,128)(2,1)S(1)}, u32[]{:S(2)}) copy-start(bf16[128,1024]{1,0:T(8,128)(2,1)S(1)} %gather_fusion.3) | copy-start | bytes 786436
  112.7 2.1 copy-start.8
  121.1 3.7 copy-start.5
  126.3 1.6 copy-start.1
  126.3 2.8 copy-start.7
  126.3 2.8 copy-start.16
  129.1 1.3 copy-start.2
  129.2 1.2 copy-start.6
  131.6 3.7 copy-start.5
  136.8 1.6 copy-start.1
  136.8 2.8 copy-start.7
  136.9 2.8 copy-start.16
  139.7 1.2 copy-start.2
  139.7 1.2 copy-start.6
  142.1 3.7 copy-start.5
  147.4 1.6 copy-start.1
  147.4 2.8 copy-start.7
  147.4 2.8 copy-start.16
  150.2 1.2 copy-start.2
  150.2 1.2 copy-start.6
  152.7 3.7 copy-start.5
  157.9 1.6 copy-start.1
  157.9 2.8 copy-start.7
  157.9 2.8 copy-start.16
  160.7 1.3 copy-start.2
  160.8 1.3 copy-start.6
  163.2 3.7 copy-start.5
  168.5 1.6 copy-start.1
  168.5 2.8 copy-start.7
  168.5 2.8 copy-start.16
  171.3 1.2 copy-start.2
  171.3 1.2 copy-start.6
  173.8 3.7 copy-start.5
  179.0 1.6 copy-start.1
  179.0 2.8 copy-start.7
  179.0 2.8 copy-start.16
  181.8 1.3 copy-start.2
  181.9 1.2 copy-start.6
  184.3 3.7 copy-start.5
  189.5 1.6 copy-start.1
  189.5 2.8 copy-start.7
  189.6 2.8 copy-start.16
  192.4 1.2 copy-start.2
  192.4 1.2 copy-start.6
  194.8 3.7 copy-start.5
  200.0 1.6 copy-start.1
  200.1 2.8 copy-start.7
  200.1 2.8 copy-start.16
  202.9 1.2 copy-start.2
  202.9 1.2 copy-start.6
  217.9 662.9 %reduce-scatter.8.cloned.1.call-start = ((), (), s32[]{:S(2)}) async-start(), calls=%async_computation.11 | async-start | bytes 4227072 | tf_op jit(solution)/shard_map/reduce_scatter | solution.py:191
  221.6 1320.8 %reduce-scatter.6.cloned.1.call-start = ((), (), s32[]{:S(2)}) async-start(), calls=%async_computation.10 | async-start | bytes 16908288 | tf_op jit(solution)/shard_map/reduce_scatter | solution.py:190
  253.5 1.2 copy-start.12
  269.8 16.9 %all-to-all-start.1 = ((bf16[16,8,1024]{2,1,0:T(8,128)(2,1)}), bf16[16,8,1024]{2,1,0:T(8,128)(2,1)}, u32[]{:S(2)}, u32[]{:S(2)}) async-start(bf16[16,8,1024]{2,1,0:T(8,128)(2,1)} %bitcast.129), calls=%async_computation.1 | async-start | bytes 524288 | tf_op jit(solution)/shard_map/all_to_all | solution.py:196
  286.6 17.3 %all-to-all-start.3 = ((bf16[16,8,1024]{2,1,0:T(8,128)(2,1)}), bf16[16,8,1024]{2,1,0:T(8,128)(2,1)S(1)}, u32[]{:S(2)}, u32[]{:S(2)}) async-start(bf16[16,8,1024]{2,1,0:T(8,128)(2,1)} %bitcast.19), calls=%async_computation.4 | async-start | bytes 524288 | tf_op jit(solution)/shard_map/all_to_all | solution.py:197
  (4 other events, 4.1 us)
Sparse Core Ops, SparseCore 0:
  36.9 21.1 all-gather.4
  59.9 25.7 all-gather.2
  218.0 35.4 reduce-scatter.3
  256.3 624.4 reduce-scatter.7
  883.7 658.6 reduce-scatter.5
where the time goes:
time: 1570 us; the launch traced here: 1550 us
  waiting for transfers between devices  1320 us (84%)
  matrix products  107 us (7%)
  local copies, waits for them, and re-layouts  66.6 us (4%)
  starting transfers between devices  26.3 us (2%)
    reduce_scatter x1, waiting for transfers between devices, local(): lax.psum_scatter(project_part, ('dp', 'ctx'), scatter_dimension=0, tiled=...  662 us
    reduce_scatter x1, waiting for transfers between devices, local(): lax.psum_scatter(mixing_part, ('dp', 'ctx'), scatter_dimension=0, tiled=T...  575 us
  transfers between devices with their start and end apart: 9, of which 8 were waited for; matrix products, arithmetic and copies ran while one was open for 3% of the time, Pallas kernels for 0%

commit v1 on v0

v1 whole, which is shorter than its diff:
```python
import jax
import jax.numpy as jnp
from jax import lax
from jax.experimental import pallas as pl
from jax.experimental.pallas import tpu as pltpu
from jax.sharding import PartitionSpec as P


D = 1024
WIDE = 128
HEAD = 64
N_DP = 16
N_CTX = 8
R = 128
GROUP = 1024
BLOCK = 256
EPS = 1e-6
BF = jnp.bfloat16
F32 = jnp.float32
NN = (((1,), (0,)), ((), ()))
NT = (((1,), (1,)), ((), ()))


def dot(a, b, dims=NN):
    return lax.dot_general(a, b, dims, preferred_element_type=F32)


def sigmoid(v):
    return 0.5 * jnp.tanh(0.5 * v) + 0.5


def iota(shape, dim):
    return lax.broadcasted_iota(jnp.int32, shape, dim)


def row_norm(values):
    centred = values - jnp.mean(values, axis=-1, keepdims=True)
    inverse = lax.rsqrt(jnp.mean(centred * centred, axis=-1, keepdims=True) + EPS)
    return centred * inverse, inverse


def call(body, outs, *args, smem=0, scratch=()):
    specs = [pl.BlockSpec(memory_space=pltpu.SMEM)] * smem
    specs += [pl.BlockSpec(memory_space=pltpu.VMEM)] * (len(args) - smem)
    return pl.pallas_call(
        body,
        out_shape=[jax.ShapeDtypeStruct(s, t) for s, t in outs],
        in_specs=specs,
        out_specs=[pl.BlockSpec(memory_space=pltpu.VMEM)] * len(outs),
        scratch_shapes=list(scratch),
        compiler_params=pltpu.CompilerParams(vmem_limit_bytes=48 * 1024 * 1024),
    )(*args)


REL = [(0, 0), (0, 1), (1, 0), (1, 1), (2, 0), (2, 1), (3, 0), (3, 1)]


def place_of(ctx, rel):
    chip = lax.rem((ctx >> 1) + rel[0], 4)
    return chip * 2 + ((ctx & 1) ^ rel[1])


def send(x, step, flip):
    pairs = [(2 * a + b, 2 * ((a + step) % 4) + (b ^ flip)) for a in range(4) for b in range(2)]
    return lax.ppermute(x, "ctx", pairs)


def ring_gather(x):
    half = x.shape[0] // 2
    up = send(x, 3, 0)
    down = send(x, 1, 0)
    far = (send(up[:half], 3, 0), send(down[half:], 1, 0))
    return [
        x,
        send(x, 0, 1),
        up,
        send(up, 0, 1),
        far[0],
        far[1],
        send(far[0], 0, 1),
        send(far[1], 0, 1),
        down,
        send(down, 0, 1),
    ]


def join(refs):
    far = [jnp.concatenate([refs[i][...], refs[i + 1][...]], axis=0) for i in (4, 6)]
    return [refs[0][...], refs[1][...], refs[2][...], refs[3][...], *far, refs[8][...], refs[9][...]]


def exchange(parts):
    got = {(0, 0): parts[0]}
    for part, (step, flip) in zip(parts[1:], REL[1:]):
        got[((4 - step) % 4, flip)] = send(part, step, flip)
    return [got[rel] for rel in REL]


def at(index):
    return pl.ds(pl.multiple_of(index * R, R), R)


def pack_kernel(hist, gout, order, out):
    xn = row_norm(hist[...].astype(F32))[0].astype(BF)
    pick = (order[...] == iota((R, R), 1)).astype(BF)
    a = dot(pick, xn).reshape(N_DP, 8, D)
    b = dot(pick, gout[...]).reshape(N_DP, 8, D)
    out[...] = jnp.concatenate([a, b], axis=1).reshape(2 * R, D).astype(BF)


def place_kernel(recv, place, xt, up):
    at_row = (place[...] >> 3) * 16 + (place[...] & 7)
    lanes = iota((R, 2 * R), 1)
    x = dot((at_row == lanes).astype(BF), recv[...])
    xt[...] = x.T.astype(BF)
    up[...] = dot((at_row + 8 == lanes).astype(BF), recv[...]).astype(BF)


def first_visible(lengths):
    rows = iota((1, GROUP), 1)
    low = jnp.full((1, GROUP), 1 << 20, jnp.int32)
    start = jnp.int32(0)
    for j in range(4):
        length = lengths[0, j]
        low = jnp.where((rows >= start) & (rows < start + length), start, low)
        start = start + ((length + 127) >> 7) * 128
    return low


def visible_block(low, rb, tb):
    rs = slice(rb * BLOCK, (rb + 1) * BLOCK)
    keys = iota((BLOCK, BLOCK), 0) + tb * BLOCK
    seen = keys >= low[:, rs]
    if tb == rb:
        seen = seen & (keys <= iota((BLOCK, BLOCK), 1) + rb * BLOCK)
    return seen


def masked_head(x, h, scale=None):
    rows = iota(x.shape, 0)
    x = jnp.where((rows >= h * HEAD) & (rows < (h + 1) * HEAD), x, 0.0)
    if scale is not None:
        x = x * scale
    return x.astype(BF)


def forward_kernel(lengths, ctx, wt, *refs):
    shards = refs[:10]
    xn, pre, proj, att = refs[10:]
    c = ctx[0]
    for value, rel in zip(join(shards), REL):
        xn[:, at(place_of(c, rel))] = value
    for n in range(GROUP // BLOCK):
        cols = slice(n * BLOCK, (n + 1) * BLOCK)
        p = dot(wt[...], xn[:, cols])
        pre[:, cols] = p
        proj[:, cols] = (p * sigmoid(p)).astype(BF)
    low = first_visible(lengths)
    keys = proj[3 * WIDE :, :].astype(F32).T.astype(BF)
    for rb in range(GROUP // BLOCK):
        rs = slice(rb * BLOCK, (rb + 1) * BLOCK)
        query = proj[2 * WIDE : 3 * WIDE, rs].astype(F32)
        for h in range(2):
            hs = slice(h * HEAD, (h + 1) * HEAD)
            vs = slice(WIDE + h * HEAD, WIDE + (h + 1) * HEAD)
            q = masked_head(query, h, 0.125)
            total = jnp.zeros((HEAD, BLOCK), F32)
            for tb in range(rb + 1):
                ts = slice(tb * BLOCK, (tb + 1) * BLOCK)
                s = dot(keys[ts], q)
                w = jnp.where(visible_block(low, rb, tb), s * sigmoid(s), 0.0).astype(BF)
                total = total + dot(proj[vs, ts], w)
            att[hs, rs] = total


def sums_kernel(ctx, w, proj, att, *refs):
    shards = refs[:10]
    gh, sums = refs[10:]
    c = ctx[0]
    for value, rel in zip(join(shards), REL):
        gh[:, at(place_of(c, rel))] = dot(w[...], value, NT)
    a = att[...]
    mean = jnp.mean(a, axis=0, keepdims=True)
    dev = a - mean
    gz = gh[...] * proj[:WIDE, :].astype(F32)
    sums[0:1, :] = mean
    sums[1:2, :] = jnp.sum(dev * dev, axis=0, keepdims=True)
    sums[2:3, :] = jnp.sum(gz, axis=0, keepdims=True)
    sums[3:4, :] = jnp.sum(gz * dev, axis=0, keepdims=True)
    sums[4:8, :] = jnp.zeros((4, GROUP), F32)


def norm_kernel(ctx, proj, att, gh, pre, *refs):
    sums, shards = refs[:8], refs[8:18]
    hidden, (gatt, ggate, mixing) = refs[18:26], refs[26:29]
    c = ctx[0]
    each = [s[...] for s in sums]
    mean = sum(s[0:1, :] for s in each) * (1.0 / N_CTX)
    spread = sum(s[1:2, :] + WIDE * jnp.square(s[0:1, :] - mean) for s in each)
    inverse = lax.rsqrt(spread * (1.0 / D) + EPS)
    first = sum(s[2:3, :] for s in each) * (1.0 / D)
    second = sum(s[3:4, :] + (s[0:1, :] - mean) * s[2:3, :] for s in each) * inverse * (1.0 / D)
    z = (att[...] - mean) * inverse
    gate = proj[:WIDE, :].astype(F32)
    hid = (z * gate).astype(BF)
    gatt[...] = (inverse * (gh[...] * gate - first - z * second)).astype(BF)
    p = pre[:WIDE, :]
    sig = sigmoid(p)
    ggate[...] = (gh[...] * z * (sig * (1.0 + p * (1.0 - sig)))).astype(BF)
    att_hidden = refs[29]
    att_hidden[...] = hid
    total = jnp.zeros((WIDE, D), F32)
    for i, (value, rel) in enumerate(zip(join(shards), REL)):
        piece = att_hidden[:, at(place_of(c, rel))]
        hidden[i][...] = piece
        total = total + dot(piece, value)
    mixing[...] = total.astype(BF)


def backward_kernel(lengths, ctx, pre, proj, gatt, ggate, *refs):
    parts, gp, (dk, dv) = refs[:8], refs[8], refs[9:11]
    c = ctx[0]
    low = first_visible(lengths)
    keys = proj[3 * WIDE :, :].astype(F32).T.astype(BF)
    values = proj[WIDE : 2 * WIDE, :].astype(F32).T.astype(BF)
    dk[...] = jnp.zeros((WIDE, GROUP), F32)
    dv[...] = jnp.zeros((WIDE, GROUP), F32)

    def slope(v):
        sig = sigmoid(v)
        return sig * (1.0 + v * (1.0 - sig))

    gp[:WIDE, :] = ggate[...]
    for rb in range(GROUP // BLOCK):
        rs = slice(rb * BLOCK, (rb + 1) * BLOCK)
        query = proj[2 * WIDE : 3 * WIDE, rs].astype(F32)
        grad = gatt[:, rs].astype(F32)
        for h in range(2):
            hs = slice(h * HEAD, (h + 1) * HEAD)
            q = masked_head(query, h, 0.125)
            g = masked_head(grad, h)
            total = jnp.zeros((HEAD, BLOCK), F32)
            for tb in range(rb + 1):
                ts = slice(tb * BLOCK, (tb + 1) * BLOCK)
                s = dot(keys[ts], q)
                gw = dot(values[ts], g)
                seen = visible_block(low, rb, tb)
                sig = sigmoid(s)
                w = jnp.where(seen, s * sig, 0.0)
                gs = jnp.where(seen, gw * (sig + w * (1.0 - sig)), 0.0).astype(BF)
                dv[hs, ts] += dot(g[hs], w.astype(BF), NT)
                dk[hs, ts] += dot(q[hs], gs, NT)
                total = total + dot(proj[3 * WIDE + h * HEAD : 3 * WIDE + (h + 1) * HEAD, ts], gs)
            qs = slice(2 * WIDE + h * HEAD, 2 * WIDE + (h + 1) * HEAD)
            gp[qs, rs] = (total * 0.125 * slope(pre[qs, rs])).astype(BF)
    gp[WIDE : 2 * WIDE, :] = (dv[...] * slope(pre[WIDE : 2 * WIDE, :])).astype(BF)
    gp[3 * WIDE :, :] = (dk[...] * slope(pre[3 * WIDE :, :])).astype(BF)
    for part, rel in zip(parts, REL):
        part[...] = gp[:, at(place_of(c, rel))]


def project_kernel(xn, gp, out):
    for n in range(4):
        rows = slice(n * BLOCK, (n + 1) * BLOCK)
        out[rows, :] = dot(xn[rows, :], gp[...], NT).astype(BF)


def finish_kernel(ctx, place, w_project, w_out, mixing, *refs):
    hidden, grads, out, (hid, gp) = refs[:8], refs[8:16], refs[16], refs[17:19]
    c = ctx[0]
    for value, grad, rel in zip(hidden, grads, REL):
        src = place_of(c, rel)
        hid[at(src), :] = value[...]
        for kind in range(4):
            gp[at(kind * 8 + src), :] = grad[kind * WIDE : (kind + 1) * WIDE, :]
    back = (place[...] == iota((R, R), 0)).astype(BF)
    o = dot(dot(back, hid[...], NT).astype(BF), w_out[...])
    gx = dot(w_project[...], gp[...])
    gx = dot(back, gx.astype(BF), NT)
    mix = mixing[...].astype(F32)
    parts = [v.reshape(N_DP, 8, D) for v in (o, gx, mix)]
    out[...] = jnp.concatenate(parts, axis=1).reshape(3 * R, D).astype(BF)


def unpack_kernel(recv, hist, gout, order, out, grad, mixing):
    got = recv[...].astype(F32).reshape(N_DP, 24, D)
    back = (order[...] == iota((R, R), 0)).astype(BF)
    o = dot(back, got[:, 0:8].reshape(R, D).astype(BF))
    gx = dot(back, got[:, 8:16].reshape(R, D).astype(BF))
    x = hist[...].astype(F32)
    out[...] = (o + x).astype(BF)
    normed, inverse = row_norm(x)
    first = jnp.mean(gx, axis=-1, keepdims=True)
    second = jnp.mean(gx * normed, axis=-1, keepdims=True)
    grad[...] = (inverse * (gx - first - normed * second) + gout[...].astype(F32)).astype(BF)
    mixing[...] = jnp.sum(got[:, 16:24], axis=0)


def weight_kernel(recv, out):
    total = jnp.sum(recv[...].astype(F32).reshape(N_DP, N_CTX, 8, 4 * WIDE), axis=0)
    for c in range(N_CTX):
        for kind in range(4):
            start = kind * D + c * WIDE
            out[:, start : start + WIDE] = total[c, :, kind * WIDE : (kind + 1) * WIDE]


def local(history, grad_output, lengths, send_order, place_order, w_project, w_out):
    ctx = lax.axis_index("ctx").astype(jnp.int32)
    ctx_s = ctx.reshape(1)
    first = ctx * WIDE
    w_own = jnp.concatenate(
        [lax.dynamic_slice_in_dim(w_project, kind * D + first, WIDE, 1) for kind in range(4)], axis=1
    ).T
    w_out_own = lax.dynamic_slice_in_dim(w_out, first, WIDE, 0)

    (packed,) = call(
        pack_kernel, [((2 * R, D), BF)], history, grad_output, send_order.reshape(R, 1)
    )
    arrived = lax.all_to_all(packed, "dp", split_axis=0, concat_axis=0, tiled=True)
    xt, up = call(
        place_kernel, [((D, R), BF), ((R, D), BF)], arrived, place_order.reshape(R, 1)
    )
    xt_shards = ring_gather(xt)
    up_shards = ring_gather(up)

    xn, pre, proj, att = call(
        forward_kernel,
        [((D, GROUP), BF), ((4 * WIDE, GROUP), F32), ((4 * WIDE, GROUP), BF), ((WIDE, GROUP), F32)],
        lengths,
        ctx_s,
        w_own,
        *xt_shards,
        smem=2,
    )
    gh, sums = call(
        sums_kernel,
        [((WIDE, GROUP), F32), ((8, GROUP), F32)],
        ctx_s,
        w_out_own,
        proj,
        att,
        *up_shards,
        smem=1,
    )
    all_sums = [sums] + [send(sums, step, flip) for step, flip in REL[1:]]
    *hidden, gatt, ggate, mixing = call(
        norm_kernel,
        [((WIDE, R), BF)] * 8 + [((WIDE, GROUP), BF)] * 2 + [((WIDE, D), BF)],
        ctx_s,
        proj,
        att,
        gh,
        pre,
        *all_sums,
        *up_shards,
        smem=1,
        scratch=[pltpu.VMEM((WIDE, GROUP), BF)],
    )
    hidden = exchange(hidden)
    *grads, gp = call(
        backward_kernel,
        [((4 * WIDE, R), BF)] * 8 + [((4 * WIDE, GROUP), BF)],
        lengths,
        ctx_s,
        pre,
        proj,
        gatt,
        ggate,
        smem=2,
        scratch=[pltpu.VMEM((WIDE, GROUP), F32)] * 2,
    )
    grads = exchange(grads)
    (project,) = call(project_kernel, [((D, 4 * WIDE), BF)], xn, gp)
    project = lax.all_to_all(project, ("dp", "ctx"), split_axis=0, concat_axis=0, tiled=True)

    (returned,) = call(
        finish_kernel,
        [((3 * R, D), BF)],
        ctx_s,
        place_order.reshape(1, R),
        w_project,
        w_out,
        mixing,
        *hidden,
        *grads,
        smem=1,
        scratch=[pltpu.VMEM((D, R), BF), pltpu.VMEM((4 * D, R), BF)],
    )
    returned = lax.all_to_all(returned, "dp", split_axis=0, concat_axis=0, tiled=True)
    output, input_grad, mixing_part = call(
        unpack_kernel,
        [((R, D), BF), ((R, D), BF), ((8, D), F32)],
        returned,
        history,
        grad_output,
        send_order.reshape(1, R),
    )
    (project_grad,) = call(weight_kernel, [((8, 4 * D), F32)], project)
    owners = [(d * 8 + c, (2 * c + d // 8) * 8 + d % 8) for d in range(N_DP) for c in range(N_CTX)]
    mixing_grad = lax.ppermute(mixing_part, ("dp", "ctx"), owners)
    return output, input_grad, project_grad, mixing_grad


def solution(mesh):
    rows = P(("dp", "ctx"), None)
    ids = P(("dp", "ctx"))
    return jax.shard_map(
        local,
        mesh=mesh,
        in_specs=(rows, rows, P("dp", None), ids, ids, P(), P()),
        out_specs=(rows, rows, rows, rows),
        check_vma=False,
    )
```

time: 1570 us -> 175 us (0.11); the launches traced: 1550 us -> 173 us
  waiting for transfers between devices: 1320 us -> 58 us
  matrix products: 107 us -> 0 us
  local copies, waits for them, and re-layouts: 66.6 us -> 18.9 us
  starting transfers between devices: 26.3 us -> 62.5 us
  Pallas kernels: 0 us -> 31.1 us
    reduce_scatter x3 -> x0, waiting for transfers between devices: 1270 us -> none  [the longest x1 662 us: local(): lax.psum_scatter(project_part, ('dp', 'ctx'), scatter_dimension=0, tiled=...]
    dot_general x54 -> x0, matrix products: 107 us -> none  [the longest x8 22.6 us: attend_back(): jnp.einsum('rhd,lhd->hrl', query_rows, key_rows, preferred_element_type=j...]
    ppermute x0 -> x40, starting transfers between devices: none -> 44.5 us  [the longest x39 39.2 us: send(): return lax.ppermute(x, 'ctx', pairs)]
    ppermute x0 -> x40, waiting for transfers between devices: none -> 33.9 us  [the longest x39 24 us: send(): return lax.ppermute(x, 'ctx', pairs)]
    pallas_call x0 -> x10, Pallas kernels: none -> 31.1 us  [call(): pl.pallas_call(body, out_shape=[jax.ShapeDtypeStruct(s, t) for s, t in ou...]
    all_gather x2 -> x0, waiting for transfers between devices: 28.3 us -> none  [the longest x1 23.6 us: local(): lax.all_gather(proj[:, model_width:2 * model_width], 'ctx', axis=0, tiled...]
  transfers between devices with their start and end apart: 9 -> 43, of which waited for: 8 -> 15; matrix products, arithmetic and copies ran while one was open for 3% -> 8% of each run, Pallas kernels for 0% -> 6%
where the time goes in v1:
time: 175 us; the launch traced here: 173 us
  starting transfers between devices  62.5 us (36%)
  waiting for transfers between devices  58 us (33%)
  Pallas kernels  31.1 us (18%)
  local copies, waits for them, and re-layouts  18.9 us (11%)
    ppermute x39, starting transfers between devices, send(): return lax.ppermute(x, 'ctx', pairs)  39.2 us
    pallas_call x10, Pallas kernels, call(): pl.pallas_call(body, out_shape=[jax.ShapeDtypeStruct(s, t) for s, t in ou...  31.1 us
    ppermute x39, waiting for transfers between devices, send(): return lax.ppermute(x, 'ctx', pairs)  24 us
    unnamed x41, local copies, waits for them, and re-layouts  13.3 us
    all_to_all x1, waiting for transfers between devices, local(): lax.all_to_all(packed, 'dp', split_axis=0, concat_axis=0, tiled=True)  11.4 us
    all_to_all x1, waiting for transfers between devices, local(): lax.all_to_all(returned, 'dp', split_axis=0, concat_axis=0, tiled=True)  10.6 us
    ppermute x1, waiting for transfers between devices, local(): mixing_grad = lax.ppermute(mixing_part, ('dp', 'ctx'), owners)  9.91 us
    all_to_all x1, starting transfers between devices, local(): lax.all_to_all(packed, 'dp', split_axis=0, concat_axis=0, tiled=True)  8.05 us
  transfers between devices with their start and end apart: 43, of which 15 were waited for; matrix products, arithmetic and copies ran while one was open for 8% of the time, Pallas kernels for 6%

profile of v1, /device:TPU:6, one launch (start us, length us, event | category | flops | bytes accessed | tf_op | source)
XLA Modules:
  0.0 172.8 jit_solution(15021575079755615341)
XLA Ops:
  0.6 0.8 copy.15.order
  1.4 0.9 copy-done.3
  2.4 0.9 copy-done.5
  3.3 1.4 shard_map.102
  4.7 8.0 %all-to-all-start = ((bf16[16,16,1024]{2,1,0:T(8,128)(2,1)}), bf16[16,16,1024]{2,1,0:T(8,128)(2,1)S(1)}, u32[]{:S(2)}, u32[]{:S(2)}) async-start(bf16[16,16,1024]{2,1,0:T(8,128)(2,1)} %bitcast.4), calls=%async_computation | async-start | bytes 1048576 | tf_op jit(solution)/shard_map/all_to_all | solution.py:319
  12.9 11.4 %all-to-all-done = bf16[16,16,1024]{2,1,0:T(8,128)(2,1)S(1)} async-done(((bf16[16,16,1024]{2,1,0:T(8,128)(2,1)}), bf16[16,16,1024]{2,1,0:T(8,128)(2,1)S(1)}, u32[]{:S(2)}, u32[]{:S(2)}) %all-to-all-start) | async-done | bytes 524320 | tf_op jit(solution)/shard_map/all_to_all | solution.py:319
  24.3 0.4 shard_map.103
  24.6 0.9 collective-permute-start.1
  25.5 2.4 %collective-permute-start.4 = (bf16[1024,128]{1,0:T(8,128)(2,1)S(1)}, bf16[1024,128]{1,0:T(8,128)(2,1)}, u32[]{:S(2)}, u32[]{:S(2)}) collective-permute-start(bf16[1024,128]{1,0:T(8,128)(2,1)S(1)} %get-tuple-element.35.refs_0_), channel_id=1, source_target_pairs={{0,2},{1,3},{2,4},{3,5},{4,6},{5,7},{6,0},{7,1},{8,10},{9,11},{10,... | collective-permute-start | bytes 786440 | tf_op jit(solution)/shard_map/ppermute | solution.py:65
  28.0 3.2 %collective-permute-start.13 = (bf16[128,1024]{1,0:T(8,128)(2,1)S(1)}, bf16[128,1024]{1,0:T(8,128)(2,1)S(1)}, u32[]{:S(2)}, u32[]{:S(2)}) collective-permute-start(bf16[128,1024]{1,0:T(8,128)(2,1)S(1)} %get-tuple-element.38.refs_0_.refs_8_), channel_id=1, source_target_pairs={{0,2},{1,3},{2,4},{3,5},{4,6},{5,7},{6,0},{7,1},{8,10},{9,11},{10,... | collective-permute-start | bytes 786440 | tf_op jit(solution)/shard_map/ppermute | solution.py:65
  31.2 4.1 %collective-permute-done.1.refs_2_ = bf16[1024,128]{1,0:T(8,128)(2,1)} collective-permute-done((bf16[1024,128]{1,0:T(8,128)(2,1)S(1)}, bf16[1024,128]{1,0:T(8,128)(2,1)}, u32[]{:S(2)}, u32[]{:S(2)}) %collective-permute-start.1) | collective-permute-done | bytes 262176 | tf_op jit(solution)/shard_map/ppermute | solution.py:65
  35.3 0.9 slice.16
  36.3 0.9 slice.17
  37.2 3.3 %collective-permute-start.5 = (bf16[512,128]{1,0:T(8,128)(2,1)S(1)}, bf16[512,128]{1,0:T(8,128)(2,1)}, u32[]{:S(2)}, u32[]{:S(2)}) collective-permute-start(bf16[512,128]{1,0:T(8,128)(2,1)S(1)} %slice.17), channel_id=1, source_target_pairs={{0,2},{1,3},{2,4},{3,5},{4,6},{5,7},{6,0},{7,1},{8,10},{9,11},{10,... | collective-permute-start | bytes 393224 | tf_op jit(solution)/shard_map/ppermute | solution.py:65
  40.6 0.7 slice.19
  41.3 3.2 %collective-permute-start.14 = (bf16[64,1024]{1,0:T(8,128)(2,1)}, bf16[64,1024]{1,0:T(8,128)(2,1)}, u32[]{:S(2)}, u32[]{:S(2)}) collective-permute-start(bf16[64,1024]{1,0:T(8,128)(2,1)} %slice.19), channel_id=1, source_target_pairs={{0,2},{1,3},{2,4},{3,5},{4,6},{5,7},{6,0},{7,1},{8,10},{9,11},{10,... | collective-permute-start | bytes 393224 | tf_op jit(solution)/shard_map/ppermute | solution.py:65
  44.5 0.7 copy-done.11
  45.1 0.5 collective-permute-start.7
  45.7 0.7 copy-done.9
  46.4 0.4 collective-permute-done.12.refs_4_.refs_12_
  46.9 0.4 collective-permute-done.14.refs_5_.refs_13_
  47.3 0.7 copy-done.13
  48.0 0.5 collective-permute-start.11
  48.5 2.2 %constant_dynamic-slice_fusion.4 = (bf16[1024,128]{1,0:T(8,128)(2,1)}, bf16[1024,128]{1,0:T(8,128)(2,1)}, bf16[1024,128]{1,0:T(8,128)(2,1)}, bf16[1024,128]{1,0:T(8,128)(2,1)}) fusion(bf16[1024,4096]{1,0:T(8,128)(2,1)} %w_project.1, s32[]{:T(128)S(6)} %select_n.15, s32[]{:T(128)S(6)} %select_n.17, s32[]{:T(128)S(6)} %select_n.16, s32[]{:T(128)S(6)} %select_n.18), kind=kLoop, calls=%fused_computation.5 | loop fusion | bytes 2097168 | tf_op jit(solution)/shard_map/dynamic_slice | solution.py:312
  50.7 1.8 %copy.17 = bf16[1024,128]{0,1:T(8,128)(2,1)} copy(bf16[1024,128]{1,0:T(8,128)(2,1)} %get-tuple-element.66) | data formatting | bytes 524288
  52.5 1.8 %copy.18 = bf16[1024,128]{0,1:T(8,128)(2,1)} copy(bf16[1024,128]{1,0:T(8,128)(2,1)} %get-tuple-element.68) | data formatting | bytes 524288
  54.3 1.8 %copy.19 = bf16[1024,128]{0,1:T(8,128)(2,1)} copy(bf16[1024,128]{1,0:T(8,128)(2,1)} %get-tuple-element.67) | data formatting | bytes 524288
  56.1 1.8 %copy.20 = bf16[1024,128]{0,1:T(8,128)(2,1)} copy(bf16[1024,128]{1,0:T(8,128)(2,1)} %get-tuple-element.69) | data formatting | bytes 524288
  57.9 0.6 collective-permute-start.15
  58.8 1.3 maximum_bitcast_fusion.wt
  60.1 6.0 %shard_map.104 = (bf16[1024,1024]{1,0:T(8,128)(2,1)}, f32[512,1024]{1,0:T(8,128)}, bf16[512,1024]{1,0:T(8,128)(2,1)S(1)}, f32[128,1024]{1,0:T(8,128)S(1)}) custom-call(s32[1,4]{1,0:T(1,128)S(1)} %copy-done.15, s32[1]{0:T(128)} %bitcast.ctx, bf16[512,1024]{1,0:T(8,128)(2,1)S(1)} %maximum_bitcast_fusion.wt, bf16[1024,128]{1,0:T(8,128)(2,1)S(1)} %copy-done.8, ...), custom_call_target="tpu_custom_call" | custom-call | tf_op jit(solution)/shard_map/pallas_call | solution.py:45
  66.2 1.9 %shard_map.105 = (f32[128,1024]{1,0:T(8,128)S(1)}, f32[8,1024]{1,0:T(8,128)S(1)}) custom-call(s32[1]{0:T(128)} %bitcast.ctx, bf16[128,1024]{1,0:T(8,128)(2,1)S(1)} %constant_dynamic-slice_fusion.w, bf16[512,1024]{1,0:T(8,128)(2,1)S(1)} %get-tuple-element.36.proj, f32[128,1024]{1,0:T(8,128)S(1)} %get-tuple-element.37.att, ...), custom_call_target="tpu_custom_call" | custom-call | tf_op jit(solution)/shard_map/pallas_call | solution.py:45
  68.2 0.3 collective-permute-start.18
  68.5 3.7 %collective-permute-start.19 = (f32[8,1024]{1,0:T(8,128)S(1)}, f32[8,1024]{1,0:T(8,128)S(1)}, u32[]{:S(2)}, u32[]{:S(2)}) collective-permute-start(f32[8,1024]{1,0:T(8,128)S(1)} %get-tuple-element.41.refs_0_), channel_id=1, source_target_pairs={{0,2},{1,3},{2,4},{3,5},{4,6},{5,7},{6,0},{7,1},{8,10},{9,11},{10,... | collective-permute-start | bytes 98312 | tf_op jit(solution)/shard_map/ppermute | solution.py:65
  72.2 3.0 %collective-permute-start.22 = (f32[8,1024]{1,0:T(8,128)S(1)}, f32[8,1024]{1,0:T(8,128)S(1)}, u32[]{:S(2)}, u32[]{:S(2)}) collective-permute-start(f32[8,1024]{1,0:T(8,128)S(1)} %get-tuple-element.41.refs_0_), channel_id=1, source_target_pairs={{0,5},{1,4},{2,7},{3,6},{4,1},{5,0},{6,3},{7,2},{8,13},{9,12},{10,... | collective-permute-start | bytes 98312 | tf_op jit(solution)/shard_map/ppermute | solution.py:65
  75.1 2.0 %collective-permute-start.23 = (f32[8,1024]{1,0:T(8,128)S(1)}, f32[8,1024]{1,0:T(8,128)S(1)}, u32[]{:S(2)}, u32[]{:S(2)}) collective-permute-start(f32[8,1024]{1,0:T(8,128)S(1)} %get-tuple-element.41.refs_0_), channel_id=1, source_target_pairs={{0,6},{1,7},{2,0},{3,1},{4,2},{5,3},{6,4},{7,5},{8,14},{9,15},{10,... | collective-permute-start | bytes 98312 | tf_op jit(solution)/shard_map/ppermute | solution.py:65
  77.6 2.7 %collective-permute-done.23.refs_6_ = f32[8,1024]{1,0:T(8,128)S(1)} collective-permute-done((f32[8,1024]{1,0:T(8,128)S(1)}, f32[8,1024]{1,0:T(8,128)S(1)}, u32[]{:S(2)}, u32[]{:S(2)}) %collective-permute-start.23) | collective-permute-done | bytes 32800 | tf_op jit(solution)/shard_map/ppermute | solution.py:65
  80.3 1.6 collective-permute-done.24.refs_7_
  81.9 3.3 %shard_map.106 = (bf16[128,128]{1,0:T(8,128)(2,1)S(1)}, bf16[128,128]{1,0:T(8,128)(2,1)S(1)}, bf16[128,128]{1,0:T(8,128)(2,1)S(1)}, bf16[128,128]{1,0:T(8,128)(2...) custom-call(s32[1]{0:T(128)} %bitcast.ctx, ...), custom_call_target="tpu_custom_call" | custom-call | tf_op jit(solution)/shard_map/pallas_call | solution.py:45
  85.2 6.5 %shard_map.107 = (bf16[512,128]{1,0:T(8,128)(2,1)S(1)}, bf16[512,128]{1,0:T(8,128)(2,1)S(1)}, bf16[512,128]{1,0:T(8,128)(2,1)S(1)}, bf16[512,128]{1,0:T(8,128)(2...) custom-call(s32[1,4]{1,0:T(1,128)S(1)} %copy-done.15, ...), custom_call_target="tpu_custom_call" | custom-call | tf_op jit(solution)/shard_map/pallas_call | solution.py:45
  91.8 0.4 collective-permute-start.25
  92.3 0.9 collective-permute-start.27
  93.2 3.5 %collective-permute-start.28 = (bf16[128,128]{1,0:T(8,128)(2,1)S(1)}, bf16[128,128]{1,0:T(8,128)(2,1)S(1)}, u32[]{:S(2)}, u32[]{:S(2)}) collective-permute-start(bf16[128,128]{1,0:T(8,128)(2,1)S(1)} %get-tuple-element.47), channel_id=1, source_target_pairs={{0,4},{1,5},{2,6},{3,7},{4,0},{5,1},{6,2},{7,3},{8,12},{9,13},{10,... | collective-permute-start | bytes 98312 | tf_op jit(solution)/shard_map/ppermute | solution.py:65
  96.7 3.9 %collective-permute-done.26.refs_2_ = bf16[128,128]{1,0:T(8,128)(2,1)S(1)} collective-permute-done((bf16[128,128]{1,0:T(8,128)(2,1)S(1)}, bf16[128,128]{1,0:T(8,128)(2,1)S(1)}, u32[]{:S(2)}, u32[]{:S(2)}) %collective-permute-start.26) | collective-permute-done | bytes 32800 | tf_op jit(solution)/shard_map/ppermute | solution.py:65
  100.7 3.5 %collective-permute-start.31 = (bf16[128,128]{1,0:T(8,128)(2,1)S(1)}, bf16[128,128]{1,0:T(8,128)(2,1)S(1)}, u32[]{:S(2)}, u32[]{:S(2)}) collective-permute-start(bf16[128,128]{1,0:T(8,128)(2,1)S(1)} %get-tuple-element.50), channel_id=1, source_target_pairs={{0,3},{1,2},{2,5},{3,4},{4,7},{5,6},{6,1},{7,0},{8,11},{9,10},{10,... | collective-permute-start | bytes 98312 | tf_op jit(solution)/shard_map/ppermute | solution.py:65
  104.2 1.3 collective-permute-done.29.refs_5_
  105.5 1.1 collective-permute-start.35
  106.6 1.0 collective-permute-start.36
  107.7 4.0 %collective-permute-start.37 = (bf16[512,128]{1,0:T(8,128)(2,1)S(1)}, bf16[512,128]{1,0:T(8,128)(2,1)S(1)}, u32[]{:S(2)}, u32[]{:S(2)}) collective-permute-start(bf16[512,128]{1,0:T(8,128)(2,1)S(1)} %get-tuple-element.59), channel_id=1, source_target_pairs={{0,2},{1,3},{2,4},{3,5},{4,6},{5,7},{6,0},{7,1},{8,10},{9,11},{10,... | collective-permute-start | bytes 393224 | tf_op jit(solution)/shard_map/ppermute | solution.py:65
  111.7 5.5 %collective-permute-done.34.refs_11_ = bf16[512,128]{1,0:T(8,128)(2,1)S(1)} collective-permute-done((bf16[512,128]{1,0:T(8,128)(2,1)S(1)}, bf16[512,128]{1,0:T(8,128)(2,1)S(1)}, u32[]{:S(2)}, u32[]{:S(2)}) %collective-permute-start.34) | collective-permute-done | bytes 131104 | tf_op jit(solution)/shard_map/ppermute | solution.py:65
  117.2 0.4 collective-permute-done.37.refs_14_
  117.6 3.3 %collective-permute-done.38.refs_15_ = bf16[512,128]{1,0:T(8,128)(2,1)S(1)} collective-permute-done((bf16[512,128]{1,0:T(8,128)(2,1)S(1)}, bf16[512,128]{1,0:T(8,128)(2,1)S(1)}, u32[]{:S(2)}, u32[]{:S(2)}) %collective-permute-start.38) | collective-permute-done | bytes 131104 | tf_op jit(solution)/shard_map/ppermute | solution.py:65
  121.0 7.3 %shard_map.108 = bf16[384,1024]{1,0:T(8,128)(2,1)} custom-call(s32[1]{0:T(128)} %bitcast.ctx, s32[1,128]{1,0:T(1,128)S(1)} %bitcast.17, bf16[1024,4096]{1,0:T(8,128)(2,1)} %w_project.1, bf16[1024,1024]{1,0:T(8,128)(2,1)S(1)} %copy-done.1, bf16[128,1024]{1,0:T(8,128)(2,1)S(1)} %get-tuple-element.42.mixing, bf16[128,128]{1,0:T(8,128)(2,1)S(1)} %get-tuple-element.43.refs_0_, ...), custom_call_target="tpu_custom_call" | custom-call | tf_op jit(solution)/shard_map/pallas_call | solution.py:45
  128.3 3.6 %all-to-all-start.1 = ((bf16[16,24,1024]{2,1,0:T(8,128)(2,1)}), bf16[16,24,1024]{2,1,0:T(8,128)(2,1)S(1)}, u32[]{:S(2)}, u32[]{:S(2)}) async-start(bf16[16,24,1024]{2,1,0:T(8,128)(2,1)} %bitcast.7), calls=%async_computation.1 | async-start | bytes 1572864 | tf_op jit(solution)/shard_map/all_to_all | solution.py:389
  131.9 1.6 copy-done.2
  133.5 2.3 %shard_map.110 = bf16[1024,512]{1,0:T(8,128)(2,1)} custom-call(bf16[1024,1024]{1,0:T(8,128)(2,1)S(1)} %copy-done.2, bf16[512,1024]{1,0:T(8,128)(2,1)S(1)} %get-tuple-element.64.gp), custom_call_target="tpu_custom_call" | custom-call | tf_op jit(solution)/shard_map/pallas_call | solution.py:45
  135.8 10.6 %all-to-all-done.1 = bf16[16,24,1024]{2,1,0:T(8,128)(2,1)S(1)} async-done(((bf16[16,24,1024]{2,1,0:T(8,128)(2,1)}), bf16[16,24,1024]{2,1,0:T(8,128)(2,1)S(1)}, u32[]{:S(2)}, u32[]{:S(2)}) %all-to-all-start.1) | async-done | bytes 786464 | tf_op jit(solution)/shard_map/all_to_all | solution.py:389
  146.4 6.4 %all-to-all-start.2 = ((bf16[128,8,512]{2,1,0:T(8,128)(2,1)}), bf16[128,8,512]{2,1,0:T(8,128)(2,1)S(1)}, u32[]{:S(2)}, u32[]{:S(2)}) async-start(bf16[128,8,512]{2,1,0:T(8,128)(2,1)} %bitcast.10), calls=%async_computation.2 | async-start | bytes 2097152 | tf_op jit(solution)/shard_map/all_to_all | solution.py:374
  152.8 1.3 shard_map.109
  154.1 5.3 %collective-permute-start.39 = (f32[8,1024]{1,0:T(8,128)S(1)}, f32[8,1024]{1,0:T(8,128)S(1)}, u32[]{:S(2)}, u32[]{:S(2)}) collective-permute-start(f32[8,1024]{1,0:T(8,128)S(1)} %get-tuple-element.65), channel_id=1, source_target_pairs={{0,0},{1,16},{2,32},{3,48},{4,64},{5,80},{6,96},{7,112},{8,1},{9,1... | collective-permute-start | bytes 98312 | tf_op jit(solution)/shard_map/ppermute | solution.py:400
  159.4 9.9 %collective-permute-done.39 = f32[8,1024]{1,0:T(8,128)S(1)} collective-permute-done((f32[8,1024]{1,0:T(8,128)S(1)}, f32[8,1024]{1,0:T(8,128)S(1)}, u32[]{:S(2)}, u32[]{:S(2)}) %collective-permute-start.39) | collective-permute-done | bytes 32800 | tf_op jit(solution)/shard_map/ppermute | solution.py:400
  169.3 2.1 %all-to-all-done.2 = bf16[128,8,512]{2,1,0:T(8,128)(2,1)S(1)} async-done(((bf16[128,8,512]{2,1,0:T(8,128)(2,1)}), bf16[128,8,512]{2,1,0:T(8,128)(2,1)S(1)}, u32[]{:S(2)}, u32[]{:S(2)}) %all-to-all-start.2) | async-done | bytes 1048608 | tf_op jit(solution)/shard_map/all_to_all | solution.py:374
  171.4 0.8 shard_map.111
  172.2 0.6 copy.22
  (82 shorter events, 1.7 us)
Async XLA Ops:
  0.6 12.1 %copy-start.16 = (s32[128]{0:T(128)S(1)}, s32[128]{0:T(128)}, u32[]{:S(2)}) copy-start(s32[128]{0:T(128)} %param.11) | copy-start | bytes 1540
  1.4 0.9 copy-start.3
  2.4 0.9 copy-start.5
  4.7 19.6 %all-to-all-start = ((bf16[16,16,1024]{2,1,0:T(8,128)(2,1)}), bf16[16,16,1024]{2,1,0:T(8,128)(2,1)S(1)}, u32[]{:S(2)}, u32[]{:S(2)}) async-start(bf16[16,16,1024]{2,1,0:T(8,128)(2,1)} %bitcast.4), calls=%async_computation | async-start | bytes 1048576 | tf_op jit(solution)/shard_map/all_to_all | solution.py:319
  24.6 22.1 %copy-start.7 = (bf16[1024,128]{1,0:T(8,128)(2,1)}, bf16[1024,128]{1,0:T(8,128)(2,1)S(1)}, u32[]{:S(2)}) copy-start(bf16[1024,128]{1,0:T(8,128)(2,1)S(1)} %get-tuple-element.35.refs_0_) | copy-start | bytes 786436
  24.6 10.6 %collective-permute-start.1 = (bf16[1024,128]{1,0:T(8,128)(2,1)S(1)}, bf16[1024,128]{1,0:T(8,128)(2,1)}, u32[]{:S(2)}, u32[]{:S(2)}) collective-permute-start(bf16[1024,128]{1,0:T(8,128)(2,1)S(1)} %get-tuple-element.35.refs_0_), channel_id=1, source_target_pairs={{0,6},{1,7},{2,0},{3,1},{4,2},{5,3},{6,4},{7,5},{8,14},{9,15},{10,... | collective-permute-start | bytes 786440 | tf_op jit(solution)/shard_map/ppermute | solution.py:65
  25.5 10.7 %collective-permute-start.4 = (bf16[1024,128]{1,0:T(8,128)(2,1)S(1)}, bf16[1024,128]{1,0:T(8,128)(2,1)}, u32[]{:S(2)}, u32[]{:S(2)}) collective-permute-start(bf16[1024,128]{1,0:T(8,128)(2,1)S(1)} %get-tuple-element.35.refs_0_), channel_id=1, source_target_pairs={{0,2},{1,3},{2,4},{3,5},{4,6},{5,7},{6,0},{7,1},{8,10},{9,11},{10,... | collective-permute-start | bytes 786440 | tf_op jit(solution)/shard_map/ppermute | solution.py:65
  28.0 12.5 %collective-permute-start.10 = (bf16[128,1024]{1,0:T(8,128)(2,1)S(1)}, bf16[128,1024]{1,0:T(8,128)(2,1)S(1)}, u32[]{:S(2)}, u32[]{:S(2)}) collective-permute-start(bf16[128,1024]{1,0:T(8,128)(2,1)S(1)} %get-tuple-element.38.refs_0_.refs_8_), channel_id=1, source_target_pairs={{0,6},{1,7},{2,0},{3,1},{4,2},{5,3},{6,4},{7,5},{8,14},{9,15},{10,... | collective-permute-start | bytes 786440 | tf_op jit(solution)/shard_map/ppermute | solution.py:65
  28.0 12.6 %collective-permute-start.13 = (bf16[128,1024]{1,0:T(8,128)(2,1)S(1)}, bf16[128,1024]{1,0:T(8,128)(2,1)S(1)}, u32[]{:S(2)}, u32[]{:S(2)}) collective-permute-start(bf16[128,1024]{1,0:T(8,128)(2,1)S(1)} %get-tuple-element.38.refs_0_.refs_8_), channel_id=1, source_target_pairs={{0,2},{1,3},{2,4},{3,5},{4,6},{5,7},{6,0},{7,1},{8,10},{9,11},{10,... | collective-permute-start | bytes 786440 | tf_op jit(solution)/shard_map/ppermute | solution.py:65
  31.2 14.5 %collective-permute-start = (bf16[1024,128]{1,0:T(8,128)(2,1)S(1)}, bf16[1024,128]{1,0:T(8,128)(2,1)S(1)}, u32[]{:S(2)}, u32[]{:S(2)}) collective-permute-start(bf16[1024,128]{1,0:T(8,128)(2,1)S(1)} %get-tuple-element.35.refs_0_), channel_id=1, source_target_pairs={{0,1},{1,0},{2,3},{3,2},{4,5},{5,4},{6,7},{7,6},{8,9},{9,8},{10,11... | collective-permute-start | bytes 786440 | tf_op jit(solution)/shard_map/ppermute | solution.py:65
  36.2 8.3 %collective-permute-start.3 = (bf16[512,128]{1,0:T(8,128)(2,1)S(1)}, bf16[512,128]{1,0:T(8,128)(2,1)S(1)}, u32[]{:S(2)}, u32[]{:S(2)}) collective-permute-start(bf16[512,128]{1,0:T(8,128)(2,1)S(1)} %slice.16), channel_id=1, source_target_pairs={{0,6},{1,7},{2,0},{3,1},{4,2},{5,3},{6,4},{7,5},{8,14},{9,15},{10,... | collective-permute-start | bytes 393224 | tf_op jit(solution)/shard_map/ppermute | solution.py:65
  37.2 7.9 %collective-permute-start.5 = (bf16[512,128]{1,0:T(8,128)(2,1)S(1)}, bf16[512,128]{1,0:T(8,128)(2,1)}, u32[]{:S(2)}, u32[]{:S(2)}) collective-permute-start(bf16[512,128]{1,0:T(8,128)(2,1)S(1)} %slice.17), channel_id=1, source_target_pairs={{0,2},{1,3},{2,4},{3,5},{4,6},{5,7},{6,0},{7,1},{8,10},{9,11},{10,... | collective-permute-start | bytes 393224 | tf_op jit(solution)/shard_map/ppermute | solution.py:65
  40.5 6.2 %collective-permute-start.12 = (bf16[64,1024]{1,0:T(8,128)(2,1)S(1)}, bf16[64,1024]{1,0:T(8,128)(2,1)S(1)}, u32[]{:S(2)}, u32[]{:S(2)}) collective-permute-start(bf16[64,1024]{1,0:T(8,128)(2,1)S(1)} %slice.18), channel_id=1, source_target_pairs={{0,6},{1,7},{2,0},{3,1},{4,2},{5,3},{6,4},{7,5},{8,14},{9,15},{10,... | collective-permute-start | bytes 393224 | tf_op jit(solution)/shard_map/ppermute | solution.py:65
  41.3 6.1 %collective-permute-start.14 = (bf16[64,1024]{1,0:T(8,128)(2,1)}, bf16[64,1024]{1,0:T(8,128)(2,1)}, u32[]{:S(2)}, u32[]{:S(2)}) collective-permute-start(bf16[64,1024]{1,0:T(8,128)(2,1)} %slice.19), channel_id=1, source_target_pairs={{0,2},{1,3},{2,4},{3,5},{4,6},{5,7},{6,0},{7,1},{8,10},{9,11},{10,... | collective-permute-start | bytes 393224 | tf_op jit(solution)/shard_map/ppermute | solution.py:65
  44.5 2.8 %collective-permute-start.6 = (bf16[512,128]{1,0:T(8,128)(2,1)S(1)}, bf16[512,128]{1,0:T(8,128)(2,1)S(1)}, u32[]{:S(2)}, u32[]{:S(2)}) collective-permute-start(bf16[512,128]{1,0:T(8,128)(2,1)S(1)} %collective-permute-done.3.refs_4_), channel_id=1, source_target_pairs={{0,1},{1,0},{2,3},{3,2},{4,5},{5,4},{6,7},{7,6},{8,9},{9,8},{10,11... | collective-permute-start | bytes 393224 | tf_op jit(solution)/shard_map/ppermute | solution.py:65
  44.5 0.7 copy-start.11
  45.1 3.4 %collective-permute-start.7 = (bf16[512,128]{1,0:T(8,128)(2,1)}, bf16[512,128]{1,0:T(8,128)(2,1)}, u32[]{:S(2)}, u32[]{:S(2)}) collective-permute-start(bf16[512,128]{1,0:T(8,128)(2,1)} %collective-permute-done.5.refs_5_), channel_id=1, source_target_pairs={{0,1},{1,0},{2,3},{3,2},{4,5},{5,4},{6,7},{7,6},{8,9},{9,8},{10,11... | collective-permute-start | bytes 393224 | tf_op jit(solution)/shard_map/ppermute | solution.py:65
  45.7 0.7 copy-start.9
  46.4 11.6 %collective-permute-start.2 = (bf16[1024,128]{1,0:T(8,128)(2,1)}, bf16[1024,128]{1,0:T(8,128)(2,1)}, u32[]{:S(2)}, u32[]{:S(2)}) collective-permute-start(bf16[1024,128]{1,0:T(8,128)(2,1)} %collective-permute-done.1.refs_2_), channel_id=1, source_target_pairs={{0,1},{1,0},{2,3},{3,2},{4,5},{5,4},{6,7},{7,6},{8,9},{9,8},{10,11... | collective-permute-start | bytes 786440 | tf_op jit(solution)/shard_map/ppermute | solution.py:65
  46.8 11.8 %collective-permute-start.8 = (bf16[1024,128]{1,0:T(8,128)(2,1)}, bf16[1024,128]{1,0:T(8,128)(2,1)}, u32[]{:S(2)}, u32[]{:S(2)}) collective-permute-start(bf16[1024,128]{1,0:T(8,128)(2,1)} %collective-permute-done.4.refs_8_), channel_id=1, source_target_pairs={{0,1},{1,0},{2,3},{3,2},{4,5},{5,4},{6,7},{7,6},{8,9},{9,8},{10,11... | collective-permute-start | bytes 786440 | tf_op jit(solution)/shard_map/ppermute | solution.py:65
  46.9 11.0 %copy-start.1 = (bf16[1024,1024]{1,0:T(8,128)(2,1)S(1)}, bf16[1024,1024]{1,0:T(8,128)(2,1)}, u32[]{:S(2)}) copy-start(bf16[1024,1024]{1,0:T(8,128)(2,1)} %w_out.1) | copy-start | bytes 6291460
  47.3 18.9 %collective-permute-start.9 = (bf16[128,1024]{1,0:T(8,128)(2,1)S(1)}, bf16[128,1024]{1,0:T(8,128)(2,1)S(1)}, u32[]{:S(2)}, u32[]{:S(2)}) collective-permute-start(bf16[128,1024]{1,0:T(8,128)(2,1)S(1)} %get-tuple-element.38.refs_0_.refs_8_), channel_id=1, source_target_pairs={{0,1},{1,0},{2,3},{3,2},{4,5},{5,4},{6,7},{7,6},{8,9},{9,8},{10,11... | collective-permute-start | bytes 786440 | tf_op jit(solution)/shard_map/ppermute | solution.py:65
  47.3 0.7 copy-start.13
  48.0 18.2 %collective-permute-start.11 = (bf16[128,1024]{1,0:T(8,128)(2,1)S(1)}, bf16[128,1024]{1,0:T(8,128)(2,1)S(1)}, u32[]{:S(2)}, u32[]{:S(2)}) collective-permute-start(bf16[128,1024]{1,0:T(8,128)(2,1)S(1)} %collective-permute-done.10.refs_2_.refs_10_), channel_id=1, source_target_pairs={{0,1},{1,0},{2,3},{3,2},{4,5},{5,4},{6,7},{7,6},{8,9},{9,8},{10,11... | collective-permute-start | bytes 786440 | tf_op jit(solution)/shard_map/ppermute | solution.py:65
  48.5 17.7 %collective-permute-start.17 = (bf16[128,1024]{1,0:T(8,128)(2,1)S(1)}, bf16[128,1024]{1,0:T(8,128)(2,1)}, u32[]{:S(2)}, u32[]{:S(2)}) collective-permute-start(bf16[128,1024]{1,0:T(8,128)(2,1)S(1)} %collective-permute-done.13.refs_8_.refs_16_), channel_id=1, source_target_pairs={{0,1},{1,0},{2,3},{3,2},{4,5},{5,4},{6,7},{7,6},{8,9},{9,8},{10,11... | collective-permute-start | bytes 786440 | tf_op jit(solution)/shard_map/ppermute | solution.py:65
  52.5 7.6 %copy-start.15 = (s32[1,4]{1,0:T(1,128)S(1)}, s32[1,4]{1,0:T(1,128)}, u32[]{:S(2)}) copy-start(s32[1,4]{1,0:T(1,128)} %lengths.3) | copy-start | bytes 52
  57.9 2.2 %copy-start.8 = (bf16[1024,128]{1,0:T(8,128)(2,1)S(1)}, bf16[1024,128]{1,0:T(8,128)(2,1)}, u32[]{:S(2)}) copy-start(bf16[1024,128]{1,0:T(8,128)(2,1)} %copy-done.7) | copy-start | bytes 786436
  57.9 2.2 %copy-start.10 = (bf16[1024,128]{1,0:T(8,128)(2,1)S(1)}, bf16[1024,128]{1,0:T(8,128)(2,1)}, u32[]{:S(2)}) copy-start(bf16[1024,128]{1,0:T(8,128)(2,1)} %copy-done.9) | copy-start | bytes 786436
  57.9 2.2 %copy-start.12 = (bf16[512,128]{1,0:T(8,128)(2,1)S(1)}, bf16[512,128]{1,0:T(8,128)(2,1)}, u32[]{:S(2)}) copy-start(bf16[512,128]{1,0:T(8,128)(2,1)} %copy-done.11) | copy-start | bytes 393220
  57.9 2.2 %copy-start.14 = (bf16[512,128]{1,0:T(8,128)(2,1)S(1)}, bf16[512,128]{1,0:T(8,128)(2,1)}, u32[]{:S(2)}) copy-start(bf16[512,128]{1,0:T(8,128)(2,1)} %copy-done.13) | copy-start | bytes 393220
  57.9 8.2 %collective-permute-start.15 = (bf16[64,1024]{1,0:T(8,128)(2,1)S(1)}, bf16[64,1024]{1,0:T(8,128)(2,1)S(1)}, u32[]{:S(2)}, u32[]{:S(2)}) collective-permute-start(bf16[64,1024]{1,0:T(8,128)(2,1)S(1)} %collective-permute-done.12.refs_4_.refs_12_), channel_id=1, source_target_pairs={{0,1},{1,0},{2,3},{3,2},{4,5},{5,4},{6,7},{7,6},{8,9},{9,8},{10,11... | collective-permute-start | bytes 393224 | tf_op jit(solution)/shard_map/ppermute | solution.py:65
  58.5 7.7 %collective-permute-start.16 = (bf16[64,1024]{1,0:T(8,128)(2,1)}, bf16[64,1024]{1,0:T(8,128)(2,1)S(1)}, u32[]{:S(2)}, u32[]{:S(2)}) collective-permute-start(bf16[64,1024]{1,0:T(8,128)(2,1)} %collective-permute-done.14.refs_5_.refs_13_), channel_id=1, source_target_pairs={{0,1},{1,0},{2,3},{3,2},{4,5},{5,4},{6,7},{7,6},{8,9},{9,8},{10,11... | collective-permute-start | bytes 393224 | tf_op jit(solution)/shard_map/ppermute | solution.py:65
  68.2 7.0 %collective-permute-start.18 = (f32[8,1024]{1,0:T(8,128)S(1)}, f32[8,1024]{1,0:T(8,128)S(1)}, u32[]{:S(2)}, u32[]{:S(2)}) collective-permute-start(f32[8,1024]{1,0:T(8,128)S(1)} %get-tuple-element.41.refs_0_), channel_id=1, source_target_pairs={{0,1},{1,0},{2,3},{3,2},{4,5},{5,4},{6,7},{7,6},{8,9},{9,8},{10,11... | collective-permute-start | bytes 98312 | tf_op jit(solution)/shard_map/ppermute | solution.py:65
  68.5 8.7 %collective-permute-start.19 = (f32[8,1024]{1,0:T(8,128)S(1)}, f32[8,1024]{1,0:T(8,128)S(1)}, u32[]{:S(2)}, u32[]{:S(2)}) collective-permute-start(f32[8,1024]{1,0:T(8,128)S(1)} %get-tuple-element.41.refs_0_), channel_id=1, source_target_pairs={{0,2},{1,3},{2,4},{3,5},{4,6},{5,7},{6,0},{7,1},{8,10},{9,11},{10,... | collective-permute-start | bytes 98312 | tf_op jit(solution)/shard_map/ppermute | solution.py:65
  72.1 5.2 %collective-permute-start.20 = (f32[8,1024]{1,0:T(8,128)S(1)}, f32[8,1024]{1,0:T(8,128)S(1)}, u32[]{:S(2)}, u32[]{:S(2)}) collective-permute-start(f32[8,1024]{1,0:T(8,128)S(1)} %get-tuple-element.41.refs_0_), channel_id=1, source_target_pairs={{0,3},{1,2},{2,5},{3,4},{4,7},{5,6},{6,1},{7,0},{8,11},{9,10},{10,... | collective-permute-start | bytes 98312 | tf_op jit(solution)/shard_map/ppermute | solution.py:65
  72.1 5.4 %collective-permute-start.21 = (f32[8,1024]{1,0:T(8,128)S(1)}, f32[8,1024]{1,0:T(8,128)S(1)}, u32[]{:S(2)}, u32[]{:S(2)}) collective-permute-start(f32[8,1024]{1,0:T(8,128)S(1)} %get-tuple-element.41.refs_0_), channel_id=1, source_target_pairs={{0,4},{1,5},{2,6},{3,7},{4,0},{5,1},{6,2},{7,3},{8,12},{9,13},{10,... | collective-permute-start | bytes 98312 | tf_op jit(solution)/shard_map/ppermute | solution.py:65
  72.2 5.4 %collective-permute-start.22 = (f32[8,1024]{1,0:T(8,128)S(1)}, f32[8,1024]{1,0:T(8,128)S(1)}, u32[]{:S(2)}, u32[]{:S(2)}) collective-permute-start(f32[8,1024]{1,0:T(8,128)S(1)} %get-tuple-element.41.refs_0_), channel_id=1, source_target_pairs={{0,5},{1,4},{2,7},{3,6},{4,1},{5,0},{6,3},{7,2},{8,13},{9,12},{10,... | collective-permute-start | bytes 98312 | tf_op jit(solution)/shard_map/ppermute | solution.py:65
  75.1 5.2 %collective-permute-start.23 = (f32[8,1024]{1,0:T(8,128)S(1)}, f32[8,1024]{1,0:T(8,128)S(1)}, u32[]{:S(2)}, u32[]{:S(2)}) collective-permute-start(f32[8,1024]{1,0:T(8,128)S(1)} %get-tuple-element.41.refs_0_), channel_id=1, source_target_pairs={{0,6},{1,7},{2,0},{3,1},{4,2},{5,3},{6,4},{7,5},{8,14},{9,15},{10,... | collective-permute-start | bytes 98312 | tf_op jit(solution)/shard_map/ppermute | solution.py:65
  77.1 4.7 %collective-permute-start.24 = (f32[8,1024]{1,0:T(8,128)S(1)}, f32[8,1024]{1,0:T(8,128)S(1)}, u32[]{:S(2)}, u32[]{:S(2)}) collective-permute-start(f32[8,1024]{1,0:T(8,128)S(1)} %get-tuple-element.41.refs_0_), channel_id=1, source_target_pairs={{0,7},{1,6},{2,1},{3,0},{4,3},{5,2},{6,5},{7,4},{8,15},{9,14},{10,... | collective-permute-start | bytes 98312 | tf_op jit(solution)/shard_map/ppermute | solution.py:65
  81.9 3.3 %copy-start = (f32[512,1024]{1,0:T(8,128)S(1)}, f32[512,1024]{1,0:T(8,128)}, u32[]{:S(2)}) copy-start(f32[512,1024]{1,0:T(8,128)} %get-tuple-element.40.pre) | copy-start | bytes 6291460
  91.7 16.0 %collective-permute-start.32 = (bf16[512,128]{1,0:T(8,128)(2,1)S(1)}, bf16[512,128]{1,0:T(8,128)(2,1)S(1)}, u32[]{:S(2)}, u32[]{:S(2)}) collective-permute-start(bf16[512,128]{1,0:T(8,128)(2,1)S(1)} %get-tuple-element.54), channel_id=1, source_target_pairs={{0,1},{1,0},{2,3},{3,2},{4,5},{5,4},{6,7},{7,6},{8,9},{9,8},{10,11... | collective-permute-start | bytes 393224 | tf_op jit(solution)/shard_map/ppermute | solution.py:65
  91.8 19.9 %collective-permute-start.33 = (bf16[512,128]{1,0:T(8,128)(2,1)S(1)}, bf16[512,128]{1,0:T(8,128)(2,1)S(1)}, u32[]{:S(2)}, u32[]{:S(2)}) collective-permute-start(bf16[512,128]{1,0:T(8,128)(2,1)S(1)} %get-tuple-element.55), channel_id=1, source_target_pairs={{0,6},{1,7},{2,0},{3,1},{4,2},{5,3},{6,4},{7,5},{8,14},{9,15},{10,... | collective-permute-start | bytes 393224 | tf_op jit(solution)/shard_map/ppermute | solution.py:65
  91.8 1.4 collective-permute-start.25
  92.2 8.4 %collective-permute-start.26 = (bf16[128,128]{1,0:T(8,128)(2,1)S(1)}, bf16[128,128]{1,0:T(8,128)(2,1)S(1)}, u32[]{:S(2)}, u32[]{:S(2)}) collective-permute-start(bf16[128,128]{1,0:T(8,128)(2,1)S(1)} %get-tuple-element.45), channel_id=1, source_target_pairs={{0,6},{1,7},{2,0},{3,1},{4,2},{5,3},{6,4},{7,5},{8,14},{9,15},{10,... | collective-permute-start | bytes 98312 | tf_op jit(solution)/shard_map/ppermute | solution.py:65
  92.3 8.3 %collective-permute-start.27 = (bf16[128,128]{1,0:T(8,128)(2,1)S(1)}, bf16[128,128]{1,0:T(8,128)(2,1)S(1)}, u32[]{:S(2)}, u32[]{:S(2)}) collective-permute-start(bf16[128,128]{1,0:T(8,128)(2,1)S(1)} %get-tuple-element.46), channel_id=1, source_target_pairs={{0,7},{1,6},{2,1},{3,0},{4,3},{5,2},{6,5},{7,4},{8,15},{9,14},{10,... | collective-permute-start | bytes 98312 | tf_op jit(solution)/shard_map/ppermute | solution.py:65
  93.2 7.5 %collective-permute-start.28 = (bf16[128,128]{1,0:T(8,128)(2,1)S(1)}, bf16[128,128]{1,0:T(8,128)(2,1)S(1)}, u32[]{:S(2)}, u32[]{:S(2)}) collective-permute-start(bf16[128,128]{1,0:T(8,128)(2,1)S(1)} %get-tuple-element.47), channel_id=1, source_target_pairs={{0,4},{1,5},{2,6},{3,7},{4,0},{5,1},{6,2},{7,3},{8,12},{9,13},{10,... | collective-permute-start | bytes 98312 | tf_op jit(solution)/shard_map/ppermute | solution.py:65
  100.6 4.8 %collective-permute-start.29 = (bf16[128,128]{1,0:T(8,128)(2,1)S(1)}, bf16[128,128]{1,0:T(8,128)(2,1)S(1)}, u32[]{:S(2)}, u32[]{:S(2)}) collective-permute-start(bf16[128,128]{1,0:T(8,128)(2,1)S(1)} %get-tuple-element.48), channel_id=1, source_target_pairs={{0,5},{1,4},{2,7},{3,6},{4,1},{5,0},{6,3},{7,2},{8,13},{9,12},{10,... | collective-permute-start | bytes 98312 | tf_op jit(solution)/shard_map/ppermute | solution.py:65
  100.6 4.8 %collective-permute-start.30 = (bf16[128,128]{1,0:T(8,128)(2,1)S(1)}, bf16[128,128]{1,0:T(8,128)(2,1)S(1)}, u32[]{:S(2)}, u32[]{:S(2)}) collective-permute-start(bf16[128,128]{1,0:T(8,128)(2,1)S(1)} %get-tuple-element.49), channel_id=1, source_target_pairs={{0,2},{1,3},{2,4},{3,5},{4,6},{5,7},{6,0},{7,1},{8,10},{9,11},{10,... | collective-permute-start | bytes 98312 | tf_op jit(solution)/shard_map/ppermute | solution.py:65
  100.7 5.9 %collective-permute-start.31 = (bf16[128,128]{1,0:T(8,128)(2,1)S(1)}, bf16[128,128]{1,0:T(8,128)(2,1)S(1)}, u32[]{:S(2)}, u32[]{:S(2)}) collective-permute-start(bf16[128,128]{1,0:T(8,128)(2,1)S(1)} %get-tuple-element.50), channel_id=1, source_target_pairs={{0,3},{1,2},{2,5},{3,4},{4,7},{5,6},{6,1},{7,0},{8,11},{9,10},{10,... | collective-permute-start | bytes 98312 | tf_op jit(solution)/shard_map/ppermute | solution.py:65
  105.5 11.8 %collective-permute-start.34 = (bf16[512,128]{1,0:T(8,128)(2,1)S(1)}, bf16[512,128]{1,0:T(8,128)(2,1)S(1)}, u32[]{:S(2)}, u32[]{:S(2)}) collective-permute-start(bf16[512,128]{1,0:T(8,128)(2,1)S(1)} %get-tuple-element.56), channel_id=1, source_target_pairs={{0,7},{1,6},{2,1},{3,0},{4,3},{5,2},{6,5},{7,4},{8,15},{9,14},{10,... | collective-permute-start | bytes 393224 | tf_op jit(solution)/shard_map/ppermute | solution.py:65
  105.5 11.7 %collective-permute-start.35 = (bf16[512,128]{1,0:T(8,128)(2,1)S(1)}, bf16[512,128]{1,0:T(8,128)(2,1)S(1)}, u32[]{:S(2)}, u32[]{:S(2)}) collective-permute-start(bf16[512,128]{1,0:T(8,128)(2,1)S(1)} %get-tuple-element.57), channel_id=1, source_target_pairs={{0,4},{1,5},{2,6},{3,7},{4,0},{5,1},{6,2},{7,3},{8,12},{9,13},{10,... | collective-permute-start | bytes 393224 | tf_op jit(solution)/shard_map/ppermute | solution.py:65
  106.6 10.6 %collective-permute-start.36 = (bf16[512,128]{1,0:T(8,128)(2,1)S(1)}, bf16[512,128]{1,0:T(8,128)(2,1)S(1)}, u32[]{:S(2)}, u32[]{:S(2)}) collective-permute-start(bf16[512,128]{1,0:T(8,128)(2,1)S(1)} %get-tuple-element.58), channel_id=1, source_target_pairs={{0,5},{1,4},{2,7},{3,6},{4,1},{5,0},{6,3},{7,2},{8,13},{9,12},{10,... | collective-permute-start | bytes 393224 | tf_op jit(solution)/shard_map/ppermute | solution.py:65
  107.7 9.9 %collective-permute-start.37 = (bf16[512,128]{1,0:T(8,128)(2,1)S(1)}, bf16[512,128]{1,0:T(8,128)(2,1)S(1)}, u32[]{:S(2)}, u32[]{:S(2)}) collective-permute-start(bf16[512,128]{1,0:T(8,128)(2,1)S(1)} %get-tuple-element.59), channel_id=1, source_target_pairs={{0,2},{1,3},{2,4},{3,5},{4,6},{5,7},{6,0},{7,1},{8,10},{9,11},{10,... | collective-permute-start | bytes 393224 | tf_op jit(solution)/shard_map/ppermute | solution.py:65
  111.7 9.2 %collective-permute-start.38 = (bf16[512,128]{1,0:T(8,128)(2,1)S(1)}, bf16[512,128]{1,0:T(8,128)(2,1)S(1)}, u32[]{:S(2)}, u32[]{:S(2)}) collective-permute-start(bf16[512,128]{1,0:T(8,128)(2,1)S(1)} %get-tuple-element.60), channel_id=1, source_target_pairs={{0,3},{1,2},{2,5},{3,4},{4,7},{5,6},{6,1},{7,0},{8,11},{9,10},{10,... | collective-permute-start | bytes 393224 | tf_op jit(solution)/shard_map/ppermute | solution.py:65
  128.3 18.1 %all-to-all-start.1 = ((bf16[16,24,1024]{2,1,0:T(8,128)(2,1)}), bf16[16,24,1024]{2,1,0:T(8,128)(2,1)S(1)}, u32[]{:S(2)}, u32[]{:S(2)}) async-start(bf16[16,24,1024]{2,1,0:T(8,128)(2,1)} %bitcast.7), calls=%async_computation.1 | async-start | bytes 1572864 | tf_op jit(solution)/shard_map/all_to_all | solution.py:389
  131.9 1.6 copy-start.2
  135.8 17.0 %copy-start.4 = (bf16[128,1024]{1,0:T(8,128)(2,1)S(1)}, bf16[128,1024]{1,0:T(8,128)(2,1)}, u32[]{:S(2)}) copy-start(bf16[128,1024]{1,0:T(8,128)(2,1)} %hist.3) | copy-start | bytes 786436
  135.8 17.0 %copy-start.6 = (bf16[128,1024]{1,0:T(8,128)(2,1)S(1)}, bf16[128,1024]{1,0:T(8,128)(2,1)}, u32[]{:S(2)}) copy-start(bf16[128,1024]{1,0:T(8,128)(2,1)} %gout.3) | copy-start | bytes 786436
  135.8 17.0 %copy-start.17 = (s32[128]{0:T(128)S(1)}, s32[128]{0:T(128)}, u32[]{:S(2)}) copy-start(s32[128]{0:T(128)} %param.10) | copy-start | bytes 1540
  146.4 25.0 %all-to-all-start.2 = ((bf16[128,8,512]{2,1,0:T(8,128)(2,1)}), bf16[128,8,512]{2,1,0:T(8,128)(2,1)S(1)}, u32[]{:S(2)}, u32[]{:S(2)}) async-start(bf16[128,8,512]{2,1,0:T(8,128)(2,1)} %bitcast.10), calls=%async_computation.2 | async-start | bytes 2097152 | tf_op jit(solution)/shard_map/all_to_all | solution.py:374
  154.1 15.2 %collective-permute-start.39 = (f32[8,1024]{1,0:T(8,128)S(1)}, f32[8,1024]{1,0:T(8,128)S(1)}, u32[]{:S(2)}, u32[]{:S(2)}) collective-permute-start(f32[8,1024]{1,0:T(8,128)S(1)} %get-tuple-element.65), channel_id=1, source_target_pairs={{0,0},{1,16},{2,32},{3,48},{4,64},{5,80},{6,96},{7,112},{8,1},{9,1... | collective-permute-start | bytes 98312 | tf_op jit(solution)/shard_map/ppermute | solution.py:400

commit v2 on v1

v2 whole, which is shorter than its diff:
```python
import jax
import jax.numpy as jnp
from jax import lax
from jax.experimental import pallas as pl
from jax.experimental.pallas import tpu as pltpu
from jax.sharding import PartitionSpec as P


D = 1024
WIDE = 128
PART = 5 * WIDE
HEAD = 64
N_DP = 16
N_CTX = 8
R = 128
GROUP = 1024
BLOCK = 256
EPS = 1e-6
BF = jnp.bfloat16
F32 = jnp.float32
NN = (((1,), (0,)), ((), ()))
NT = (((1,), (1,)), ((), ()))
VMEM_BYTES = 32 * 1024 * 1024


def dot(a, b, dims=NN):
    return lax.dot_general(a, b, dims, preferred_element_type=F32)


def sigmoid(v):
    return 0.5 * jnp.tanh(0.5 * v) + 0.5


def iota(shape, dim):
    return lax.broadcasted_iota(jnp.int32, shape, dim)


def row_norm(values):
    centred = values - jnp.mean(values, axis=-1, keepdims=True)
    inverse = lax.rsqrt(jnp.mean(centred * centred, axis=-1, keepdims=True) + EPS)
    return centred * inverse, inverse


def skip(body, first, count):
    def kernel(*refs):
        body(*refs[:first], *refs[first + count :])

    return kernel if count else body


def hbm(x):
    return pltpu.with_memory_space_constraint(x, pltpu.HBM)


def call(body, outs, *args, smem=0, plain=0, scratch=(), late=()):
    specs = [pl.BlockSpec(memory_space=pltpu.SMEM)] * smem
    specs += [pl.BlockSpec(memory_space=pltpu.VMEM)] * (len(args) - smem - plain)
    specs += [pl.BlockSpec(memory_space=pl.ANY)] * (plain + len(late))
    return pl.pallas_call(
        skip(body, len(args), len(late)),
        out_shape=[pltpu.HBM(s, t) for s, t in outs],
        in_specs=specs,
        out_specs=[pl.BlockSpec(memory_space=pltpu.VMEM)] * len(outs),
        scratch_shapes=list(scratch),
        compiler_params=pltpu.CompilerParams(vmem_limit_bytes=VMEM_BYTES),
    )(*args, *late)


REL = [(0, 0), (0, 1), (1, 0), (1, 1), (2, 0), (2, 1), (3, 0), (3, 1)]


def place_of(ctx, rel):
    chip = lax.rem((ctx >> 1) + rel[0], 4)
    return chip * 2 + ((ctx & 1) ^ rel[1])


def send(x, step, flip):
    pairs = [(2 * a + b, 2 * ((a + step) % 4) + (b ^ flip)) for a in range(4) for b in range(2)]
    return lax.ppermute(x, "ctx", pairs)


def ring_gather(x):
    half = x.shape[0] // 2
    up = send(x, 3, 0)
    down = send(x, 1, 0)
    far = (send(up[:half], 3, 0), send(down[half:], 1, 0))
    shards = [x, send(x, 0, 1), up, send(up, 0, 1), *far]
    shards += [send(far[0], 0, 1), send(far[1], 0, 1), down, send(down, 0, 1)]
    return shards


def relay(own, other, near, far):
    far = [send(send(far[0], 1, 0), 1, 0), send(send(far[1], 3, 0), 3, 0)]
    near = [send(near[0], 1, 0), send(near[1], 3, 0)]
    got = [own, send(other, 0, 1)]
    for v in near + far:
        got += [v, send(v, 0, 1)]
    return got


def at(index):
    return pl.ds(pl.multiple_of(index * R, R), R)


def copy_kernel(ctx, x, out):
    del ctx
    out[...] = x[...]


def pick_rows(ids):
    return (ids == iota((R, R), 0)).astype(F32).T.astype(BF)


def pack_kernel(hist, gout, order, out):
    xn = row_norm(hist[...].astype(F32))[0].astype(BF)
    pick = pick_rows(order[...])
    a = dot(pick, xn).reshape(N_DP, 8, D)
    b = dot(pick, gout[...]).reshape(N_DP, 8, D)
    out[...] = jnp.concatenate([a, b], axis=1).reshape(2 * R, D).astype(BF)


def own_weights_kernel(ctx, w, out):
    del ctx
    out[...] = w[...].astype(F32).T.astype(BF)


def place_kernel(recv, place, out):
    pick = pick_rows(place[...])
    got = recv[...].astype(F32).reshape(N_DP, 2, 8, D)
    for i in range(2):
        rows = dot(pick, got[:, i].reshape(R, D).astype(BF))
        out[i * D : (i + 1) * D, :] = rows.T.astype(BF)


def first_visible(lengths):
    rows = iota((1, GROUP), 1)
    low = jnp.full((1, GROUP), 1 << 20, jnp.int32)
    start = jnp.int32(0)
    for j in range(4):
        length = lengths[0, j]
        low = jnp.where((rows >= start) & (rows < start + length), start, low)
        start = start + ((length + 127) >> 7) * 128
    return low


def visible_block(low, rb, tb):
    rs = slice(rb * BLOCK, (rb + 1) * BLOCK)
    keys = iota((BLOCK, BLOCK), 0) + tb * BLOCK
    seen = keys >= low[:, rs]
    if tb == rb:
        seen = seen & (keys <= iota((BLOCK, BLOCK), 1) + rb * BLOCK)
    return seen


def masked_head(x, h, scale=None):
    rows = iota(x.shape, 0)
    x = jnp.where((rows >= h * HEAD) & (rows < (h + 1) * HEAD), x, 0.0)
    if scale is not None:
        x = x * scale
    return x.astype(BF)


def forward_kernel(lengths, ctx, wt, w_out, *refs):
    shards = refs[:10]
    xn, up, slopes, proj, att, gh, sums = refs[10:]
    c = ctx[0]
    for i, rel in zip((0, 1, 2, 3, 8, 9), REL[:4] + REL[6:]):
        to = at(place_of(c, rel))
        xn[:, to] = shards[i][:D, :]
        up[:, to] = shards[i][D:, :]
    for i, core in ((4, 0), (6, 1)):
        to = at(place_of(c, (2, core)))
        xn[:, to] = shards[i][...]
        up[:, to] = shards[i + 1][...]
    for n in range(GROUP // BLOCK):
        cols = slice(n * BLOCK, (n + 1) * BLOCK)
        p = dot(wt[...], xn[:, cols])
        sig = sigmoid(p)
        out = p * sig
        slopes[:, cols] = (sig + out * (1.0 - sig)).astype(BF)
        proj[:, cols] = out.astype(BF)
        gh[:, cols] = dot(w_out[...], up[:, cols])
    low = first_visible(lengths)
    keys = proj[3 * WIDE :, :].astype(F32).T.astype(BF)
    for rb in range(GROUP // BLOCK):
        rs = slice(rb * BLOCK, (rb + 1) * BLOCK)
        query = proj[2 * WIDE : 3 * WIDE, rs].astype(F32)
        for h in range(2):
            hs = slice(h * HEAD, (h + 1) * HEAD)
            q = masked_head(query, h, 0.125)
            total = jnp.zeros((HEAD, BLOCK), F32)
            for tb in range(rb + 1):
                ts = slice(tb * BLOCK, (tb + 1) * BLOCK)
                s = dot(keys[ts], q)
                w = jnp.where(visible_block(low, rb, tb), s * sigmoid(s), 0.0).astype(BF)
                total = total + dot(proj[WIDE + h * HEAD : WIDE + (h + 1) * HEAD, ts], w)
            att[hs, rs] = total
    a = att[...]
    mean = jnp.mean(a, axis=0, keepdims=True)
    dev = a - mean
    gz = gh[...] * proj[:WIDE, :].astype(F32)
    sums[0:1, :] = mean
    sums[1:2, :] = jnp.sum(dev * dev, axis=0, keepdims=True)
    sums[2:3, :] = jnp.sum(gz, axis=0, keepdims=True)
    sums[3:4, :] = jnp.sum(gz * dev, axis=0, keepdims=True)
    sums[4:8, :] = jnp.zeros((4, GROUP), F32)


def backward_kernel(lengths, ctx, slopes, proj, att, gh, *refs):
    sums, (xn_hbm, up_hbm) = refs[:8], refs[8:10]
    own, other, up_part, down_part, far_up, far_down, weights = refs[10:17]
    gp, gatt, dk, dv, xn, up, sems = refs[17:]
    loads = [
        pltpu.make_async_copy(xn_hbm, xn, sems.at[0]),
        pltpu.make_async_copy(up_hbm, up, sems.at[1]),
    ]
    for load in loads:
        load.start()
    c = ctx[0]
    each = [s[...] for s in sums]
    mean = sum(s[0:1, :] for s in each) * (1.0 / N_CTX)
    spread = sum(s[1:2, :] + WIDE * jnp.square(s[0:1, :] - mean) for s in each)
    inverse = lax.rsqrt(spread * (1.0 / D) + EPS)
    first = sum(s[2:3, :] for s in each) * (1.0 / D)
    second = sum(s[3:4, :] + (s[0:1, :] - mean) * s[2:3, :] for s in each) * inverse * (1.0 / D)
    for n in range(GROUP // BLOCK):
        cols = slice(n * BLOCK, (n + 1) * BLOCK)
        z = (att[:, cols] - mean[:, cols]) * inverse[:, cols]
        gate = proj[:WIDE, cols].astype(F32)
        grad = gh[:, cols]
        gp[:WIDE, cols] = (z * gate).astype(BF)
        gp[WIDE : 2 * WIDE, cols] = (grad * z * slopes[:WIDE, cols].astype(F32)).astype(BF)
        rest = grad * gate - first[:, cols] - z * second[:, cols]
        gatt[:, cols] = (inverse[:, cols] * rest).astype(BF)

    low = first_visible(lengths)
    keys = proj[3 * WIDE :, :].astype(F32).T.astype(BF)
    values = proj[WIDE : 2 * WIDE, :].astype(F32).T.astype(BF)
    dk[...] = jnp.zeros((WIDE, GROUP), F32)
    dv[...] = jnp.zeros((WIDE, GROUP), F32)
    for rb in range(GROUP // BLOCK):
        rs = slice(rb * BLOCK, (rb + 1) * BLOCK)
        query = proj[2 * WIDE : 3 * WIDE, rs].astype(F32)
        grad = gatt[:, rs].astype(F32)
        for h in range(2):
            hs = slice(h * HEAD, (h + 1) * HEAD)
            q = masked_head(query, h, 0.125)
            g = masked_head(grad, h)
            total = jnp.zeros((HEAD, BLOCK), F32)
            for tb in range(rb + 1):
                ts = slice(tb * BLOCK, (tb + 1) * BLOCK)
                s = dot(keys[ts], q)
                gw = dot(values[ts], g)
                seen = visible_block(low, rb, tb)
                sig = sigmoid(s)
                w = jnp.where(seen, s * sig, 0.0)
                gs = jnp.where(seen, gw * (sig + w * (1.0 - sig)), 0.0).astype(BF)
                dv[hs, ts] += dot(g[hs], w.astype(BF), NT)
                dk[hs, ts] += dot(q[hs], gs, NT)
                total = total + dot(proj[3 * WIDE + h * HEAD : 3 * WIDE + (h + 1) * HEAD, ts], gs)
            qs = slice(2 * WIDE + h * HEAD, 2 * WIDE + (h + 1) * HEAD)
            to = slice(3 * WIDE + h * HEAD, 3 * WIDE + (h + 1) * HEAD)
            gp[to, rs] = (total * 0.125 * slopes[qs, rs].astype(F32)).astype(BF)
    gp[2 * WIDE : 3 * WIDE, :] = (dv[...] * slopes[WIDE : 2 * WIDE, :].astype(F32)).astype(BF)
    gp[4 * WIDE :, :] = (dk[...] * slopes[3 * WIDE :, :].astype(F32)).astype(BF)

    n, half = PART, PART // 2
    for core in range(2):
        (own, other)[core][...] = gp[:, at(place_of(c, (0, core)))]
        up_part[core * n : core * n + n, :] = gp[:, at(place_of(c, (1, core)))]
        down_part[core * n : core * n + n, :] = gp[:, at(place_of(c, (3, core)))]
        opposite = at(place_of(c, (2, core)))
        far_up[core * half : core * half + half, :] = gp[:half, opposite]
        far_down[core * half : core * half + half, :] = gp[half:, opposite]

    for load in loads:
        load.wait()
    for n in range(4):
        rows = slice(n * BLOCK, (n + 1) * BLOCK)
        part = dot(xn[rows, :], gp[WIDE:, :], NT).astype(BF)
        weights[4 * n : 4 * n + 4, :64, :] = part.reshape(4, 64, 4 * WIDE)
    mix = [dot(gp[:WIDE, :], up[h : h + 512, :], NT).reshape(N_DP, 8, 512) for h in (0, 512)]
    weights[:, 64:, :] = jnp.concatenate(mix, axis=1).astype(BF)


def sum_kernel(recv, project, mixing):
    total = recv[0].astype(F32)
    for d in range(1, N_DP):
        total = total + recv[d].astype(F32)
    project[...] = total[:64]
    mixing[:, :512] = total[64:72]
    mixing[:, 512:] = total[72:]


def join_kernel(ctx, parts, out):
    own = pl.multiple_of(ctx[0] * 8, 8)
    for c in range(N_CTX):
        got = parts[c, pl.ds(own, 8), :]
        for kind in range(4):
            start = kind * D + c * WIDE
            out[:, start : start + WIDE] = got[:, kind * WIDE : (kind + 1) * WIDE]


def rows_kernel(ctx, place, w, w_out, *refs):
    parts, out, (hid, gp) = refs[:10], refs[10], refs[11:]
    back = (place[...] == iota((R, R), 0)).astype(BF)

    @pl.when(pl.program_id(0) == 0)
    def _():
        c = ctx[0]
        n, half = PART, PART // 2
        hidden = [None] * 8
        for core in range(2):
            near = slice(core * n, core * n + n)
            rest = slice(core * half, core * half + half)
            far = [parts[6 + core][rest, :], parts[8 + core][rest, :]]
            got = [
                ((0, core), parts[core][...]),
                ((3, core), parts[2 + core][near, :]),
                ((1, core), parts[4 + core][near, :]),
                ((2, core), jnp.concatenate(far, axis=0)),
            ]
            for rel, part in got:
                src = place_of(c, rel)
                hid[:, at(src)] = dot(back, part[:WIDE, :], NT).astype(BF)
                for kind in range(4):
                    start = (kind + 1) * WIDE
                    gp[at(kind * 8 + src), :] = part[start : start + WIDE, :]

    o = dot(hid[...], w_out[...])
    gx = dot(back, dot(w[...], gp[...]).astype(BF), NT)
    cols = gx.shape[1]
    values = [v.reshape(N_DP, 8, cols) for v in (o, gx)]
    out[...] = jnp.concatenate(values, axis=1).reshape(2 * R, cols).astype(BF)


def unpack_kernel(recv, hist, gout, order, out, grad):
    got = recv[...].astype(F32).reshape(N_DP, 2, 8, D)
    back = (order[...] == iota((R, R), 0)).astype(BF)
    o = dot(back, got[:, 0].reshape(R, D).astype(BF))
    gx = dot(back, got[:, 1].reshape(R, D).astype(BF))
    x = hist[...].astype(F32)
    out[...] = (o + x).astype(BF)
    normed, inverse = row_norm(x)
    first = jnp.mean(gx, axis=-1, keepdims=True)
    second = jnp.mean(gx * normed, axis=-1, keepdims=True)
    grad[...] = (inverse * (gx - first - normed * second) + gout[...].astype(F32)).astype(BF)


def own_weights(ctx_s, w_project):
    return pl.pallas_call(
        own_weights_kernel,
        grid_spec=pltpu.PrefetchScalarGridSpec(
            num_scalar_prefetch=1,
            grid=(4,),
            in_specs=[pl.BlockSpec((D, WIDE), lambda k, ctx: (0, k * N_CTX + ctx[0]))],
            out_specs=pl.BlockSpec((WIDE, D), lambda k, ctx: (k, 0)),
        ),
        out_shape=pltpu.HBM((4 * WIDE, D), BF),
        compiler_params=pltpu.CompilerParams(vmem_limit_bytes=VMEM_BYTES),
    )(ctx_s, w_project)


def own_rows(ctx_s, w_out):
    return pl.pallas_call(
        copy_kernel,
        grid_spec=pltpu.PrefetchScalarGridSpec(
            num_scalar_prefetch=1,
            grid=(1,),
            in_specs=[pl.BlockSpec((WIDE, D), lambda k, ctx: (ctx[0], 0))],
            out_specs=pl.BlockSpec((WIDE, D), lambda k, ctx: (0, 0)),
        ),
        out_shape=pltpu.HBM((WIDE, D), BF),
        compiler_params=pltpu.CompilerParams(vmem_limit_bytes=VMEM_BYTES),
    )(ctx_s, w_out)


def rows_back(ctx_s, place, w_project, w_out, parts, late):
    cols = 256
    whole = pl.BlockSpec(memory_space=pltpu.VMEM)
    return pl.pallas_call(
        skip(rows_kernel, 14, 1),
        grid=(D // cols,),
        in_specs=[
            pl.BlockSpec(memory_space=pltpu.SMEM),
            whole,
            pl.BlockSpec((cols, 4 * D), lambda n: (n, 0)),
            pl.BlockSpec((D, cols), lambda n: (0, n)),
        ]
        + [whole] * 10
        + [pl.BlockSpec(memory_space=pl.ANY)],
        out_specs=pl.BlockSpec((2 * R, cols), lambda n: (0, n)),
        out_shape=pltpu.HBM((2 * R, D), BF),
        scratch_shapes=[pltpu.VMEM((R, D), BF), pltpu.VMEM((4 * D, R), BF)],
        compiler_params=pltpu.CompilerParams(vmem_limit_bytes=VMEM_BYTES),
    )(ctx_s, place, w_project, w_out, *parts, late)


def across(x, axis):
    return lax.all_to_all(x, axis, split_axis=0, concat_axis=0, tiled=True)


def local(history, grad_output, lengths, send_order, place_order, w_project, w_out):
    ctx_s = lax.axis_index("ctx").astype(jnp.int32).reshape(1)
    history, grad_output = hbm(history), hbm(grad_output)
    w_project, w_out = hbm(w_project), hbm(w_out)
    order = send_order.reshape(1, R)
    place = place_order.reshape(1, R)

    (packed,) = call(pack_kernel, [((2 * R, D), BF)], history, grad_output, order)
    w_own, w_out_own = own_weights(ctx_s, w_project), own_rows(ctx_s, w_out)
    arrived = across(packed, "dp")
    (shard,) = call(place_kernel, [((2 * D, R), BF)], arrived, place, late=(w_own, w_out_own))
    xn, up, slopes, proj, att, gh, sums = call(
        forward_kernel,
        [
            ((D, GROUP), BF),
            ((D, GROUP), BF),
            ((4 * WIDE, GROUP), BF),
            ((4 * WIDE, GROUP), BF),
            ((WIDE, GROUP), F32),
            ((WIDE, GROUP), F32),
            ((8, GROUP), F32),
        ],
        lengths,
        ctx_s,
        *[hbm(v) for v in (w_own, w_out_own, *ring_gather(shard))],
        smem=2,
    )
    all_sums = [sums] + [send(sums, step, 0) for step in (2, 1, 3)]
    all_sums += [send(v, 0, 1) for v in all_sums]
    own, other, up_part, down_part, far_up, far_down, weights = call(
        backward_kernel,
        [
            ((PART, R), BF),
            ((PART, R), BF),
            ((2 * PART, R), BF),
            ((2 * PART, R), BF),
            ((PART, R), BF),
            ((PART, R), BF),
            ((N_DP, 80, 4 * WIDE), BF),
        ],
        lengths,
        ctx_s,
        *[hbm(v) for v in (slopes, proj, att, gh)],
        *all_sums,
        hbm(xn),
        hbm(up),
        smem=2,
        plain=2,
        scratch=[
            pltpu.VMEM((PART, GROUP), BF),
            pltpu.VMEM((WIDE, GROUP), BF),
            pltpu.VMEM((WIDE, GROUP), F32),
            pltpu.VMEM((WIDE, GROUP), F32),
            pltpu.VMEM((D, GROUP), BF),
            pltpu.VMEM((D, GROUP), BF),
            pltpu.SemaphoreType.DMA((2,)),
        ],
    )
    parts = relay(own, other, (up_part, down_part), (far_up, far_down))
    project, mixing = call(
        sum_kernel,
        [((64, 4 * WIDE), F32), ((8, D), F32)],
        across(weights, "dp"),
        late=parts[1:],
    )
    owners = [(d * 8 + c, (2 * c + d // 8) * 8 + d % 8) for d in range(N_DP) for c in range(N_CTX)]
    mixing_grad = lax.ppermute(mixing, ("dp", "ctx"), owners)
    project_all = lax.all_gather(project, "ctx")
    rows = rows_back(ctx_s, place, w_project, w_out, parts, project)
    returned = across(rows, "dp")
    output, input_grad = call(
        unpack_kernel, [((R, D), BF), ((R, D), BF)], returned, history, grad_output, order
    )
    (project_grad,) = call(join_kernel, [((8, 4 * D), F32)], ctx_s, project_all, smem=1)
    return output, input_grad, project_grad, mixing_grad


def solution(mesh):
    rows = P(("dp", "ctx"), None)
    ids = P(("dp", "ctx"))
    return jax.shard_map(
        local,
        mesh=mesh,
        in_specs=(rows, rows, P("dp", None), ids, ids, P(), P()),
        out_specs=(rows, rows, rows, rows),
        check_vma=False,
    )
```

time: 175 us -> 157 us (0.90)
  starting transfers between devices: 62.5 us -> 38.7 us
  between operations: 0.98 us -> 14.3 us
  local copies, waits for them, and re-layouts: 18.9 us -> 7.83 us
  Pallas kernels: 31.1 us -> 40.1 us
  waiting for transfers between devices: 58 us -> 55.6 us
    ppermute x39 -> x27, starting transfers between devices: 39.2 us -> 15.2 us  [send(): return lax.ppermute(x, 'ctx', pairs)]
    ppermute x39 -> x27, waiting for transfers between devices: 24 us -> 41.3 us  [send(): return lax.ppermute(x, 'ctx', pairs)]
    all_to_all x3, waiting for transfers between devices: 24.1 us -> 7.67 us  [across(): return lax.all_to_all(x, axis, split_axis=0, concat_axis=0, tiled=True)]
    pallas_call x10, Pallas kernels: 31.1 us -> 40.1 us  [the longest x7 27.3 us: call(): pl.pallas_call(skip(body, len(args), len(late)), out_shape=[pltpu.HBM(s,...]
    unnamed x41 -> x49, local copies, waits for them, and re-layouts: 13.3 us -> 7.8 us
    ppermute x1, waiting for transfers between devices: 9.91 us -> 6.67 us  [local(): mixing_grad = lax.ppermute(mixing, ('dp', 'ctx'), owners)]
    slice x4 -> x2, local copies, waits for them, and re-layouts: 2.5 us -> 0.04 us  [ring_gather(): far = (send(up[:half], 3, 0), send(down[half:], 1, 0))]
    dynamic_slice x2 -> x0, local copies, waits for them, and re-layouts: 2.21 us -> none  [the longest x1 2.18 us: local(): lax.dynamic_slice_in_dim(w_project, kind * D + first, WIDE, 1)]
  transfers between devices with their start and end apart: 43 -> 32, of which waited for: 15 -> 14; matrix products, arithmetic and copies ran while one was open for 8% -> 0% of each run, Pallas kernels for 6% -> 10%
where the time goes in v2:
time: 157 us
  waiting for transfers between devices  55.6 us (35%)
  Pallas kernels  40.1 us (26%)
  starting transfers between devices  38.7 us (25%)
  between operations  14.3 us (9%)
  local copies, waits for them, and re-layouts  7.83 us (5%)
    ppermute x27, waiting for transfers between devices, send(): return lax.ppermute(x, 'ctx', pairs)  41.3 us
    pallas_call x7, Pallas kernels, call(): pl.pallas_call(skip(body, len(args), len(late)), out_shape=[pltpu.HBM(s,...  27.3 us
    all_to_all x3, starting transfers between devices, across(): return lax.all_to_all(x, axis, split_axis=0, concat_axis=0, tiled=True)  18.7 us
    ppermute x27, starting transfers between devices, send(): return lax.ppermute(x, 'ctx', pairs)  15.2 us
    unnamed x49, local copies, waits for them, and re-layouts  7.8 us
    all_to_all x3, waiting for transfers between devices, across(): return lax.all_to_all(x, axis, split_axis=0, concat_axis=0, tiled=True)  7.67 us
    pallas_call x1, Pallas kernels, rows_back(): pl.pallas_call(skip(rows_kernel, 14, 1), grid=(D // cols,), in_specs=[pl....  7.45 us
    ppermute x1, waiting for transfers between devices, local(): mixing_grad = lax.ppermute(mixing, ('dp', 'ctx'), owners)  6.67 us
  transfers between devices with their start and end apart: 32, of which 14 were waited for; matrix products, arithmetic and copies ran while one was open for 0% of the time, Pallas kernels for 10%

profile of v2, /device:TPU:6, one launch (start us, length us, event | category | flops | bytes accessed | tf_op | source)
XLA Modules:
  0.0 156.5 jit_solution(13755020008220917208)
XLA Ops:
  7.2 0.0 copy-start.8
  7.2 0.6 copy-done.8
  7.8 2.4 %shard_map.104 = bf16[256,1024]{1,0:T(8,128)(2,1)} custom-call(bf16[128,1024]{1,0:T(8,128)(2,1)} %hist.3, bf16[128,1024]{1,0:T(8,128)(2,1)} %gout.3, s32[1,128]{1,0:T(1,128)S(1)} %bitcast.13), custom_call_target="tpu_custom_call" | custom-call | tf_op jit(solution)/shard_map/pallas_call | solution.py:59
  10.2 8.0 %all-to-all-start = ((bf16[16,16,1024]{2,1,0:T(8,128)(2,1)}), bf16[16,16,1024]{2,1,0:T(8,128)(2,1)S(1)}, u32[]{:S(2)}, u32[]{:S(2)}) async-start(bf16[16,16,1024]{2,1,0:T(8,128)(2,1)} %bitcast.15), calls=%async_computation | async-start | bytes 1048576 | tf_op jit(solution)/shard_map/all_to_all | solution.py:400
  18.2 1.7 %shard_map.103.refs_3_.w_out = bf16[128,1024]{1,0:T(8,128)(2,1)} custom-call(s32[1]{0:T(128)} %bitcast.ctx.refs_0_, bf16[1024,1024]{1,0:T(8,128)(2,1)} %refs_3_.1), custom_call_target="tpu_custom_call" | custom-call | tf_op jit(solution)/shard_map/pallas_call | solution.py:365
  19.9 3.7 %shard_map.102.refs_2_.wt = bf16[512,1024]{1,0:T(8,128)(2,1)} custom-call(s32[1]{0:T(128)} %bitcast.ctx.refs_0_, bf16[1024,4096]{1,0:T(8,128)(2,1)} %refs_2_.1), custom_call_target="tpu_custom_call" | custom-call | tf_op jit(solution)/shard_map/pallas_call | solution.py:351
  23.6 6.2 %all-to-all-done = bf16[16,16,1024]{2,1,0:T(8,128)(2,1)S(1)} async-done(((bf16[16,16,1024]{2,1,0:T(8,128)(2,1)}), bf16[16,16,1024]{2,1,0:T(8,128)(2,1)S(1)}, u32[]{:S(2)}, u32[]{:S(2)}) %all-to-all-start) | async-done | bytes 524320 | tf_op jit(solution)/shard_map/all_to_all | solution.py:400
  29.8 1.2 copy-done
  31.0 1.2 shard_map.105.refs_0_
  32.2 0.5 collective-permute-start.4
  32.7 1.5 collective-permute-start.1
  34.3 0.0 collective-permute-start
  34.3 10.5 %collective-permute-done.4.refs_8_ = bf16[2048,128]{1,0:T(8,128)(2,1)S(1)} collective-permute-done((bf16[2048,128]{1,0:T(8,128)(2,1)}, bf16[2048,128]{1,0:T(8,128)(2,1)S(1)}, u32[]{:S(2)}, u32[]{:S(2)}) %collective-permute-start.4) | collective-permute-done | bytes 524320 | tf_op jit(solution)/shard_map/ppermute | solution.py:79
  44.8 1.8 %collective-permute-start.5 = (bf16[1024,128]{1,0:T(8,128)(2,1)S(1)}, bf16[1024,128]{1,0:T(8,128)(2,1)S(1)}, u32[]{:S(2)}, u32[]{:S(2)}) collective-permute-start(bf16[1024,128]{1,0:T(8,128)(2,1)S(1)} %slice.9), channel_id=1, source_target_pairs={{0,2},{1,3},{2,4},{3,5},{4,6},{5,7},{6,0},{7,1},{8,10},{9,11},{10,... | collective-permute-start | bytes 786440 | tf_op jit(solution)/shard_map/ppermute | solution.py:79
  46.6 0.4 collective-permute-start.3
  47.0 0.0 collective-permute-start.8
  47.0 0.5 collective-permute-start.2
  47.5 3.7 %collective-permute-done.5.refs_5_ = bf16[1024,128]{1,0:T(8,128)(2,1)S(1)} collective-permute-done((bf16[1024,128]{1,0:T(8,128)(2,1)S(1)}, bf16[1024,128]{1,0:T(8,128)(2,1)S(1)}, u32[]{:S(2)}, u32[]{:S(2)}) %collective-permute-start.5) | collective-permute-done | bytes 262176 | tf_op jit(solution)/shard_map/ppermute | solution.py:79
  51.3 0.0 collective-permute-start.7
  51.3 3.0 %collective-permute-done.3.refs_4_ = bf16[1024,128]{1,0:T(8,128)(2,1)S(1)} collective-permute-done((bf16[1024,128]{1,0:T(8,128)(2,1)S(1)}, bf16[1024,128]{1,0:T(8,128)(2,1)S(1)}, u32[]{:S(2)}, u32[]{:S(2)}) %collective-permute-start.3) | collective-permute-done | bytes 262176 | tf_op jit(solution)/shard_map/ppermute | solution.py:79
  54.3 0.0 collective-permute-done.refs_1_
  54.3 0.0 collective-permute-done.8.refs_9_
  54.3 1.5 collective-permute-done.6.refs_6_
  55.9 0.7 copy-done.18
  56.5 0.8 copy-done.14
  57.3 9.1 %shard_map.106 = (bf16[1024,1024]{1,0:T(8,128)(2,1)}, bf16[1024,1024]{1,0:T(8,128)(2,1)}, bf16[512,1024]{1,0:T(8,128)(2,1)}, bf16[512,1024]{1,0:T(8,128)(2,1)}, ...) custom-call(s32[1,4]{1,0:T(1,128)S(1)} %copy-done.6, s32[1]{0:T(128)} %bitcast.ctx.refs_0_, ...), custom_call_target="tpu_custom_call" | custom-call | tf_op jit(solution)/shard_map/pallas_call | solution.py:59
  66.4 3.2 %collective-permute-start.10 = (f32[8,1024]{1,0:T(8,128)}, f32[8,1024]{1,0:T(8,128)S(1)}, u32[]{:S(2)}, u32[]{:S(2)}) collective-permute-start(f32[8,1024]{1,0:T(8,128)} %get-tuple-element.26.refs_0_), channel_id=1, source_target_pairs={{0,2},{1,3},{2,4},{3,5},{4,6},{5,7},{6,0},{7,1},{8,10},{9,11},{10,... | collective-permute-start | bytes 98312 | tf_op jit(solution)/shard_map/ppermute | solution.py:79
  69.7 0.0 collective-permute-start.9
  69.7 0.0 collective-permute-start.12
  69.7 2.1 %collective-permute-done.11.refs_3_ = f32[8,1024]{1,0:T(8,128)S(1)} collective-permute-done((f32[8,1024]{1,0:T(8,128)}, f32[8,1024]{1,0:T(8,128)S(1)}, u32[]{:S(2)}, u32[]{:S(2)}) %collective-permute-start.11) | collective-permute-done | bytes 32800 | tf_op jit(solution)/shard_map/ppermute | solution.py:79
  71.8 0.5 collective-permute-start.14
  72.3 3.0 %collective-permute-done.9.refs_1_ = f32[8,1024]{1,0:T(8,128)S(1)} collective-permute-done((f32[8,1024]{1,0:T(8,128)}, f32[8,1024]{1,0:T(8,128)S(1)}, u32[]{:S(2)}, u32[]{:S(2)}) %collective-permute-start.9) | collective-permute-done | bytes 32800 | tf_op jit(solution)/shard_map/ppermute | solution.py:79
  75.3 0.0 collective-permute-start.13
  75.3 1.2 collective-permute-done.13.refs_5_
  76.5 0.8 copy-done.5
  77.3 10.9 %shard_map.107 = (bf16[640,128]{1,0:T(8,128)(2,1)}, bf16[640,128]{1,0:T(8,128)(2,1)}, bf16[1280,128]{1,0:T(8,128)(2,1)}, bf16[1280,128]{1,0:T(8,128)(2,1)}, bf16...) custom-call(s32[1,4]{1,0:T(1,128)S(1)} %copy-done.6, s32[1]{0:T(128)} %bitcast.ctx.refs_0_, ...), custom_call_target="tpu_custom_call" | custom-call | tf_op jit(solution)/shard_map/pallas_call | solution.py:59
  88.2 3.8 %all-to-all-start.1 = ((bf16[16,80,512]{2,1,0:T(8,128)(2,1)}), bf16[16,80,512]{2,1,0:T(8,128)(2,1)S(1)}, u32[]{:S(2)}, u32[]{:S(2)}) async-start(bf16[16,80,512]{2,1,0:T(8,128)(2,1)} %get-tuple-element.35), calls=%async_computation.1 | async-start | bytes 2621440 | tf_op jit(solution)/shard_map/all_to_all | solution.py:400
  92.0 0.0 all-gather.3.cloned.1.call-start
  92.1 0.3 collective-permute-start.17
  92.4 1.8 %collective-permute-start.19 = (bf16[1280,128]{1,0:T(8,128)(2,1)S(1)}, bf16[1280,128]{1,0:T(8,128)(2,1)S(1)}, u32[]{:S(2)}, u32[]{:S(2)}) collective-permute-start(bf16[1280,128]{1,0:T(8,128)(2,1)S(1)} %copy-done.19), channel_id=1, source_target_pairs={{0,6},{1,7},{2,0},{3,1},{4,2},{5,3},{6,4},{7,5},{8,14},{9,15},{10,... | collective-permute-start | bytes 983048 | tf_op jit(solution)/shard_map/ppermute | solution.py:79
  94.2 1.4 collective-permute-start.21
  95.6 0.6 collective-permute-start.24
  96.2 9.2 %collective-permute-done.21 = bf16[640,128]{1,0:T(8,128)(2,1)S(1)} collective-permute-done((bf16[640,128]{1,0:T(8,128)(2,1)S(1)}, bf16[640,128]{1,0:T(8,128)(2,1)S(1)}, u32[]{:S(2)}, u32[]{:S(2)}) %collective-permute-start.21) | collective-permute-done | bytes 163872 | tf_op jit(solution)/shard_map/ppermute | solution.py:79
  105.4 1.6 %collective-permute-start.22 = (bf16[640,128]{1,0:T(8,128)(2,1)S(1)}, bf16[640,128]{1,0:T(8,128)(2,1)S(1)}, u32[]{:S(2)}, u32[]{:S(2)}) collective-permute-start(bf16[640,128]{1,0:T(8,128)(2,1)S(1)} %collective-permute-done.21), channel_id=1, source_target_pairs={{0,2},{1,3},{2,4},{3,5},{4,6},{5,7},{6,0},{7,1},{8,10},{9,11},{10,... | collective-permute-start | bytes 491528 | tf_op jit(solution)/shard_map/ppermute | solution.py:79
  107.1 0.4 collective-permute-start.25
  107.5 0.5 collective-permute-start.20
  108.0 0.1 collective-permute-start.16
  108.1 2.8 %collective-permute-done.22.refs_6_.refs_10_ = bf16[640,128]{1,0:T(8,128)(2,1)S(1)} collective-permute-done((bf16[640,128]{1,0:T(8,128)(2,1)S(1)}, bf16[640,128]{1,0:T(8,128)(2,1)S(1)}, u32[]{:S(2)}, u32[]{:S(2)}) %collective-permute-start.22) | collective-permute-done | bytes 163872 | tf_op jit(solution)/shard_map/ppermute | solution.py:79
  110.9 2.8 %collective-permute-done.25.refs_8_.refs_12_ = bf16[640,128]{1,0:T(8,128)(2,1)S(1)} collective-permute-done((bf16[640,128]{1,0:T(8,128)(2,1)S(1)}, bf16[640,128]{1,0:T(8,128)(2,1)S(1)}, u32[]{:S(2)}, u32[]{:S(2)}) %collective-permute-start.25) | collective-permute-done | bytes 163872 | tf_op jit(solution)/shard_map/ppermute | solution.py:79
  113.7 1.4 collective-permute-done.26.refs_9_.refs_13_
  115.1 0.8 shard_map.108
  115.9 0.0 all-gather.3.cloned.1.call-update
  115.9 0.0 copy-start.3
  115.9 0.9 copy-done.3
  116.8 0.9 copy-done.4
  117.7 7.5 %shard_map.109 = bf16[256,1024]{1,0:T(8,128)(2,1)} custom-call(s32[1]{0:T(128)} %bitcast.ctx.refs_0_, s32[1,128]{1,0:T(1,128)S(1)} %bitcast.12, bf16[1024,4096]{1,0:T(8,128)(2,1)} %refs_2_.1, bf16[1024,1024]{1,0:T(8,128)(2,1)} %refs_3_.1, bf16[640,128]{1,0:T(8,128)(2,1)S(1)} %copy-done.4, bf16[640,128]{1,0:T(8,128)(2,1)S(1)} %collective-permute-done.16.refs_1_.refs_5_, ...), custom_call_target="tpu_custom_call" | custom-call | tf_op jit(solution)/shard_map/pallas_call | solution.py:381
  125.2 6.8 %all-to-all-start.2 = ((bf16[16,16,1024]{2,1,0:T(8,128)(2,1)}), bf16[16,16,1024]{2,1,0:T(8,128)(2,1)S(1)}, u32[]{:S(2)}, u32[]{:S(2)}) async-start(bf16[16,16,1024]{2,1,0:T(8,128)(2,1)} %bitcast.16), calls=%async_computation.2 | async-start | bytes 1048576 | tf_op jit(solution)/shard_map/all_to_all | solution.py:400
  132.0 4.7 %collective-permute-start.27 = (f32[8,1024]{1,0:T(8,128)S(1)}, f32[8,1024]{1,0:T(8,128)S(1)}, u32[]{:S(2)}, u32[]{:S(2)}) collective-permute-start(f32[8,1024]{1,0:T(8,128)S(1)} %copy-done.23), channel_id=1, source_target_pairs={{0,0},{1,16},{2,32},{3,48},{4,64},{5,80},{6,96},{7,112},{8,1},{9,1... | collective-permute-start | bytes 98312 | tf_op jit(solution)/shard_map/ppermute | solution.py:469
  136.7 6.7 %collective-permute-done.27 = f32[8,1024]{1,0:T(8,128)S(1)} collective-permute-done((f32[8,1024]{1,0:T(8,128)S(1)}, f32[8,1024]{1,0:T(8,128)S(1)}, u32[]{:S(2)}, u32[]{:S(2)}) %collective-permute-start.27) | collective-permute-done | bytes 32800 | tf_op jit(solution)/shard_map/ppermute | solution.py:469
  143.4 1.5 all-to-all-done.2
  144.9 2.3 %shard_map.110 = (bf16[128,1024]{1,0:T(8,128)(2,1)}, bf16[128,1024]{1,0:T(8,128)(2,1)}) custom-call(bf16[256,1024]{1,0:T(8,128)(2,1)S(1)} %bitcast.9, bf16[128,1024]{1,0:T(8,128)(2,1)} %hist.3, bf16[128,1024]{1,0:T(8,128)(2,1)} %gout.3, s32[1,128]{1,0:T(1,128)S(1)} %bitcast.14), custom_call_target="tpu_custom_call" | custom-call | tf_op jit(solution)/shard_map/pallas_call | solution.py:59
  147.2 1.2 copy-done.2
  148.4 0.7 shard_map.111
  149.1 0.6 copy.12
  (62 shorter events, 0.2 us)
Async XLA Ops:
  7.2 0.7 copy-start.8
  10.2 19.6 %all-to-all-start = ((bf16[16,16,1024]{2,1,0:T(8,128)(2,1)}), bf16[16,16,1024]{2,1,0:T(8,128)(2,1)S(1)}, u32[]{:S(2)}, u32[]{:S(2)}) async-start(bf16[16,16,1024]{2,1,0:T(8,128)(2,1)} %bitcast.15), calls=%async_computation | async-start | bytes 1048576 | tf_op jit(solution)/shard_map/all_to_all | solution.py:400
  19.9 9.9 %copy-start.1 = (bf16[128,1024]{1,0:T(8,128)(2,1)S(1)}, bf16[128,1024]{1,0:T(8,128)(2,1)}, u32[]{:S(2)}) copy-start(bf16[128,1024]{1,0:T(8,128)(2,1)} %shard_map.103.refs_3_.w_out) | copy-start | bytes 786436
  19.9 9.9 %copy-start.7 = (s32[128]{0:T(128)S(1)}, s32[128]{0:T(128)}, u32[]{:S(2)}) copy-start(s32[128]{0:T(128)} %param.11) | copy-start | bytes 1540
  23.6 33.7 %copy-start.6 = (s32[1,4]{1,0:T(1,128)S(1)}, s32[1,4]{1,0:T(1,128)}, u32[]{:S(2)}) copy-start(s32[1,4]{1,0:T(1,128)} %lengths.3) | copy-start | bytes 52
  29.8 1.2 copy-start
  32.2 12.6 %collective-permute-start.4 = (bf16[2048,128]{1,0:T(8,128)(2,1)}, bf16[2048,128]{1,0:T(8,128)(2,1)S(1)}, u32[]{:S(2)}, u32[]{:S(2)}) collective-permute-start(bf16[2048,128]{1,0:T(8,128)(2,1)} %shard_map.105.refs_0_), channel_id=1, source_target_pairs={{0,2},{1,3},{2,4},{3,5},{4,6},{5,7},{6,0},{7,1},{8,10},{9,11},{10,... | collective-permute-start | bytes 1572872 | tf_op jit(solution)/shard_map/ppermute | solution.py:79
  32.7 13.9 %collective-permute-start.1 = (bf16[2048,128]{1,0:T(8,128)(2,1)}, bf16[2048,128]{1,0:T(8,128)(2,1)S(1)}, u32[]{:S(2)}, u32[]{:S(2)}) collective-permute-start(bf16[2048,128]{1,0:T(8,128)(2,1)} %shard_map.105.refs_0_), channel_id=1, source_target_pairs={{0,6},{1,7},{2,0},{3,1},{4,2},{5,3},{6,4},{7,5},{8,14},{9,15},{10,... | collective-permute-start | bytes 1572872 | tf_op jit(solution)/shard_map/ppermute | solution.py:79
  34.3 20.0 %collective-permute-start = (bf16[2048,128]{1,0:T(8,128)(2,1)}, bf16[2048,128]{1,0:T(8,128)(2,1)S(1)}, u32[]{:S(2)}, u32[]{:S(2)}) collective-permute-start(bf16[2048,128]{1,0:T(8,128)(2,1)} %shard_map.105.refs_0_), channel_id=1, source_target_pairs={{0,1},{1,0},{2,3},{3,2},{4,5},{5,4},{6,7},{7,6},{8,9},{9,8},{10,11... | collective-permute-start | bytes 1572872 | tf_op jit(solution)/shard_map/ppermute | solution.py:79
  44.8 11.0 %copy-start.10 = (bf16[2048,128]{1,0:T(8,128)(2,1)}, bf16[2048,128]{1,0:T(8,128)(2,1)S(1)}, u32[]{:S(2)}) copy-start(bf16[2048,128]{1,0:T(8,128)(2,1)S(1)} %collective-permute-done.4.refs_8_) | copy-start | bytes 1572868
  44.8 6.4 %collective-permute-start.5 = (bf16[1024,128]{1,0:T(8,128)(2,1)S(1)}, bf16[1024,128]{1,0:T(8,128)(2,1)S(1)}, u32[]{:S(2)}, u32[]{:S(2)}) collective-permute-start(bf16[1024,128]{1,0:T(8,128)(2,1)S(1)} %slice.9), channel_id=1, source_target_pairs={{0,2},{1,3},{2,4},{3,5},{4,6},{5,7},{6,0},{7,1},{8,10},{9,11},{10,... | collective-permute-start | bytes 786440 | tf_op jit(solution)/shard_map/ppermute | solution.py:79
  46.6 9.2 %copy-start.11 = (bf16[2048,128]{1,0:T(8,128)(2,1)}, bf16[2048,128]{1,0:T(8,128)(2,1)S(1)}, u32[]{:S(2)}) copy-start(bf16[2048,128]{1,0:T(8,128)(2,1)S(1)} %collective-permute-done.1.refs_2_) | copy-start | bytes 1572868
  46.6 7.7 %collective-permute-start.3 = (bf16[1024,128]{1,0:T(8,128)(2,1)S(1)}, bf16[1024,128]{1,0:T(8,128)(2,1)S(1)}, u32[]{:S(2)}, u32[]{:S(2)}) collective-permute-start(bf16[1024,128]{1,0:T(8,128)(2,1)S(1)} %slice.8), channel_id=1, source_target_pairs={{0,6},{1,7},{2,0},{3,1},{4,2},{5,3},{6,4},{7,5},{8,14},{9,15},{10,... | collective-permute-start | bytes 786440 | tf_op jit(solution)/shard_map/ppermute | solution.py:79
  47.0 7.3 %collective-permute-start.8 = (bf16[2048,128]{1,0:T(8,128)(2,1)S(1)}, bf16[2048,128]{1,0:T(8,128)(2,1)S(1)}, u32[]{:S(2)}, u32[]{:S(2)}) collective-permute-start(bf16[2048,128]{1,0:T(8,128)(2,1)S(1)} %collective-permute-done.4.refs_8_), channel_id=1, source_target_pairs={{0,1},{1,0},{2,3},{3,2},{4,5},{5,4},{6,7},{7,6},{8,9},{9,8},{10,11... | collective-permute-start | bytes 1572872 | tf_op jit(solution)/shard_map/ppermute | solution.py:79
  47.0 8.8 %collective-permute-start.2 = (bf16[2048,128]{1,0:T(8,128)(2,1)S(1)}, bf16[2048,128]{1,0:T(8,128)(2,1)S(1)}, u32[]{:S(2)}, u32[]{:S(2)}) collective-permute-start(bf16[2048,128]{1,0:T(8,128)(2,1)S(1)} %collective-permute-done.1.refs_2_), channel_id=1, source_target_pairs={{0,1},{1,0},{2,3},{3,2},{4,5},{5,4},{6,7},{7,6},{8,9},{9,8},{10,11... | collective-permute-start | bytes 1572872 | tf_op jit(solution)/shard_map/ppermute | solution.py:79
  51.3 4.6 %copy-start.15 = (bf16[1024,128]{1,0:T(8,128)(2,1)}, bf16[1024,128]{1,0:T(8,128)(2,1)S(1)}, u32[]{:S(2)}) copy-start(bf16[1024,128]{1,0:T(8,128)(2,1)S(1)} %collective-permute-done.5.refs_5_) | copy-start | bytes 786436
  51.3 3.0 %collective-permute-start.7 = (bf16[1024,128]{1,0:T(8,128)(2,1)S(1)}, bf16[1024,128]{1,0:T(8,128)(2,1)S(1)}, u32[]{:S(2)}, u32[]{:S(2)}) collective-permute-start(bf16[1024,128]{1,0:T(8,128)(2,1)S(1)} %collective-permute-done.5.refs_5_), channel_id=1, source_target_pairs={{0,1},{1,0},{2,3},{3,2},{4,5},{5,4},{6,7},{7,6},{8,9},{9,8},{10,11... | collective-permute-start | bytes 786440 | tf_op jit(solution)/shard_map/ppermute | solution.py:79
  54.3 1.6 %copy-start.16 = (bf16[1024,128]{1,0:T(8,128)(2,1)}, bf16[1024,128]{1,0:T(8,128)(2,1)S(1)}, u32[]{:S(2)}) copy-start(bf16[1024,128]{1,0:T(8,128)(2,1)S(1)} %collective-permute-done.3.refs_4_) | copy-start | bytes 786436
  54.3 1.5 collective-permute-start.6
  54.3 1.6 %copy-start.12 = (bf16[2048,128]{1,0:T(8,128)(2,1)}, bf16[2048,128]{1,0:T(8,128)(2,1)S(1)}, u32[]{:S(2)}) copy-start(bf16[2048,128]{1,0:T(8,128)(2,1)S(1)} %collective-permute-done.refs_1_) | copy-start | bytes 1572868
  54.3 1.6 copy-start.17
  54.3 1.5 copy-start.13
  55.8 0.7 copy-start.18
  56.5 0.8 copy-start.14
  66.4 5.3 %collective-permute-start.11 = (f32[8,1024]{1,0:T(8,128)}, f32[8,1024]{1,0:T(8,128)S(1)}, u32[]{:S(2)}, u32[]{:S(2)}) collective-permute-start(f32[8,1024]{1,0:T(8,128)} %get-tuple-element.26.refs_0_), channel_id=1, source_target_pairs={{0,6},{1,7},{2,0},{3,1},{4,2},{5,3},{6,4},{7,5},{8,14},{9,15},{10,... | collective-permute-start | bytes 98312 | tf_op jit(solution)/shard_map/ppermute | solution.py:79
  66.4 5.3 %collective-permute-start.10 = (f32[8,1024]{1,0:T(8,128)}, f32[8,1024]{1,0:T(8,128)S(1)}, u32[]{:S(2)}, u32[]{:S(2)}) collective-permute-start(f32[8,1024]{1,0:T(8,128)} %get-tuple-element.26.refs_0_), channel_id=1, source_target_pairs={{0,2},{1,3},{2,4},{3,5},{4,6},{5,7},{6,0},{7,1},{8,10},{9,11},{10,... | collective-permute-start | bytes 98312 | tf_op jit(solution)/shard_map/ppermute | solution.py:79
  69.7 5.6 %collective-permute-start.9 = (f32[8,1024]{1,0:T(8,128)}, f32[8,1024]{1,0:T(8,128)S(1)}, u32[]{:S(2)}, u32[]{:S(2)}) collective-permute-start(f32[8,1024]{1,0:T(8,128)} %get-tuple-element.26.refs_0_), channel_id=1, source_target_pairs={{0,4},{1,5},{2,6},{3,7},{4,0},{5,1},{6,2},{7,3},{8,12},{9,13},{10,... | collective-permute-start | bytes 98312 | tf_op jit(solution)/shard_map/ppermute | solution.py:79
  69.7 5.6 %collective-permute-start.12 = (f32[8,1024]{1,0:T(8,128)}, f32[8,1024]{1,0:T(8,128)S(1)}, u32[]{:S(2)}, u32[]{:S(2)}) collective-permute-start(f32[8,1024]{1,0:T(8,128)} %get-tuple-element.26.refs_0_), channel_id=1, source_target_pairs={{0,1},{1,0},{2,3},{3,2},{4,5},{5,4},{6,7},{7,6},{8,9},{9,8},{10,11... | collective-permute-start | bytes 98312 | tf_op jit(solution)/shard_map/ppermute | solution.py:79
  71.8 3.5 %collective-permute-start.15 = (f32[8,1024]{1,0:T(8,128)S(1)}, f32[8,1024]{1,0:T(8,128)S(1)}, u32[]{:S(2)}, u32[]{:S(2)}) collective-permute-start(f32[8,1024]{1,0:T(8,128)S(1)} %collective-permute-done.11.refs_3_), channel_id=1, source_target_pairs={{0,1},{1,0},{2,3},{3,2},{4,5},{5,4},{6,7},{7,6},{8,9},{9,8},{10,11... | collective-permute-start | bytes 98312 | tf_op jit(solution)/shard_map/ppermute | solution.py:79
  71.8 3.5 %collective-permute-start.14 = (f32[8,1024]{1,0:T(8,128)S(1)}, f32[8,1024]{1,0:T(8,128)S(1)}, u32[]{:S(2)}, u32[]{:S(2)}) collective-permute-start(f32[8,1024]{1,0:T(8,128)S(1)} %collective-permute-done.10.refs_2_), channel_id=1, source_target_pairs={{0,1},{1,0},{2,3},{3,2},{4,5},{5,4},{6,7},{7,6},{8,9},{9,8},{10,11... | collective-permute-start | bytes 98312 | tf_op jit(solution)/shard_map/ppermute | solution.py:79
  75.3 1.2 collective-permute-start.13
  76.5 0.8 copy-start.5
  88.1 3.9 %copy-start.20 = (bf16[1280,128]{1,0:T(8,128)(2,1)S(1)}, bf16[1280,128]{1,0:T(8,128)(2,1)}, u32[]{:S(2)}) copy-start(bf16[1280,128]{1,0:T(8,128)(2,1)} %get-tuple-element.31) | copy-start | bytes 983044
  88.1 4.2 %copy-start.19 = (bf16[1280,128]{1,0:T(8,128)(2,1)S(1)}, bf16[1280,128]{1,0:T(8,128)(2,1)}, u32[]{:S(2)}) copy-start(bf16[1280,128]{1,0:T(8,128)(2,1)} %get-tuple-element.32) | copy-start | bytes 983044
  88.2 6.0 %copy-start.22 = (bf16[640,128]{1,0:T(8,128)(2,1)S(1)}, bf16[640,128]{1,0:T(8,128)(2,1)}, u32[]{:S(2)}) copy-start(bf16[640,128]{1,0:T(8,128)(2,1)} %get-tuple-element.33) | copy-start | bytes 491524
  88.2 7.5 %copy-start.21 = (bf16[640,128]{1,0:T(8,128)(2,1)S(1)}, bf16[640,128]{1,0:T(8,128)(2,1)}, u32[]{:S(2)}) copy-start(bf16[640,128]{1,0:T(8,128)(2,1)} %get-tuple-element.34) | copy-start | bytes 491524
  88.2 26.9 %all-to-all-start.1 = ((bf16[16,80,512]{2,1,0:T(8,128)(2,1)}), bf16[16,80,512]{2,1,0:T(8,128)(2,1)S(1)}, u32[]{:S(2)}, u32[]{:S(2)}) async-start(bf16[16,80,512]{2,1,0:T(8,128)(2,1)} %get-tuple-element.35), calls=%async_computation.1 | async-start | bytes 2621440 | tf_op jit(solution)/shard_map/all_to_all | solution.py:400
  92.0 55.2 %all-gather.3.cloned.1.call-start = ((), (), s32[]{:S(2)}) async-start(), calls=%async_computation.3 | async-start | bytes 1179648 | tf_op jit(solution)/shard_map/all_gather | solution.py:470
  92.1 15.4 %collective-permute-start.17 = (bf16[1280,128]{1,0:T(8,128)(2,1)S(1)}, bf16[1280,128]{1,0:T(8,128)(2,1)S(1)}, u32[]{:S(2)}, u32[]{:S(2)}) collective-permute-start(bf16[1280,128]{1,0:T(8,128)(2,1)S(1)} %copy-done.20), channel_id=1, source_target_pairs={{0,2},{1,3},{2,4},{3,5},{4,6},{5,7},{6,0},{7,1},{8,10},{9,11},{10,... | collective-permute-start | bytes 983048 | tf_op jit(solution)/shard_map/ppermute | solution.py:79
  92.4 15.1 %collective-permute-start.19 = (bf16[1280,128]{1,0:T(8,128)(2,1)S(1)}, bf16[1280,128]{1,0:T(8,128)(2,1)S(1)}, u32[]{:S(2)}, u32[]{:S(2)}) collective-permute-start(bf16[1280,128]{1,0:T(8,128)(2,1)S(1)} %copy-done.19), channel_id=1, source_target_pairs={{0,6},{1,7},{2,0},{3,1},{4,2},{5,3},{6,4},{7,5},{8,14},{9,15},{10,... | collective-permute-start | bytes 983048 | tf_op jit(solution)/shard_map/ppermute | solution.py:79
  94.2 11.3 %collective-permute-start.21 = (bf16[640,128]{1,0:T(8,128)(2,1)S(1)}, bf16[640,128]{1,0:T(8,128)(2,1)S(1)}, u32[]{:S(2)}, u32[]{:S(2)}) collective-permute-start(bf16[640,128]{1,0:T(8,128)(2,1)S(1)} %copy-done.22), channel_id=1, source_target_pairs={{0,2},{1,3},{2,4},{3,5},{4,6},{5,7},{6,0},{7,1},{8,10},{9,11},{10,... | collective-permute-start | bytes 491528 | tf_op jit(solution)/shard_map/ppermute | solution.py:79
  95.6 11.4 %collective-permute-start.24 = (bf16[640,128]{1,0:T(8,128)(2,1)S(1)}, bf16[640,128]{1,0:T(8,128)(2,1)S(1)}, u32[]{:S(2)}, u32[]{:S(2)}) collective-permute-start(bf16[640,128]{1,0:T(8,128)(2,1)S(1)} %copy-done.21), channel_id=1, source_target_pairs={{0,6},{1,7},{2,0},{3,1},{4,2},{5,3},{6,4},{7,5},{8,14},{9,15},{10,... | collective-permute-start | bytes 491528 | tf_op jit(solution)/shard_map/ppermute | solution.py:79
  105.4 5.4 %collective-permute-start.22 = (bf16[640,128]{1,0:T(8,128)(2,1)S(1)}, bf16[640,128]{1,0:T(8,128)(2,1)S(1)}, u32[]{:S(2)}, u32[]{:S(2)}) collective-permute-start(bf16[640,128]{1,0:T(8,128)(2,1)S(1)} %collective-permute-done.21), channel_id=1, source_target_pairs={{0,2},{1,3},{2,4},{3,5},{4,6},{5,7},{6,0},{7,1},{8,10},{9,11},{10,... | collective-permute-start | bytes 491528 | tf_op jit(solution)/shard_map/ppermute | solution.py:79
  107.1 6.6 %collective-permute-start.25 = (bf16[640,128]{1,0:T(8,128)(2,1)S(1)}, bf16[640,128]{1,0:T(8,128)(2,1)S(1)}, u32[]{:S(2)}, u32[]{:S(2)}) collective-permute-start(bf16[640,128]{1,0:T(8,128)(2,1)S(1)} %collective-permute-done.24), channel_id=1, source_target_pairs={{0,6},{1,7},{2,0},{3,1},{4,2},{5,3},{6,4},{7,5},{8,14},{9,15},{10,... | collective-permute-start | bytes 491528 | tf_op jit(solution)/shard_map/ppermute | solution.py:79
  107.5 7.6 %collective-permute-start.18 = (bf16[1280,128]{1,0:T(8,128)(2,1)S(1)}, bf16[1280,128]{1,0:T(8,128)(2,1)S(1)}, u32[]{:S(2)}, u32[]{:S(2)}) collective-permute-start(bf16[1280,128]{1,0:T(8,128)(2,1)S(1)} %collective-permute-done.17.refs_2_.refs_6_), channel_id=1, source_target_pairs={{0,1},{1,0},{2,3},{3,2},{4,5},{5,4},{6,7},{7,6},{8,9},{9,8},{10,11... | collective-permute-start | bytes 983048 | tf_op jit(solution)/shard_map/ppermute | solution.py:79
  107.5 7.6 %collective-permute-start.20 = (bf16[1280,128]{1,0:T(8,128)(2,1)S(1)}, bf16[1280,128]{1,0:T(8,128)(2,1)S(1)}, u32[]{:S(2)}, u32[]{:S(2)}) collective-permute-start(bf16[1280,128]{1,0:T(8,128)(2,1)S(1)} %collective-permute-done.19.refs_4_.refs_8_), channel_id=1, source_target_pairs={{0,1},{1,0},{2,3},{3,2},{4,5},{5,4},{6,7},{7,6},{8,9},{9,8},{10,11... | collective-permute-start | bytes 983048 | tf_op jit(solution)/shard_map/ppermute | solution.py:79
  108.0 5.7 %collective-permute-start.16 = (bf16[640,128]{1,0:T(8,128)(2,1)}, bf16[640,128]{1,0:T(8,128)(2,1)S(1)}, u32[]{:S(2)}, u32[]{:S(2)}) collective-permute-start(bf16[640,128]{1,0:T(8,128)(2,1)} %get-tuple-element.30), channel_id=1, source_target_pairs={{0,1},{1,0},{2,3},{3,2},{4,5},{5,4},{6,7},{7,6},{8,9},{9,8},{10,11... | collective-permute-start | bytes 491528 | tf_op jit(solution)/shard_map/ppermute | solution.py:79
  110.9 2.8 %collective-permute-start.23 = (bf16[640,128]{1,0:T(8,128)(2,1)S(1)}, bf16[640,128]{1,0:T(8,128)(2,1)S(1)}, u32[]{:S(2)}, u32[]{:S(2)}) collective-permute-start(bf16[640,128]{1,0:T(8,128)(2,1)S(1)} %collective-permute-done.22.refs_6_.refs_10_), channel_id=1, source_target_pairs={{0,1},{1,0},{2,3},{3,2},{4,5},{5,4},{6,7},{7,6},{8,9},{9,8},{10,11... | collective-permute-start | bytes 491528 | tf_op jit(solution)/shard_map/ppermute | solution.py:79
  113.6 1.4 collective-permute-start.26
  115.9 0.9 copy-start.3
  116.8 0.9 copy-start.4
  117.7 14.3 %copy-start.23 = (f32[8,1024]{1,0:T(8,128)S(1)}, f32[8,1024]{1,0:T(8,128)}, u32[]{:S(2)}) copy-start(f32[8,1024]{1,0:T(8,128)} %get-tuple-element.39) | copy-start | bytes 98308
  117.7 27.2 %copy-start.9 = (s32[128]{0:T(128)S(1)}, s32[128]{0:T(128)}, u32[]{:S(2)}) copy-start(s32[128]{0:T(128)} %param.10) | copy-start | bytes 1540
  125.2 19.7 %all-to-all-start.2 = ((bf16[16,16,1024]{2,1,0:T(8,128)(2,1)}), bf16[16,16,1024]{2,1,0:T(8,128)(2,1)S(1)}, u32[]{:S(2)}, u32[]{:S(2)}) async-start(bf16[16,16,1024]{2,1,0:T(8,128)(2,1)} %bitcast.16), calls=%async_computation.2 | async-start | bytes 1048576 | tf_op jit(solution)/shard_map/all_to_all | solution.py:400
  132.0 11.4 %collective-permute-start.27 = (f32[8,1024]{1,0:T(8,128)S(1)}, f32[8,1024]{1,0:T(8,128)S(1)}, u32[]{:S(2)}, u32[]{:S(2)}) collective-permute-start(f32[8,1024]{1,0:T(8,128)S(1)} %copy-done.23), channel_id=1, source_target_pairs={{0,0},{1,16},{2,32},{3,48},{4,64},{5,80},{6,96},{7,112},{8,1},{9,1... | collective-permute-start | bytes 98312 | tf_op jit(solution)/shard_map/ppermute | solution.py:469
  147.2 1.2 copy-start.2
Sparse Core Ops, SparseCore 0:
  116.0 22.4 all-gather.2

commit v3 on v2

--- a/solution.py
+++ b/solution.py
@@ -79,14 +79,14 @@
     return lax.ppermute(x, "ctx", pairs)
 
 
-def ring_gather(x):
-    half = x.shape[0] // 2
-    up = send(x, 3, 0)
-    down = send(x, 1, 0)
-    far = (send(up[:half], 3, 0), send(down[half:], 1, 0))
-    shards = [x, send(x, 0, 1), up, send(up, 0, 1), *far]
-    shards += [send(far[0], 0, 1), send(far[1], 0, 1), down, send(down, 0, 1)]
-    return shards
+def ring_gather(a, b):
+    a_up, b_down = send(a, 3, 0), send(b, 1, 0)
+    a_far, b_far = send(a_up, 3, 0), send(b_down, 1, 0)
+    b_up, a_down = send(b, 3, 0), send(a, 1, 0)
+    got = []
+    for v in (a, a_up, a_far, a_down, b, b_up, b_far, b_down):
+        got += [v, send(v, 0, 1)]
+    return got
 
 
 def relay(own, other, near, far):
@@ -124,12 +124,12 @@
     out[...] = w[...].astype(F32).T.astype(BF)
 
 
-def place_kernel(recv, place, out):
+def place_kernel(recv, place, *outs):
     pick = pick_rows(place[...])
     got = recv[...].astype(F32).reshape(N_DP, 2, 8, D)
     for i in range(2):
         rows = dot(pick, got[:, i].reshape(R, D).astype(BF))
-        out[i * D : (i + 1) * D, :] = rows.T.astype(BF)
+        outs[i][...] = rows.T.astype(BF)
 
 
 def first_visible(lengths):
@@ -161,17 +161,13 @@
 
 
 def forward_kernel(lengths, ctx, wt, w_out, *refs):
-    shards = refs[:10]
-    xn, up, slopes, proj, att, gh, sums = refs[10:]
+    shards = refs[:16]
+    xn, up, slopes, proj, att, gh, sums = refs[16:]
     c = ctx[0]
-    for i, rel in zip((0, 1, 2, 3, 8, 9), REL[:4] + REL[6:]):
+    for i, rel in enumerate(REL):
         to = at(place_of(c, rel))
-        xn[:, to] = shards[i][:D, :]
-        up[:, to] = shards[i][D:, :]
-    for i, core in ((4, 0), (6, 1)):
-        to = at(place_of(c, (2, core)))
         xn[:, to] = shards[i][...]
-        up[:, to] = shards[i + 1][...]
+        up[:, to] = shards[8 + i][...]
     for n in range(GROUP // BLOCK):
         cols = slice(n * BLOCK, (n + 1) * BLOCK)
         p = dot(wt[...], xn[:, cols])
@@ -283,22 +279,33 @@
     weights[:, 64:, :] = jnp.concatenate(mix, axis=1).astype(BF)
 
 
-def sum_kernel(recv, project, mixing):
-    total = recv[0].astype(F32)
+def sum_kernel(ctx, recv, *refs):
+    own, other, chips, mixing, total = refs[0], refs[1], refs[2:5], refs[5], refs[6]
+    got = recv[0].astype(F32)
     for d in range(1, N_DP):
-        total = total + recv[d].astype(F32)
-    project[...] = total[:64]
-    mixing[:, :512] = total[64:72]
-    mixing[:, 512:] = total[72:]
-
-
-def join_kernel(ctx, parts, out):
-    own = pl.multiple_of(ctx[0] * 8, 8)
-    for c in range(N_CTX):
-        got = parts[c, pl.ds(own, 8), :]
+        got = got + recv[d].astype(F32)
+    total[...] = got[:64]
+    mixing[:, :512] = got[64:72]
+    mixing[:, 512:] = got[72:]
+
+    def rows(rel):
+        return total[pl.ds(pl.multiple_of(place_of(ctx[0], rel) * 8, 8), 8), :]
+
+    own[...] = rows((0, 0))
+    other[...] = rows((0, 1))
+    for step, part in zip((1, 2, 3), chips):
+        part[:8, :] = rows((step, 0))
+        part[8:, :] = rows((step, 1))
+
+
+def join_kernel(ctx, *refs):
+    parts, out = refs[:8], refs[8]
+    for i, part in enumerate(parts):
+        core = i % 2
+        src = place_of(ctx[0], ((4 - i // 2) % 4, core))
+        got = part[...] if i < 2 else part[core * 8 : core * 8 + 8, :]
         for kind in range(4):
-            start = kind * D + c * WIDE
-            out[:, start : start + WIDE] = got[:, kind * WIDE : (kind + 1) * WIDE]
+            out[:, at(kind * 8 + src)] = got[:, kind * WIDE : (kind + 1) * WIDE]
 
 
 def rows_kernel(ctx, place, w, w_out, *refs):
@@ -402,15 +409,14 @@
 
 def local(history, grad_output, lengths, send_order, place_order, w_project, w_out):
     ctx_s = lax.axis_index("ctx").astype(jnp.int32).reshape(1)
-    history, grad_output = hbm(history), hbm(grad_output)
     w_project, w_out = hbm(w_project), hbm(w_out)
     order = send_order.reshape(1, R)
     place = place_order.reshape(1, R)
 
-    (packed,) = call(pack_kernel, [((2 * R, D), BF)], history, grad_output, order)
+    (packed,) = call(pack_kernel, [((2 * R, D), BF)], hbm(history), hbm(grad_output), order)
     w_own, w_out_own = own_weights(ctx_s, w_project), own_rows(ctx_s, w_out)
     arrived = across(packed, "dp")
-    (shard,) = call(place_kernel, [((2 * D, R), BF)], arrived, place, late=(w_own, w_out_own))
+    shard = call(place_kernel, [((D, R), BF)] * 2, arrived, place, late=(w_own, w_out_own))
     xn, up, slopes, proj, att, gh, sums = call(
         forward_kernel,
         [
@@ -424,7 +430,9 @@
         ],
         lengths,
         ctx_s,
-        *[hbm(v) for v in (w_own, w_out_own, *ring_gather(shard))],
+        w_own,
+        w_out_own,
+        *[hbm(v) for v in ring_gather(*shard)],
         smem=2,
     )
     all_sums = [sums] + [send(sums, step, 0) for step in (2, 1, 3)]
@@ -459,21 +467,27 @@
         ],
     )
     parts = relay(own, other, (up_part, down_part), (far_up, far_down))
-    project, mixing = call(
+    own, other, *chips, mixing = call(
         sum_kernel,
-        [((64, 4 * WIDE), F32), ((8, D), F32)],
+        [((8, 4 * WIDE), F32)] * 2 + [((16, 4 * WIDE), F32)] * 3 + [((8, D), F32)],
+        ctx_s,
         across(weights, "dp"),
+        smem=1,
         late=parts[1:],
+        scratch=[pltpu.VMEM((64, 4 * WIDE), F32)],
     )
     owners = [(d * 8 + c, (2 * c + d // 8) * 8 + d % 8) for d in range(N_DP) for c in range(N_CTX)]
     mixing_grad = lax.ppermute(mixing, ("dp", "ctx"), owners)
-    project_all = lax.all_gather(project, "ctx")
-    rows = rows_back(ctx_s, place, w_project, w_out, parts, project)
+    project = [own, send(other, 0, 1)]
+    for step, part in zip((1, 2, 3), chips):
+        part = send(part, step, 0)
+        project += [part, send(part, 0, 1)]
+    rows = rows_back(ctx_s, place, w_project, w_out, parts, own)
     returned = across(rows, "dp")
     output, input_grad = call(
         unpack_kernel, [((R, D), BF), ((R, D), BF)], returned, history, grad_output, order
     )
-    (project_grad,) = call(join_kernel, [((8, 4 * D), F32)], ctx_s, project_all, smem=1)
+    (project_grad,) = call(join_kernel, [((8, 4 * D), F32)], ctx_s, *project, smem=1)
     return output, input_grad, project_grad, mixing_grad
 
 

time: 157 us -> 142 us (0.904)
  the two profiles are of different devices: /device:TPU:6 before, /device:TPU:98 now
where the time goes in v3:
time: 142 us
  starting transfers between devices  55.1 us (39%)
  waiting for transfers between devices  41.9 us (30%)
  Pallas kernels  38.8 us (27%)
  local copies, waits for them, and re-layouts  4.85 us (3%)
    ppermute x39, waiting for transfers between devices, send(): return lax.ppermute(x, 'ctx', pairs)  31.6 us
    ppermute x39, starting transfers between devices, send(): return lax.ppermute(x, 'ctx', pairs)  31.3 us
    pallas_call x7, Pallas kernels, call(): pl.pallas_call(skip(body, len(args), len(late)), out_shape=[pltpu.HBM(s,...  25.9 us
    all_to_all x3, starting transfers between devices, across(): return lax.all_to_all(x, axis, split_axis=0, concat_axis=0, tiled=True)  20.5 us
    pallas_call x1, Pallas kernels, rows_back(): pl.pallas_call(skip(rows_kernel, 14, 1), grid=(D // cols,), in_specs=[pl....  7.54 us
    ppermute x1, waiting for transfers between devices, local(): mixing_grad = lax.ppermute(mixing, ('dp', 'ctx'), owners)  6.45 us
    unnamed x71, local copies, waits for them, and re-layouts  4.85 us
    all_to_all x3, waiting for transfers between devices, across(): return lax.all_to_all(x, axis, split_axis=0, concat_axis=0, tiled=True)  3.92 us
  transfers between devices with their start and end apart: 43, of which 18 were waited for; matrix products, arithmetic and copies ran while one was open for 0% of the time, Pallas kernels for 4%

profile of v3, /device:TPU:98, one launch (start us, length us, event | category | flops | bytes accessed | tf_op | source)
XLA Modules:
  0.0 141.6 jit_solution(7313385570325443539)
XLA Ops:
  0.6 0.6 copy-done.9
  1.3 2.3 %shard_map.104 = bf16[256,1024]{1,0:T(8,128)(2,1)} custom-call(bf16[128,1024]{1,0:T(8,128)(2,1)} %hist.3, bf16[128,1024]{1,0:T(8,128)(2,1)} %gout.3, s32[1,128]{1,0:T(1,128)S(1)} %bitcast.9), custom_call_target="tpu_custom_call" | custom-call | tf_op jit(solution)/shard_map/pallas_call | solution.py:59
  3.6 7.2 %all-to-all-start = ((bf16[16,16,1024]{2,1,0:T(8,128)(2,1)}), bf16[16,16,1024]{2,1,0:T(8,128)(2,1)S(1)}, u32[]{:S(2)}, u32[]{:S(2)}) async-start(bf16[16,16,1024]{2,1,0:T(8,128)(2,1)} %bitcast.13), calls=%async_computation | async-start | bytes 1048576 | tf_op jit(solution)/shard_map/all_to_all | solution.py:407
  10.8 1.7 %shard_map.103.refs_3_.w_out = bf16[128,1024]{1,0:T(8,128)(2,1)} custom-call(s32[1]{0:T(128)} %bitcast.ctx.refs_0_, bf16[1024,1024]{1,0:T(8,128)(2,1)} %refs_3_.1), custom_call_target="tpu_custom_call" | custom-call | tf_op jit(solution)/shard_map/pallas_call | solution.py:372
  12.5 3.7 %shard_map.102.refs_2_.wt = bf16[512,1024]{1,0:T(8,128)(2,1)} custom-call(s32[1]{0:T(128)} %bitcast.ctx.refs_0_, bf16[1024,4096]{1,0:T(8,128)(2,1)} %refs_2_.1), custom_call_target="tpu_custom_call" | custom-call | tf_op jit(solution)/shard_map/pallas_call | solution.py:358
  16.1 3.9 %all-to-all-done = bf16[16,16,1024]{2,1,0:T(8,128)(2,1)S(1)} async-done(((bf16[16,16,1024]{2,1,0:T(8,128)(2,1)}), bf16[16,16,1024]{2,1,0:T(8,128)(2,1)S(1)}, u32[]{:S(2)}, u32[]{:S(2)}) %all-to-all-start) | async-done | bytes 524320 | tf_op jit(solution)/shard_map/all_to_all | solution.py:407
  20.0 1.2 copy-done
  21.3 1.1 shard_map.105
  22.4 1.5 %collective-permute-start.5 = (bf16[1024,128]{1,0:T(8,128)(2,1)}, bf16[1024,128]{1,0:T(8,128)(2,1)S(1)}, u32[]{:S(2)}, u32[]{:S(2)}) collective-permute-start(bf16[1024,128]{1,0:T(8,128)(2,1)} %get-tuple-element.28.refs_0_), channel_id=1, source_target_pairs={{0,2},{1,3},{2,4},{3,5},{4,6},{5,7},{6,0},{7,1},{8,10},{9,11},{10,... | collective-permute-start | bytes 786440 | tf_op jit(solution)/shard_map/ppermute | solution.py:79
  23.9 0.5 collective-permute-start.1
  24.4 1.5 %collective-permute-start.10 = (bf16[1024,128]{1,0:T(8,128)(2,1)}, bf16[1024,128]{1,0:T(8,128)(2,1)S(1)}, u32[]{:S(2)}, u32[]{:S(2)}) collective-permute-start(bf16[1024,128]{1,0:T(8,128)(2,1)} %get-tuple-element.29.refs_8_), channel_id=1, source_target_pairs={{0,2},{1,3},{2,4},{3,5},{4,6},{5,7},{6,0},{7,1},{8,10},{9,11},{10,... | collective-permute-start | bytes 786440 | tf_op jit(solution)/shard_map/ppermute | solution.py:79
  25.9 0.5 collective-permute-start.8
  26.5 4.8 %collective-permute-done.5.refs_6_ = bf16[1024,128]{1,0:T(8,128)(2,1)S(1)} collective-permute-done((bf16[1024,128]{1,0:T(8,128)(2,1)}, bf16[1024,128]{1,0:T(8,128)(2,1)S(1)}, u32[]{:S(2)}, u32[]{:S(2)}) %collective-permute-start.5) | collective-permute-done | bytes 262176 | tf_op jit(solution)/shard_map/ppermute | solution.py:79
  31.2 1.2 collective-permute-done.1.refs_2_
  32.5 0.6 collective-permute-start.3
  33.1 2.0 %collective-permute-done.10.refs_14_ = bf16[1024,128]{1,0:T(8,128)(2,1)S(1)} collective-permute-done((bf16[1024,128]{1,0:T(8,128)(2,1)}, bf16[1024,128]{1,0:T(8,128)(2,1)S(1)}, u32[]{:S(2)}, u32[]{:S(2)}) %collective-permute-start.10) | collective-permute-done | bytes 262176 | tf_op jit(solution)/shard_map/ppermute | solution.py:79
  35.1 1.5 %collective-permute-start.11 = (bf16[1024,128]{1,0:T(8,128)(2,1)S(1)}, bf16[1024,128]{1,0:T(8,128)(2,1)S(1)}, u32[]{:S(2)}, u32[]{:S(2)}) collective-permute-start(bf16[1024,128]{1,0:T(8,128)(2,1)S(1)} %collective-permute-done.10.refs_14_), channel_id=1, source_target_pairs={{0,2},{1,3},{2,4},{3,5},{4,6},{5,7},{6,0},{7,1},{8,10},{9,11},{10,... | collective-permute-start | bytes 786440 | tf_op jit(solution)/shard_map/ppermute | solution.py:79
  36.6 0.4 collective-permute-done.8.refs_10_
  37.1 0.5 collective-permute-start.13
  37.6 0.1 collective-permute-start.9
  37.7 4.3 %collective-permute-done.3.refs_4_ = bf16[1024,128]{1,0:T(8,128)(2,1)S(1)} collective-permute-done((bf16[1024,128]{1,0:T(8,128)(2,1)S(1)}, bf16[1024,128]{1,0:T(8,128)(2,1)S(1)}, u32[]{:S(2)}, u32[]{:S(2)}) %collective-permute-start.3) | collective-permute-done | bytes 262176 | tf_op jit(solution)/shard_map/ppermute | solution.py:79
  42.0 1.0 collective-permute-done.11.refs_12_
  43.0 0.5 collective-permute-done.4.refs_5_
  43.5 1.0 collective-permute-done.12.refs_13_
  44.6 0.7 copy-done.25
  45.3 8.8 %shard_map.106 = (bf16[1024,1024]{1,0:T(8,128)(2,1)}, bf16[1024,1024]{1,0:T(8,128)(2,1)}, bf16[512,1024]{1,0:T(8,128)(2,1)}, bf16[512,1024]{1,0:T(8,128)(2,1)}, ...) custom-call(s32[1,4]{1,0:T(1,128)S(1)} %copy-done.8, s32[1]{0:T(128)} %bitcast.ctx.refs_0_, ...), custom_call_target="tpu_custom_call" | custom-call | tf_op jit(solution)/shard_map/pallas_call | solution.py:59
  54.1 3.0 %collective-permute-start.16 = (f32[8,1024]{1,0:T(8,128)}, f32[8,1024]{1,0:T(8,128)S(1)}, u32[]{:S(2)}, u32[]{:S(2)}) collective-permute-start(f32[8,1024]{1,0:T(8,128)} %get-tuple-element.34.refs_0_), channel_id=1, source_target_pairs={{0,6},{1,7},{2,0},{3,1},{4,2},{5,3},{6,4},{7,5},{8,14},{9,15},{10,... | collective-permute-start | bytes 98312 | tf_op jit(solution)/shard_map/ppermute | solution.py:79
  57.1 2.2 %collective-permute-start.14 = (f32[8,1024]{1,0:T(8,128)}, f32[8,1024]{1,0:T(8,128)S(1)}, u32[]{:S(2)}, u32[]{:S(2)}) collective-permute-start(f32[8,1024]{1,0:T(8,128)} %get-tuple-element.34.refs_0_), channel_id=1, source_target_pairs={{0,4},{1,5},{2,6},{3,7},{4,0},{5,1},{6,2},{7,3},{8,12},{9,13},{10,... | collective-permute-start | bytes 98312 | tf_op jit(solution)/shard_map/ppermute | solution.py:79
  59.3 0.5 collective-permute-start.20
  59.8 1.4 collective-permute-done.15.refs_2_
  61.2 1.5 %collective-permute-done.14.refs_1_ = f32[8,1024]{1,0:T(8,128)S(1)} collective-permute-done((f32[8,1024]{1,0:T(8,128)}, f32[8,1024]{1,0:T(8,128)S(1)}, u32[]{:S(2)}, u32[]{:S(2)}) %collective-permute-start.14) | collective-permute-done | bytes 32800 | tf_op jit(solution)/shard_map/ppermute | solution.py:79
  62.7 1.2 collective-permute-done.18.refs_5_
  63.9 0.8 copy-done.7
  64.7 10.8 %shard_map.107 = (bf16[640,128]{1,0:T(8,128)(2,1)}, bf16[640,128]{1,0:T(8,128)(2,1)}, bf16[1280,128]{1,0:T(8,128)(2,1)}, bf16[1280,128]{1,0:T(8,128)(2,1)}, bf16...) custom-call(s32[1,4]{1,0:T(1,128)S(1)} %copy-done.8, s32[1]{0:T(128)} %bitcast.ctx.refs_0_, ...), custom_call_target="tpu_custom_call" | custom-call | tf_op jit(solution)/shard_map/pallas_call | solution.py:59
  75.6 6.1 %all-to-all-start.1 = ((bf16[16,80,512]{2,1,0:T(8,128)(2,1)}), bf16[16,80,512]{2,1,0:T(8,128)(2,1)S(1)}, u32[]{:S(2)}, u32[]{:S(2)}) async-start(bf16[16,80,512]{2,1,0:T(8,128)(2,1)} %get-tuple-element.43), calls=%async_computation.1 | async-start | bytes 2621440 | tf_op jit(solution)/shard_map/all_to_all | solution.py:407
  81.7 0.4 collective-permute-start.22
  82.1 1.8 %collective-permute-start.24 = (bf16[1280,128]{1,0:T(8,128)(2,1)S(1)}, bf16[1280,128]{1,0:T(8,128)(2,1)S(1)}, u32[]{:S(2)}, u32[]{:S(2)}) collective-permute-start(bf16[1280,128]{1,0:T(8,128)(2,1)S(1)} %copy-done.26), channel_id=1, source_target_pairs={{0,6},{1,7},{2,0},{3,1},{4,2},{5,3},{6,4},{7,5},{8,14},{9,15},{10,... | collective-permute-start | bytes 983048 | tf_op jit(solution)/shard_map/ppermute | solution.py:79
  83.9 0.7 collective-permute-start.26
  84.5 2.6 %collective-permute-start.29 = (bf16[640,128]{1,0:T(8,128)(2,1)S(1)}, bf16[640,128]{1,0:T(8,128)(2,1)S(1)}, u32[]{:S(2)}, u32[]{:S(2)}) collective-permute-start(bf16[640,128]{1,0:T(8,128)(2,1)S(1)} %copy-done.28), channel_id=1, source_target_pairs={{0,6},{1,7},{2,0},{3,1},{4,2},{5,3},{6,4},{7,5},{8,14},{9,15},{10,... | collective-permute-start | bytes 491528 | tf_op jit(solution)/shard_map/ppermute | solution.py:79
  87.1 7.9 %collective-permute-done.26 = bf16[640,128]{1,0:T(8,128)(2,1)S(1)} collective-permute-done((bf16[640,128]{1,0:T(8,128)(2,1)S(1)}, bf16[640,128]{1,0:T(8,128)(2,1)S(1)}, u32[]{:S(2)}, u32[]{:S(2)}) %collective-permute-start.26) | collective-permute-done | bytes 163872 | tf_op jit(solution)/shard_map/ppermute | solution.py:79
  95.1 0.4 collective-permute-done.29
  95.4 2.5 %collective-permute-start.30 = (bf16[640,128]{1,0:T(8,128)(2,1)S(1)}, bf16[640,128]{1,0:T(8,128)(2,1)S(1)}, u32[]{:S(2)}, u32[]{:S(2)}) collective-permute-start(bf16[640,128]{1,0:T(8,128)(2,1)S(1)} %collective-permute-done.29), channel_id=1, source_target_pairs={{0,6},{1,7},{2,0},{3,1},{4,2},{5,3},{6,4},{7,5},{8,14},{9,15},{10,... | collective-permute-start | bytes 491528 | tf_op jit(solution)/shard_map/ppermute | solution.py:79
  98.0 0.5 collective-permute-start.25
  98.5 0.1 collective-permute-start.21
  98.6 2.8 %collective-permute-done.27.refs_7_.refs_10_ = bf16[640,128]{1,0:T(8,128)(2,1)S(1)} collective-permute-done((bf16[640,128]{1,0:T(8,128)(2,1)S(1)}, bf16[640,128]{1,0:T(8,128)(2,1)S(1)}, u32[]{:S(2)}, u32[]{:S(2)}) %collective-permute-start.27) | collective-permute-done | bytes 163872 | tf_op jit(solution)/shard_map/ppermute | solution.py:79
  101.4 0.5 collective-permute-start.31
  101.9 0.9 collective-permute-done.28.refs_8_.refs_11_
  102.8 0.2 collective-permute-done.31.refs_10_.refs_13_
  103.0 0.8 shard_map.108
  103.9 0.7 copy-done.6
  104.7 7.5 %shard_map.109 = bf16[256,1024]{1,0:T(8,128)(2,1)} custom-call(s32[1]{0:T(128)} %bitcast.ctx.refs_0_, s32[1,128]{1,0:T(1,128)S(1)} %bitcast.12, bf16[1024,4096]{1,0:T(8,128)(2,1)} %refs_2_.1, bf16[1024,1024]{1,0:T(8,128)(2,1)} %refs_3_.1, bf16[640,128]{1,0:T(8,128)(2,1)S(1)} %copy-done.5, bf16[640,128]{1,0:T(8,128)(2,1)S(1)} %collective-permute-done.21.refs_2_.refs_5_, ...), custom_call_target="tpu_custom_call" | custom-call | tf_op jit(solution)/shard_map/pallas_call | solution.py:388
  112.2 7.2 %all-to-all-start.2 = ((bf16[16,16,1024]{2,1,0:T(8,128)(2,1)}), bf16[16,16,1024]{2,1,0:T(8,128)(2,1)S(1)}, u32[]{:S(2)}, u32[]{:S(2)}) async-start(bf16[16,16,1024]{2,1,0:T(8,128)(2,1)} %bitcast.14), calls=%async_computation.2 | async-start | bytes 1048576 | tf_op jit(solution)/shard_map/all_to_all | solution.py:407
  119.5 2.4 %collective-permute-start.33 = (f32[16,512]{1,0:T(8,128)S(1)}, f32[16,512]{1,0:T(8,128)S(1)}, u32[]{:S(2)}, u32[]{:S(2)}) collective-permute-start(f32[16,512]{1,0:T(8,128)S(1)} %copy-done.33), channel_id=1, source_target_pairs={{0,2},{1,3},{2,4},{3,5},{4,6},{5,7},{6,0},{7,1},{8,10},{9,11},{10,... | collective-permute-start | bytes 98312 | tf_op jit(solution)/shard_map/ppermute | solution.py:79
  121.9 2.9 %collective-permute-start.35 = (f32[16,512]{1,0:T(8,128)S(1)}, f32[16,512]{1,0:T(8,128)S(1)}, u32[]{:S(2)}, u32[]{:S(2)}) collective-permute-start(f32[16,512]{1,0:T(8,128)S(1)} %copy-done.32), channel_id=1, source_target_pairs={{0,4},{1,5},{2,6},{3,7},{4,0},{5,1},{6,2},{7,3},{8,12},{9,13},{10,... | collective-permute-start | bytes 98312 | tf_op jit(solution)/shard_map/ppermute | solution.py:79
  124.8 2.4 %collective-permute-start.37 = (f32[16,512]{1,0:T(8,128)S(1)}, f32[16,512]{1,0:T(8,128)S(1)}, u32[]{:S(2)}, u32[]{:S(2)}) collective-permute-start(f32[16,512]{1,0:T(8,128)S(1)} %copy-done.31), channel_id=1, source_target_pairs={{0,6},{1,7},{2,0},{3,1},{4,2},{5,3},{6,4},{7,5},{8,14},{9,15},{10,... | collective-permute-start | bytes 98312 | tf_op jit(solution)/shard_map/ppermute | solution.py:79
  127.2 3.3 %collective-permute-start.39 = (f32[8,1024]{1,0:T(8,128)S(1)}, f32[8,1024]{1,0:T(8,128)S(1)}, u32[]{:S(2)}, u32[]{:S(2)}) collective-permute-start(f32[8,1024]{1,0:T(8,128)S(1)} %copy-done.30), channel_id=1, source_target_pairs={{0,0},{1,16},{2,32},{3,48},{4,64},{5,80},{6,96},{7,112},{8,1},{9,1... | collective-permute-start | bytes 98312 | tf_op jit(solution)/shard_map/ppermute | solution.py:480
  130.5 1.4 collective-permute-start.34
  131.9 0.1 collective-permute-start.36
  132.0 0.4 collective-permute-start.38
  132.4 0.1 collective-permute-start.32
  132.5 6.5 %collective-permute-done.39 = f32[8,1024]{1,0:T(8,128)S(1)} collective-permute-done((f32[8,1024]{1,0:T(8,128)S(1)}, f32[8,1024]{1,0:T(8,128)S(1)}, u32[]{:S(2)}, u32[]{:S(2)}) %collective-permute-start.39) | collective-permute-done | bytes 32800 | tf_op jit(solution)/shard_map/ppermute | solution.py:480
  139.0 0.7 shard_map.111
  139.7 1.3 shard_map.110
  141.0 0.6 copy.12
  (103 shorter events, 0.3 us)
Async XLA Ops:
  3.6 16.4 %all-to-all-start = ((bf16[16,16,1024]{2,1,0:T(8,128)(2,1)}), bf16[16,16,1024]{2,1,0:T(8,128)(2,1)S(1)}, u32[]{:S(2)}, u32[]{:S(2)}) async-start(bf16[16,16,1024]{2,1,0:T(8,128)(2,1)} %bitcast.13), calls=%async_computation | async-start | bytes 1048576 | tf_op jit(solution)/shard_map/all_to_all | solution.py:407
  12.5 7.6 %copy-start.2 = (bf16[128,1024]{1,0:T(8,128)(2,1)S(1)}, bf16[128,1024]{1,0:T(8,128)(2,1)}, u32[]{:S(2)}) copy-start(bf16[128,1024]{1,0:T(8,128)(2,1)} %shard_map.103.refs_3_.w_out) | copy-start | bytes 786436
  12.5 7.6 %copy-start.11 = (s32[128]{0:T(128)S(1)}, s32[128]{0:T(128)}, u32[]{:S(2)}) copy-start(s32[128]{0:T(128)} %param.11) | copy-start | bytes 1540
  12.5 32.9 %copy-start.8 = (s32[1,4]{1,0:T(1,128)S(1)}, s32[1,4]{1,0:T(1,128)}, u32[]{:S(2)}) copy-start(s32[1,4]{1,0:T(1,128)} %lengths.3) | copy-start | bytes 52
  21.3 24.0 %copy-start.1 = (bf16[512,1024]{1,0:T(8,128)(2,1)S(1)}, bf16[512,1024]{1,0:T(8,128)(2,1)}, u32[]{:S(2)}) copy-start(bf16[512,1024]{1,0:T(8,128)(2,1)} %shard_map.102.refs_2_.wt) | copy-start | bytes 3145732
  22.4 8.8 %collective-permute-start.5 = (bf16[1024,128]{1,0:T(8,128)(2,1)}, bf16[1024,128]{1,0:T(8,128)(2,1)S(1)}, u32[]{:S(2)}, u32[]{:S(2)}) collective-permute-start(bf16[1024,128]{1,0:T(8,128)(2,1)} %get-tuple-element.28.refs_0_), channel_id=1, source_target_pairs={{0,2},{1,3},{2,4},{3,5},{4,6},{5,7},{6,0},{7,1},{8,10},{9,11},{10,... | collective-permute-start | bytes 786440 | tf_op jit(solution)/shard_map/ppermute | solution.py:79
  23.9 8.6 %collective-permute-start.1 = (bf16[1024,128]{1,0:T(8,128)(2,1)}, bf16[1024,128]{1,0:T(8,128)(2,1)S(1)}, u32[]{:S(2)}, u32[]{:S(2)}) collective-permute-start(bf16[1024,128]{1,0:T(8,128)(2,1)} %get-tuple-element.28.refs_0_), channel_id=1, source_target_pairs={{0,6},{1,7},{2,0},{3,1},{4,2},{5,3},{6,4},{7,5},{8,14},{9,15},{10,... | collective-permute-start | bytes 786440 | tf_op jit(solution)/shard_map/ppermute | solution.py:79
  24.4 8.0 %collective-permute-start = (bf16[1024,128]{1,0:T(8,128)(2,1)}, bf16[1024,128]{1,0:T(8,128)(2,1)S(1)}, u32[]{:S(2)}, u32[]{:S(2)}) collective-permute-start(bf16[1024,128]{1,0:T(8,128)(2,1)} %get-tuple-element.28.refs_0_), channel_id=1, source_target_pairs={{0,1},{1,0},{2,3},{3,2},{4,5},{5,4},{6,7},{7,6},{8,9},{9,8},{10,11... | collective-permute-start | bytes 786440 | tf_op jit(solution)/shard_map/ppermute | solution.py:79
  24.4 10.7 %collective-permute-start.10 = (bf16[1024,128]{1,0:T(8,128)(2,1)}, bf16[1024,128]{1,0:T(8,128)(2,1)S(1)}, u32[]{:S(2)}, u32[]{:S(2)}) collective-permute-start(bf16[1024,128]{1,0:T(8,128)(2,1)} %get-tuple-element.29.refs_8_), channel_id=1, source_target_pairs={{0,2},{1,3},{2,4},{3,5},{4,6},{5,7},{6,0},{7,1},{8,10},{9,11},{10,... | collective-permute-start | bytes 786440 | tf_op jit(solution)/shard_map/ppermute | solution.py:79
  25.9 11.1 %collective-permute-start.8 = (bf16[1024,128]{1,0:T(8,128)(2,1)}, bf16[1024,128]{1,0:T(8,128)(2,1)S(1)}, u32[]{:S(2)}, u32[]{:S(2)}) collective-permute-start(bf16[1024,128]{1,0:T(8,128)(2,1)} %get-tuple-element.29.refs_8_), channel_id=1, source_target_pairs={{0,6},{1,7},{2,0},{3,1},{4,2},{5,3},{6,4},{7,5},{8,14},{9,15},{10,... | collective-permute-start | bytes 786440 | tf_op jit(solution)/shard_map/ppermute | solution.py:79
  31.2 13.3 %copy-start.12 = (bf16[1024,128]{1,0:T(8,128)(2,1)}, bf16[1024,128]{1,0:T(8,128)(2,1)S(1)}, u32[]{:S(2)}) copy-start(bf16[1024,128]{1,0:T(8,128)(2,1)S(1)} %collective-permute-done.5.refs_6_) | copy-start | bytes 786436
  31.2 5.8 %collective-permute-start.7 = (bf16[1024,128]{1,0:T(8,128)(2,1)}, bf16[1024,128]{1,0:T(8,128)(2,1)S(1)}, u32[]{:S(2)}, u32[]{:S(2)}) collective-permute-start(bf16[1024,128]{1,0:T(8,128)(2,1)} %get-tuple-element.29.refs_8_), channel_id=1, source_target_pairs={{0,1},{1,0},{2,3},{3,2},{4,5},{5,4},{6,7},{7,6},{8,9},{9,8},{10,11... | collective-permute-start | bytes 786440 | tf_op jit(solution)/shard_map/ppermute | solution.py:79
  32.5 12.0 %copy-start.13 = (bf16[1024,128]{1,0:T(8,128)(2,1)}, bf16[1024,128]{1,0:T(8,128)(2,1)S(1)}, u32[]{:S(2)}) copy-start(bf16[1024,128]{1,0:T(8,128)(2,1)S(1)} %collective-permute-done.1.refs_2_) | copy-start | bytes 786436
  32.5 5.1 %collective-permute-start.6 = (bf16[1024,128]{1,0:T(8,128)(2,1)S(1)}, bf16[1024,128]{1,0:T(8,128)(2,1)S(1)}, u32[]{:S(2)}, u32[]{:S(2)}) collective-permute-start(bf16[1024,128]{1,0:T(8,128)(2,1)S(1)} %collective-permute-done.5.refs_6_), channel_id=1, source_target_pairs={{0,1},{1,0},{2,3},{3,2},{4,5},{5,4},{6,7},{7,6},{8,9},{9,8},{10,11... | collective-permute-start | bytes 786440 | tf_op jit(solution)/shard_map/ppermute | solution.py:79
  32.5 12.0 %copy-start.14 = (bf16[1024,128]{1,0:T(8,128)(2,1)}, bf16[1024,128]{1,0:T(8,128)(2,1)S(1)}, u32[]{:S(2)}) copy-start(bf16[1024,128]{1,0:T(8,128)(2,1)S(1)} %collective-permute-done.refs_1_) | copy-start | bytes 786436
  32.5 9.5 %collective-permute-start.3 = (bf16[1024,128]{1,0:T(8,128)(2,1)S(1)}, bf16[1024,128]{1,0:T(8,128)(2,1)S(1)}, u32[]{:S(2)}, u32[]{:S(2)}) collective-permute-start(bf16[1024,128]{1,0:T(8,128)(2,1)S(1)} %collective-permute-done.1.refs_2_), channel_id=1, source_target_pairs={{0,6},{1,7},{2,0},{3,1},{4,2},{5,3},{6,4},{7,5},{8,14},{9,15},{10,... | collective-permute-start | bytes 786440 | tf_op jit(solution)/shard_map/ppermute | solution.py:79
  35.1 9.4 %copy-start.15 = (bf16[1024,128]{1,0:T(8,128)(2,1)}, bf16[1024,128]{1,0:T(8,128)(2,1)S(1)}, u32[]{:S(2)}) copy-start(bf16[1024,128]{1,0:T(8,128)(2,1)S(1)} %collective-permute-done.10.refs_14_) | copy-start | bytes 786436
  35.1 7.8 %collective-permute-start.11 = (bf16[1024,128]{1,0:T(8,128)(2,1)S(1)}, bf16[1024,128]{1,0:T(8,128)(2,1)S(1)}, u32[]{:S(2)}, u32[]{:S(2)}) collective-permute-start(bf16[1024,128]{1,0:T(8,128)(2,1)S(1)} %collective-permute-done.10.refs_14_), channel_id=1, source_target_pairs={{0,2},{1,3},{2,4},{3,5},{4,6},{5,7},{6,0},{7,1},{8,10},{9,11},{10,... | collective-permute-start | bytes 786440 | tf_op jit(solution)/shard_map/ppermute | solution.py:79
  37.0 7.5 %copy-start.16 = (bf16[1024,128]{1,0:T(8,128)(2,1)}, bf16[1024,128]{1,0:T(8,128)(2,1)S(1)}, u32[]{:S(2)}) copy-start(bf16[1024,128]{1,0:T(8,128)(2,1)S(1)} %collective-permute-done.8.refs_10_) | copy-start | bytes 786436
  37.1 5.9 %collective-permute-start.2 = (bf16[1024,128]{1,0:T(8,128)(2,1)S(1)}, bf16[1024,128]{1,0:T(8,128)(2,1)S(1)}, u32[]{:S(2)}, u32[]{:S(2)}) collective-permute-start(bf16[1024,128]{1,0:T(8,128)(2,1)S(1)} %collective-permute-done.1.refs_2_), channel_id=1, source_target_pairs={{0,1},{1,0},{2,3},{3,2},{4,5},{5,4},{6,7},{7,6},{8,9},{9,8},{10,11... | collective-permute-start | bytes 786440 | tf_op jit(solution)/shard_map/ppermute | solution.py:79
  37.1 7.5 %copy-start.17 = (bf16[1024,128]{1,0:T(8,128)(2,1)}, bf16[1024,128]{1,0:T(8,128)(2,1)S(1)}, u32[]{:S(2)}) copy-start(bf16[1024,128]{1,0:T(8,128)(2,1)S(1)} %collective-permute-done.7.refs_9_) | copy-start | bytes 786436
  37.1 5.9 %collective-permute-start.13 = (bf16[1024,128]{1,0:T(8,128)(2,1)S(1)}, bf16[1024,128]{1,0:T(8,128)(2,1)S(1)}, u32[]{:S(2)}, u32[]{:S(2)}) collective-permute-start(bf16[1024,128]{1,0:T(8,128)(2,1)S(1)} %collective-permute-done.10.refs_14_), channel_id=1, source_target_pairs={{0,1},{1,0},{2,3},{3,2},{4,5},{5,4},{6,7},{7,6},{8,9},{9,8},{10,11... | collective-permute-start | bytes 786440 | tf_op jit(solution)/shard_map/ppermute | solution.py:79
  37.6 7.0 %copy-start.18 = (bf16[1024,128]{1,0:T(8,128)(2,1)}, bf16[1024,128]{1,0:T(8,128)(2,1)S(1)}, u32[]{:S(2)}) copy-start(bf16[1024,128]{1,0:T(8,128)(2,1)S(1)} %collective-permute-done.6.refs_7_) | copy-start | bytes 786436
  37.6 5.4 %collective-permute-start.9 = (bf16[1024,128]{1,0:T(8,128)(2,1)S(1)}, bf16[1024,128]{1,0:T(8,128)(2,1)S(1)}, u32[]{:S(2)}, u32[]{:S(2)}) collective-permute-start(bf16[1024,128]{1,0:T(8,128)(2,1)S(1)} %collective-permute-done.8.refs_10_), channel_id=1, source_target_pairs={{0,1},{1,0},{2,3},{3,2},{4,5},{5,4},{6,7},{7,6},{8,9},{9,8},{10,11... | collective-permute-start | bytes 786440 | tf_op jit(solution)/shard_map/ppermute | solution.py:79
  42.0 1.5 %collective-permute-start.4 = (bf16[1024,128]{1,0:T(8,128)(2,1)S(1)}, bf16[1024,128]{1,0:T(8,128)(2,1)S(1)}, u32[]{:S(2)}, u32[]{:S(2)}) collective-permute-start(bf16[1024,128]{1,0:T(8,128)(2,1)S(1)} %collective-permute-done.3.refs_4_), channel_id=1, source_target_pairs={{0,1},{1,0},{2,3},{3,2},{4,5},{5,4},{6,7},{7,6},{8,9},{9,8},{10,11... | collective-permute-start | bytes 786440 | tf_op jit(solution)/shard_map/ppermute | solution.py:79
  43.0 1.5 %collective-permute-start.12 = (bf16[1024,128]{1,0:T(8,128)(2,1)S(1)}, bf16[1024,128]{1,0:T(8,128)(2,1)S(1)}, u32[]{:S(2)}, u32[]{:S(2)}) collective-permute-start(bf16[1024,128]{1,0:T(8,128)(2,1)S(1)} %collective-permute-done.11.refs_12_), channel_id=1, source_target_pairs={{0,1},{1,0},{2,3},{3,2},{4,5},{5,4},{6,7},{7,6},{8,9},{9,8},{10,11... | collective-permute-start | bytes 786440 | tf_op jit(solution)/shard_map/ppermute | solution.py:79
  54.1 5.2 %collective-permute-start.16 = (f32[8,1024]{1,0:T(8,128)}, f32[8,1024]{1,0:T(8,128)S(1)}, u32[]{:S(2)}, u32[]{:S(2)}) collective-permute-start(f32[8,1024]{1,0:T(8,128)} %get-tuple-element.34.refs_0_), channel_id=1, source_target_pairs={{0,6},{1,7},{2,0},{3,1},{4,2},{5,3},{6,4},{7,5},{8,14},{9,15},{10,... | collective-permute-start | bytes 98312 | tf_op jit(solution)/shard_map/ppermute | solution.py:79
  57.1 4.1 %collective-permute-start.15 = (f32[8,1024]{1,0:T(8,128)}, f32[8,1024]{1,0:T(8,128)S(1)}, u32[]{:S(2)}, u32[]{:S(2)}) collective-permute-start(f32[8,1024]{1,0:T(8,128)} %get-tuple-element.34.refs_0_), channel_id=1, source_target_pairs={{0,2},{1,3},{2,4},{3,5},{4,6},{5,7},{6,0},{7,1},{8,10},{9,11},{10,... | collective-permute-start | bytes 98312 | tf_op jit(solution)/shard_map/ppermute | solution.py:79
  57.1 5.6 %collective-permute-start.14 = (f32[8,1024]{1,0:T(8,128)}, f32[8,1024]{1,0:T(8,128)S(1)}, u32[]{:S(2)}, u32[]{:S(2)}) collective-permute-start(f32[8,1024]{1,0:T(8,128)} %get-tuple-element.34.refs_0_), channel_id=1, source_target_pairs={{0,4},{1,5},{2,6},{3,7},{4,0},{5,1},{6,2},{7,3},{8,12},{9,13},{10,... | collective-permute-start | bytes 98312 | tf_op jit(solution)/shard_map/ppermute | solution.py:79
  59.3 3.4 %collective-permute-start.17 = (f32[8,1024]{1,0:T(8,128)}, f32[8,1024]{1,0:T(8,128)S(1)}, u32[]{:S(2)}, u32[]{:S(2)}) collective-permute-start(f32[8,1024]{1,0:T(8,128)} %get-tuple-element.34.refs_0_), channel_id=1, source_target_pairs={{0,1},{1,0},{2,3},{3,2},{4,5},{5,4},{6,7},{7,6},{8,9},{9,8},{10,11... | collective-permute-start | bytes 98312 | tf_op jit(solution)/shard_map/ppermute | solution.py:79
  59.3 3.4 %collective-permute-start.20 = (f32[8,1024]{1,0:T(8,128)S(1)}, f32[8,1024]{1,0:T(8,128)S(1)}, u32[]{:S(2)}, u32[]{:S(2)}) collective-permute-start(f32[8,1024]{1,0:T(8,128)S(1)} %collective-permute-done.16.refs_3_), channel_id=1, source_target_pairs={{0,1},{1,0},{2,3},{3,2},{4,5},{5,4},{6,7},{7,6},{8,9},{9,8},{10,11... | collective-permute-start | bytes 98312 | tf_op jit(solution)/shard_map/ppermute | solution.py:79
  61.2 1.5 %collective-permute-start.19 = (f32[8,1024]{1,0:T(8,128)S(1)}, f32[8,1024]{1,0:T(8,128)S(1)}, u32[]{:S(2)}, u32[]{:S(2)}) collective-permute-start(f32[8,1024]{1,0:T(8,128)S(1)} %collective-permute-done.15.refs_2_), channel_id=1, source_target_pairs={{0,1},{1,0},{2,3},{3,2},{4,5},{5,4},{6,7},{7,6},{8,9},{9,8},{10,11... | collective-permute-start | bytes 98312 | tf_op jit(solution)/shard_map/ppermute | solution.py:79
  62.7 1.2 collective-permute-start.18
  75.6 8.3 %copy-start.29 = (bf16[640,128]{1,0:T(8,128)(2,1)S(1)}, bf16[640,128]{1,0:T(8,128)(2,1)}, u32[]{:S(2)}) copy-start(bf16[640,128]{1,0:T(8,128)(2,1)} %get-tuple-element.41) | copy-start | bytes 491524
  75.6 9.0 %copy-start.28 = (bf16[640,128]{1,0:T(8,128)(2,1)S(1)}, bf16[640,128]{1,0:T(8,128)(2,1)}, u32[]{:S(2)}) copy-start(bf16[640,128]{1,0:T(8,128)(2,1)} %get-tuple-element.42) | copy-start | bytes 491524
  75.6 27.4 %all-to-all-start.1 = ((bf16[16,80,512]{2,1,0:T(8,128)(2,1)}), bf16[16,80,512]{2,1,0:T(8,128)(2,1)S(1)}, u32[]{:S(2)}, u32[]{:S(2)}) async-start(bf16[16,80,512]{2,1,0:T(8,128)(2,1)} %get-tuple-element.43), calls=%async_computation.1 | async-start | bytes 2621440 | tf_op jit(solution)/shard_map/all_to_all | solution.py:407
  81.7 16.3 %collective-permute-start.22 = (bf16[1280,128]{1,0:T(8,128)(2,1)S(1)}, bf16[1280,128]{1,0:T(8,128)(2,1)S(1)}, u32[]{:S(2)}, u32[]{:S(2)}) collective-permute-start(bf16[1280,128]{1,0:T(8,128)(2,1)S(1)} %copy-done.27), channel_id=1, source_target_pairs={{0,2},{1,3},{2,4},{3,5},{4,6},{5,7},{6,0},{7,1},{8,10},{9,11},{10,... | collective-permute-start | bytes 983048 | tf_op jit(solution)/shard_map/ppermute | solution.py:79
  82.1 15.9 %collective-permute-start.24 = (bf16[1280,128]{1,0:T(8,128)(2,1)S(1)}, bf16[1280,128]{1,0:T(8,128)(2,1)S(1)}, u32[]{:S(2)}, u32[]{:S(2)}) collective-permute-start(bf16[1280,128]{1,0:T(8,128)(2,1)S(1)} %copy-done.26), channel_id=1, source_target_pairs={{0,6},{1,7},{2,0},{3,1},{4,2},{5,3},{6,4},{7,5},{8,14},{9,15},{10,... | collective-permute-start | bytes 983048 | tf_op jit(solution)/shard_map/ppermute | solution.py:79
  83.9 11.2 %collective-permute-start.26 = (bf16[640,128]{1,0:T(8,128)(2,1)S(1)}, bf16[640,128]{1,0:T(8,128)(2,1)S(1)}, u32[]{:S(2)}, u32[]{:S(2)}) collective-permute-start(bf16[640,128]{1,0:T(8,128)(2,1)S(1)} %copy-done.29), channel_id=1, source_target_pairs={{0,2},{1,3},{2,4},{3,5},{4,6},{5,7},{6,0},{7,1},{8,10},{9,11},{10,... | collective-permute-start | bytes 491528 | tf_op jit(solution)/shard_map/ppermute | solution.py:79
  84.5 10.9 %collective-permute-start.29 = (bf16[640,128]{1,0:T(8,128)(2,1)S(1)}, bf16[640,128]{1,0:T(8,128)(2,1)S(1)}, u32[]{:S(2)}, u32[]{:S(2)}) collective-permute-start(bf16[640,128]{1,0:T(8,128)(2,1)S(1)} %copy-done.28), channel_id=1, source_target_pairs={{0,6},{1,7},{2,0},{3,1},{4,2},{5,3},{6,4},{7,5},{8,14},{9,15},{10,... | collective-permute-start | bytes 491528 | tf_op jit(solution)/shard_map/ppermute | solution.py:79
  95.0 6.3 %collective-permute-start.27 = (bf16[640,128]{1,0:T(8,128)(2,1)S(1)}, bf16[640,128]{1,0:T(8,128)(2,1)S(1)}, u32[]{:S(2)}, u32[]{:S(2)}) collective-permute-start(bf16[640,128]{1,0:T(8,128)(2,1)S(1)} %collective-permute-done.26), channel_id=1, source_target_pairs={{0,2},{1,3},{2,4},{3,5},{4,6},{5,7},{6,0},{7,1},{8,10},{9,11},{10,... | collective-permute-start | bytes 491528 | tf_op jit(solution)/shard_map/ppermute | solution.py:79
  95.4 5.9 %collective-permute-start.30 = (bf16[640,128]{1,0:T(8,128)(2,1)S(1)}, bf16[640,128]{1,0:T(8,128)(2,1)S(1)}, u32[]{:S(2)}, u32[]{:S(2)}) collective-permute-start(bf16[640,128]{1,0:T(8,128)(2,1)S(1)} %collective-permute-done.29), channel_id=1, source_target_pairs={{0,6},{1,7},{2,0},{3,1},{4,2},{5,3},{6,4},{7,5},{8,14},{9,15},{10,... | collective-permute-start | bytes 491528 | tf_op jit(solution)/shard_map/ppermute | solution.py:79
  98.0 5.0 %collective-permute-start.23 = (bf16[1280,128]{1,0:T(8,128)(2,1)S(1)}, bf16[1280,128]{1,0:T(8,128)(2,1)S(1)}, u32[]{:S(2)}, u32[]{:S(2)}) collective-permute-start(bf16[1280,128]{1,0:T(8,128)(2,1)S(1)} %collective-permute-done.22.refs_3_.refs_6_), channel_id=1, source_target_pairs={{0,1},{1,0},{2,3},{3,2},{4,5},{5,4},{6,7},{7,6},{8,9},{9,8},{10,11... | collective-permute-start | bytes 983048 | tf_op jit(solution)/shard_map/ppermute | solution.py:79
  98.0 5.0 %collective-permute-start.25 = (bf16[1280,128]{1,0:T(8,128)(2,1)S(1)}, bf16[1280,128]{1,0:T(8,128)(2,1)S(1)}, u32[]{:S(2)}, u32[]{:S(2)}) collective-permute-start(bf16[1280,128]{1,0:T(8,128)(2,1)S(1)} %collective-permute-done.24.refs_5_.refs_8_), channel_id=1, source_target_pairs={{0,1},{1,0},{2,3},{3,2},{4,5},{5,4},{6,7},{7,6},{8,9},{9,8},{10,11... | collective-permute-start | bytes 983048 | tf_op jit(solution)/shard_map/ppermute | solution.py:79
  98.5 3.4 %collective-permute-start.21 = (bf16[640,128]{1,0:T(8,128)(2,1)}, bf16[640,128]{1,0:T(8,128)(2,1)S(1)}, u32[]{:S(2)}, u32[]{:S(2)}) collective-permute-start(bf16[640,128]{1,0:T(8,128)(2,1)} %get-tuple-element.38), channel_id=1, source_target_pairs={{0,1},{1,0},{2,3},{3,2},{4,5},{5,4},{6,7},{7,6},{8,9},{9,8},{10,11... | collective-permute-start | bytes 491528 | tf_op jit(solution)/shard_map/ppermute | solution.py:79
  101.4 1.4 collective-permute-start.28
  101.4 1.6 %collective-permute-start.31 = (bf16[640,128]{1,0:T(8,128)(2,1)S(1)}, bf16[640,128]{1,0:T(8,128)(2,1)S(1)}, u32[]{:S(2)}, u32[]{:S(2)}) collective-permute-start(bf16[640,128]{1,0:T(8,128)(2,1)S(1)} %collective-permute-done.30.refs_9_.refs_12_), channel_id=1, source_target_pairs={{0,1},{1,0},{2,3},{3,2},{4,5},{5,4},{6,7},{7,6},{8,9},{9,8},{10,11... | collective-permute-start | bytes 491528 | tf_op jit(solution)/shard_map/ppermute | solution.py:79
  104.6 14.8 %copy-start.33 = (f32[16,512]{1,0:T(8,128)S(1)}, f32[16,512]{1,0:T(8,128)}, u32[]{:S(2)}) copy-start(f32[16,512]{1,0:T(8,128)} %get-tuple-element.48) | copy-start | bytes 98308
  104.6 17.2 %copy-start.32 = (f32[16,512]{1,0:T(8,128)S(1)}, f32[16,512]{1,0:T(8,128)}, u32[]{:S(2)}) copy-start(f32[16,512]{1,0:T(8,128)} %get-tuple-element.49) | copy-start | bytes 98308
  104.6 20.1 %copy-start.31 = (f32[16,512]{1,0:T(8,128)S(1)}, f32[16,512]{1,0:T(8,128)}, u32[]{:S(2)}) copy-start(f32[16,512]{1,0:T(8,128)} %get-tuple-element.50) | copy-start | bytes 98308
  104.6 22.5 %copy-start.30 = (f32[8,1024]{1,0:T(8,128)S(1)}, f32[8,1024]{1,0:T(8,128)}, u32[]{:S(2)}) copy-start(f32[8,1024]{1,0:T(8,128)} %get-tuple-element.51) | copy-start | bytes 98308
  104.6 27.8 %copy-start.34 = (f32[8,512]{1,0:T(8,128)S(1)}, f32[8,512]{1,0:T(8,128)}, u32[]{:S(2)}) copy-start(f32[8,512]{1,0:T(8,128)} %get-tuple-element.47) | copy-start | bytes 49156
  104.7 35.1 %copy-start.3 = (bf16[128,1024]{1,0:T(8,128)(2,1)S(1)}, bf16[128,1024]{1,0:T(8,128)(2,1)}, u32[]{:S(2)}) copy-start(bf16[128,1024]{1,0:T(8,128)(2,1)} %hist.3) | copy-start | bytes 786436
  104.7 35.1 %copy-start.4 = (bf16[128,1024]{1,0:T(8,128)(2,1)S(1)}, bf16[128,1024]{1,0:T(8,128)(2,1)}, u32[]{:S(2)}) copy-start(bf16[128,1024]{1,0:T(8,128)(2,1)} %gout.3) | copy-start | bytes 786436
  104.7 35.0 %copy-start.10 = (s32[128]{0:T(128)S(1)}, s32[128]{0:T(128)}, u32[]{:S(2)}) copy-start(s32[128]{0:T(128)} %param.10) | copy-start | bytes 1540
  112.2 27.5 %all-to-all-start.2 = ((bf16[16,16,1024]{2,1,0:T(8,128)(2,1)}), bf16[16,16,1024]{2,1,0:T(8,128)(2,1)S(1)}, u32[]{:S(2)}, u32[]{:S(2)}) async-start(bf16[16,16,1024]{2,1,0:T(8,128)(2,1)} %bitcast.14), calls=%async_computation.2 | async-start | bytes 1048576 | tf_op jit(solution)/shard_map/all_to_all | solution.py:407
  119.5 11.0 %collective-permute-start.33 = (f32[16,512]{1,0:T(8,128)S(1)}, f32[16,512]{1,0:T(8,128)S(1)}, u32[]{:S(2)}, u32[]{:S(2)}) collective-permute-start(f32[16,512]{1,0:T(8,128)S(1)} %copy-done.33), channel_id=1, source_target_pairs={{0,2},{1,3},{2,4},{3,5},{4,6},{5,7},{6,0},{7,1},{8,10},{9,11},{10,... | collective-permute-start | bytes 98312 | tf_op jit(solution)/shard_map/ppermute | solution.py:79
  121.9 10.0 %collective-permute-start.35 = (f32[16,512]{1,0:T(8,128)S(1)}, f32[16,512]{1,0:T(8,128)S(1)}, u32[]{:S(2)}, u32[]{:S(2)}) collective-permute-start(f32[16,512]{1,0:T(8,128)S(1)} %copy-done.32), channel_id=1, source_target_pairs={{0,4},{1,5},{2,6},{3,7},{4,0},{5,1},{6,2},{7,3},{8,12},{9,13},{10,... | collective-permute-start | bytes 98312 | tf_op jit(solution)/shard_map/ppermute | solution.py:79
  124.8 7.3 %collective-permute-start.37 = (f32[16,512]{1,0:T(8,128)S(1)}, f32[16,512]{1,0:T(8,128)S(1)}, u32[]{:S(2)}, u32[]{:S(2)}) collective-permute-start(f32[16,512]{1,0:T(8,128)S(1)} %copy-done.31), channel_id=1, source_target_pairs={{0,6},{1,7},{2,0},{3,1},{4,2},{5,3},{6,4},{7,5},{8,14},{9,15},{10,... | collective-permute-start | bytes 98312 | tf_op jit(solution)/shard_map/ppermute | solution.py:79
  127.2 11.8 %collective-permute-start.39 = (f32[8,1024]{1,0:T(8,128)S(1)}, f32[8,1024]{1,0:T(8,128)S(1)}, u32[]{:S(2)}, u32[]{:S(2)}) collective-permute-start(f32[8,1024]{1,0:T(8,128)S(1)} %copy-done.30), channel_id=1, source_target_pairs={{0,0},{1,16},{2,32},{3,48},{4,64},{5,80},{6,96},{7,112},{8,1},{9,1... | collective-permute-start | bytes 98312 | tf_op jit(solution)/shard_map/ppermute | solution.py:480
  130.5 8.5 %collective-permute-start.34 = (f32[16,512]{1,0:T(8,128)S(1)}, f32[16,512]{1,0:T(8,128)S(1)}, u32[]{:S(2)}, u32[]{:S(2)}) collective-permute-start(f32[16,512]{1,0:T(8,128)S(1)} %collective-permute-done.33.refs_2_), channel_id=1, source_target_pairs={{0,1},{1,0},{2,3},{3,2},{4,5},{5,4},{6,7},{7,6},{8,9},{9,8},{10,11... | collective-permute-start | bytes 98312 | tf_op jit(solution)/shard_map/ppermute | solution.py:79
  131.9 7.1 %collective-permute-start.36 = (f32[16,512]{1,0:T(8,128)S(1)}, f32[16,512]{1,0:T(8,128)S(1)}, u32[]{:S(2)}, u32[]{:S(2)}) collective-permute-start(f32[16,512]{1,0:T(8,128)S(1)} %collective-permute-done.35.refs_4_), channel_id=1, source_target_pairs={{0,1},{1,0},{2,3},{3,2},{4,5},{5,4},{6,7},{7,6},{8,9},{9,8},{10,11... | collective-permute-start | bytes 98312 | tf_op jit(solution)/shard_map/ppermute | solution.py:79
  132.0 7.0 %collective-permute-start.38 = (f32[16,512]{1,0:T(8,128)S(1)}, f32[16,512]{1,0:T(8,128)S(1)}, u32[]{:S(2)}, u32[]{:S(2)}) collective-permute-start(f32[16,512]{1,0:T(8,128)S(1)} %collective-permute-done.37.refs_6_), channel_id=1, source_target_pairs={{0,1},{1,0},{2,3},{3,2},{4,5},{5,4},{6,7},{7,6},{8,9},{9,8},{10,11... | collective-permute-start | bytes 98312 | tf_op jit(solution)/shard_map/ppermute | solution.py:79
  132.4 6.6 %collective-permute-start.32 = (f32[8,512]{1,0:T(8,128)S(1)}, f32[8,512]{1,0:T(8,128)S(1)}, u32[]{:S(2)}, u32[]{:S(2)}) collective-permute-start(f32[8,512]{1,0:T(8,128)S(1)} %copy-done.34), channel_id=1, source_target_pairs={{0,1},{1,0},{2,3},{3,2},{4,5},{5,4},{6,7},{7,6},{8,9},{9,8},{10,11... | collective-permute-start | bytes 49160 | tf_op jit(solution)/shard_map/ppermute | solution.py:79
  (14 other events, 27.7 us)

commit v4 on v3

--- a/solution.py
+++ b/solution.py
@@ -52,7 +52,7 @@
     return pltpu.with_memory_space_constraint(x, pltpu.HBM)
 
 
-def call(body, outs, *args, smem=0, plain=0, scratch=(), late=()):
+def call(body, outs, *args, smem=0, plain=0, plain_outs=0, scratch=(), late=()):
     specs = [pl.BlockSpec(memory_space=pltpu.SMEM)] * smem
     specs += [pl.BlockSpec(memory_space=pltpu.VMEM)] * (len(args) - smem - plain)
     specs += [pl.BlockSpec(memory_space=pl.ANY)] * (plain + len(late))
@@ -60,7 +60,8 @@
         skip(body, len(args), len(late)),
         out_shape=[pltpu.HBM(s, t) for s, t in outs],
         in_specs=specs,
-        out_specs=[pl.BlockSpec(memory_space=pltpu.VMEM)] * len(outs),
+        out_specs=[pl.BlockSpec(memory_space=pl.ANY)] * plain_outs
+        + [pl.BlockSpec(memory_space=pltpu.VMEM)] * (len(outs) - plain_outs),
         scratch_shapes=list(scratch),
         compiler_params=pltpu.CompilerParams(vmem_limit_bytes=VMEM_BYTES),
     )(*args, *late)
@@ -160,14 +161,23 @@
     return x.astype(BF)
 
 
-def forward_kernel(lengths, ctx, wt, w_out, *refs):
-    shards = refs[:16]
-    xn, up, slopes, proj, att, gh, sums = refs[16:]
-    c = ctx[0]
+def shard_loads(c, shards, xn, up, sems):
+    loads = []
     for i, rel in enumerate(REL):
         to = at(place_of(c, rel))
-        xn[:, to] = shards[i][...]
-        up[:, to] = shards[8 + i][...]
+        loads.append(pltpu.make_async_copy(shards[i], xn.at[:, to], sems.at[i]))
+        loads.append(pltpu.make_async_copy(shards[8 + i], up.at[:, to], sems.at[8 + i]))
+    return loads
+
+
+def forward_kernel(lengths, ctx, wt, w_out, *refs):
+    shards, results, (att, sums) = refs[:16], refs[16:19], refs[19:21]
+    xn, up, slopes, proj, gh, sems, out_sems = refs[21:]
+    loads = shard_loads(ctx[0], shards, xn, up, sems)
+    for load in loads:
+        load.start()
+    for load in loads:
+        load.wait()
     for n in range(GROUP // BLOCK):
         cols = slice(n * BLOCK, (n + 1) * BLOCK)
         p = dot(wt[...], xn[:, cols])
@@ -176,6 +186,12 @@
         slopes[:, cols] = (sig + out * (1.0 - sig)).astype(BF)
         proj[:, cols] = out.astype(BF)
         gh[:, cols] = dot(w_out[...], up[:, cols])
+    stores = [
+        pltpu.make_async_copy(v, out, out_sems.at[i])
+        for i, (v, out) in enumerate(zip((slopes, proj, gh), results))
+    ]
+    for store in stores:
+        store.start()
     low = first_visible(lengths)
     keys = proj[3 * WIDE :, :].astype(F32).T.astype(BF)
     for rb in range(GROUP // BLOCK):
@@ -200,19 +216,18 @@
     sums[2:3, :] = jnp.sum(gz, axis=0, keepdims=True)
     sums[3:4, :] = jnp.sum(gz * dev, axis=0, keepdims=True)
     sums[4:8, :] = jnp.zeros((4, GROUP), F32)
+    for store in stores:
+        store.wait()
 
 
 def backward_kernel(lengths, ctx, slopes, proj, att, gh, *refs):
-    sums, (xn_hbm, up_hbm) = refs[:8], refs[8:10]
-    own, other, up_part, down_part, far_up, far_down, weights = refs[10:17]
-    gp, gatt, dk, dv, xn, up, sems = refs[17:]
-    loads = [
-        pltpu.make_async_copy(xn_hbm, xn, sems.at[0]),
-        pltpu.make_async_copy(up_hbm, up, sems.at[1]),
-    ]
+    sums, shards = refs[:8], refs[8:24]
+    own, other, up_part, down_part, far_up, far_down, weights = refs[24:31]
+    gp, gatt, dk, dv, xn, up, sems, out_sems = refs[31:]
+    c = ctx[0]
+    loads = shard_loads(c, shards, xn, up, sems)
     for load in loads:
         load.start()
-    c = ctx[0]
     each = [s[...] for s in sums]
     mean = sum(s[0:1, :] for s in each) * (1.0 / N_CTX)
     spread = sum(s[1:2, :] + WIDE * jnp.square(s[0:1, :] - mean) for s in each)
@@ -261,13 +276,20 @@
     gp[4 * WIDE :, :] = (dk[...] * slopes[3 * WIDE :, :].astype(F32)).astype(BF)
 
     n, half = PART, PART // 2
+    moves = []
     for core in range(2):
-        (own, other)[core][...] = gp[:, at(place_of(c, (0, core)))]
-        up_part[core * n : core * n + n, :] = gp[:, at(place_of(c, (1, core)))]
-        down_part[core * n : core * n + n, :] = gp[:, at(place_of(c, (3, core)))]
-        opposite = at(place_of(c, (2, core)))
-        far_up[core * half : core * half + half, :] = gp[:half, opposite]
-        far_down[core * half : core * half + half, :] = gp[half:, opposite]
+        opposite = gp.at[:, at(place_of(c, (2, core)))]
+        mine = pl.ds(core * half, half)
+        moves += [
+            (gp.at[:, at(place_of(c, (0, core)))], (own, other)[core]),
+            (gp.at[:, at(place_of(c, (1, core)))], up_part.at[pl.ds(core * n, n), :]),
+            (gp.at[:, at(place_of(c, (3, core)))], down_part.at[pl.ds(core * n, n), :]),
+            (opposite.at[pl.ds(0, half), :], far_up.at[mine, :]),
+            (opposite.at[pl.ds(half, half), :], far_down.at[mine, :]),
+        ]
+    stores = [pltpu.make_async_copy(*m, out_sems.at[i]) for i, m in enumerate(moves)]
+    for store in stores:
+        store.start()
 
     for load in loads:
         load.wait()
@@ -277,6 +299,8 @@
         weights[4 * n : 4 * n + 4, :64, :] = part.reshape(4, 64, 4 * WIDE)
     mix = [dot(gp[:WIDE, :], up[h : h + 512, :], NT).reshape(N_DP, 8, 512) for h in (0, 512)]
     weights[:, 64:, :] = jnp.concatenate(mix, axis=1).astype(BF)
+    for store in stores:
+        store.wait()
 
 
 def sum_kernel(ctx, recv, *refs):
@@ -298,8 +322,9 @@
         part[8:, :] = rows((step, 1))
 
 
-def join_kernel(ctx, *refs):
-    parts, out = refs[:8], refs[8]
+def join_kernel(ctx, mixing, *refs):
+    parts, out, mixing_out = refs[:8], refs[8], refs[9]
+    mixing_out[...] = mixing[...]
     for i, part in enumerate(parts):
         core = i % 2
         src = place_of(ctx[0], ((4 - i // 2) % 4, core))
@@ -382,11 +407,11 @@
     )(ctx_s, w_out)
 
 
-def rows_back(ctx_s, place, w_project, w_out, parts, late):
-    cols = 256
+def rows_back(ctx_s, place, w_project, w_out, parts):
+    cols = 512
     whole = pl.BlockSpec(memory_space=pltpu.VMEM)
     return pl.pallas_call(
-        skip(rows_kernel, 14, 1),
+        rows_kernel,
         grid=(D // cols,),
         in_specs=[
             pl.BlockSpec(memory_space=pltpu.SMEM),
@@ -394,13 +419,12 @@
             pl.BlockSpec((cols, 4 * D), lambda n: (n, 0)),
             pl.BlockSpec((D, cols), lambda n: (0, n)),
         ]
-        + [whole] * 10
-        + [pl.BlockSpec(memory_space=pl.ANY)],
+        + [whole] * 10,
         out_specs=pl.BlockSpec((2 * R, cols), lambda n: (0, n)),
         out_shape=pltpu.HBM((2 * R, D), BF),
         scratch_shapes=[pltpu.VMEM((R, D), BF), pltpu.VMEM((4 * D, R), BF)],
         compiler_params=pltpu.CompilerParams(vmem_limit_bytes=VMEM_BYTES),
-    )(ctx_s, place, w_project, w_out, *parts, late)
+    )(ctx_s, place, w_project, w_out, *parts)
 
 
 def across(x, axis):
@@ -417,11 +441,10 @@
     w_own, w_out_own = own_weights(ctx_s, w_project), own_rows(ctx_s, w_out)
     arrived = across(packed, "dp")
     shard = call(place_kernel, [((D, R), BF)] * 2, arrived, place, late=(w_own, w_out_own))
-    xn, up, slopes, proj, att, gh, sums = call(
+    shards = [hbm(v) for v in ring_gather(*shard)]
+    slopes, proj, gh, att, sums = call(
         forward_kernel,
         [
-            ((D, GROUP), BF),
-            ((D, GROUP), BF),
             ((4 * WIDE, GROUP), BF),
             ((4 * WIDE, GROUP), BF),
             ((WIDE, GROUP), F32),
@@ -432,8 +455,19 @@
         ctx_s,
         w_own,
         w_out_own,
-        *[hbm(v) for v in ring_gather(*shard)],
+        *shards,
         smem=2,
+        plain=16,
+        plain_outs=3,
+        scratch=[
+            pltpu.VMEM((D, GROUP), BF),
+            pltpu.VMEM((D, GROUP), BF),
+            pltpu.VMEM((4 * WIDE, GROUP), BF),
+            pltpu.VMEM((4 * WIDE, GROUP), BF),
+            pltpu.VMEM((WIDE, GROUP), F32),
+            pltpu.SemaphoreType.DMA((16,)),
+            pltpu.SemaphoreType.DMA((3,)),
+        ],
     )
     all_sums = [sums] + [send(sums, step, 0) for step in (2, 1, 3)]
     all_sums += [send(v, 0, 1) for v in all_sums]
@@ -452,10 +486,10 @@
         ctx_s,
         *[hbm(v) for v in (slopes, proj, att, gh)],
         *all_sums,
-        hbm(xn),
-        hbm(up),
+        *shards,
         smem=2,
-        plain=2,
+        plain=16,
+        plain_outs=6,
         scratch=[
             pltpu.VMEM((PART, GROUP), BF),
             pltpu.VMEM((WIDE, GROUP), BF),
@@ -463,31 +497,35 @@
             pltpu.VMEM((WIDE, GROUP), F32),
             pltpu.VMEM((D, GROUP), BF),
             pltpu.VMEM((D, GROUP), BF),
-            pltpu.SemaphoreType.DMA((2,)),
+            pltpu.SemaphoreType.DMA((16,)),
+            pltpu.SemaphoreType.DMA((10,)),
         ],
     )
     parts = relay(own, other, (up_part, down_part), (far_up, far_down))
+    weights = across(weights, "dp")
+    rows = rows_back(ctx_s, place, w_project, w_out, parts)
     own, other, *chips, mixing = call(
         sum_kernel,
         [((8, 4 * WIDE), F32)] * 2 + [((16, 4 * WIDE), F32)] * 3 + [((8, D), F32)],
         ctx_s,
-        across(weights, "dp"),
+        weights,
         smem=1,
-        late=parts[1:],
+        late=(rows,),
         scratch=[pltpu.VMEM((64, 4 * WIDE), F32)],
     )
     owners = [(d * 8 + c, (2 * c + d // 8) * 8 + d % 8) for d in range(N_DP) for c in range(N_CTX)]
-    mixing_grad = lax.ppermute(mixing, ("dp", "ctx"), owners)
+    mixing = lax.ppermute(mixing, ("dp", "ctx"), owners)
     project = [own, send(other, 0, 1)]
     for step, part in zip((1, 2, 3), chips):
         part = send(part, step, 0)
         project += [part, send(part, 0, 1)]
-    rows = rows_back(ctx_s, place, w_project, w_out, parts, own)
     returned = across(rows, "dp")
     output, input_grad = call(
         unpack_kernel, [((R, D), BF), ((R, D), BF)], returned, history, grad_output, order
     )
-    (project_grad,) = call(join_kernel, [((8, 4 * D), F32)], ctx_s, *project, smem=1)
+    project_grad, mixing_grad = call(
+        join_kernel, [((8, 4 * D), F32), ((8, D), F32)], ctx_s, mixing, *project, smem=1
+    )
     return output, input_grad, project_grad, mixing_grad
 
 

time: 142 us -> 140 us (0.986)
  Pallas kernels: 38.8 us -> 37.3 us
    unnamed x71 -> x64, local copies, waits for them, and re-layouts: 4.85 us -> 5.22 us
  transfers between devices with their start and end apart: 43 -> 43, of which waited for: 18 -> 18; matrix products, arithmetic and copies ran while one was open for 0% -> 0% of each run, Pallas kernels for 4% -> 10%
where the time goes in v4:
time: 140 us; the launch traced here: 139 us
  starting transfers between devices  55.1 us (39%)
  waiting for transfers between devices  40.8 us (29%)
  Pallas kernels  37.3 us (27%)
  local copies, waits for them, and re-layouts  5.22 us (4%)
    ppermute x39, waiting for transfers between devices, send(): return lax.ppermute(x, 'ctx', pairs)  31.6 us
    ppermute x39, starting transfers between devices, send(): return lax.ppermute(x, 'ctx', pairs)  31.2 us
    pallas_call x7, Pallas kernels, call(): pl.pallas_call(skip(body, len(args), len(late)), out_shape=[pltpu.HBM(s,...  25.2 us
    all_to_all x3, starting transfers between devices, across(): return lax.all_to_all(x, axis, split_axis=0, concat_axis=0, tiled=True)  20.6 us
    pallas_call x1, Pallas kernels, rows_back(): pl.pallas_call(rows_kernel, grid=(D // cols,), in_specs=[pl.BlockSpec(mem...  6.8 us
    ppermute x1, waiting for transfers between devices, local(): mixing = lax.ppermute(mixing, ('dp', 'ctx'), owners)  5.37 us
    unnamed x64, local copies, waits for them, and re-layouts  5.22 us
    all_to_all x3, waiting for transfers between devices, across(): return lax.all_to_all(x, axis, split_axis=0, concat_axis=0, tiled=True)  3.89 us
  transfers between devices with their start and end apart: 43, of which 18 were waited for; matrix products, arithmetic and copies ran while one was open for 0% of the time, Pallas kernels for 10%

profile of v4, /device:TPU:98, one launch (start us, length us, event | category | flops | bytes accessed | tf_op | source)
XLA Modules:
  0.0 139.5 jit_solution(9493252281026160480)
XLA Ops:
  0.6 0.6 copy-done.10
  1.3 2.4 %shard_map.104 = bf16[256,1024]{1,0:T(8,128)(2,1)} custom-call(bf16[128,1024]{1,0:T(8,128)(2,1)} %hist.3, bf16[128,1024]{1,0:T(8,128)(2,1)} %gout.3, s32[1,128]{1,0:T(1,128)S(1)} %bitcast.10), custom_call_target="tpu_custom_call" | custom-call | tf_op jit(solution)/shard_map/pallas_call | solution.py:59
  3.6 7.2 %all-to-all-start = ((bf16[16,16,1024]{2,1,0:T(8,128)(2,1)}), bf16[16,16,1024]{2,1,0:T(8,128)(2,1)S(1)}, u32[]{:S(2)}, u32[]{:S(2)}) async-start(bf16[16,16,1024]{2,1,0:T(8,128)(2,1)} %bitcast.14), calls=%async_computation | async-start | bytes 1048576 | tf_op jit(solution)/shard_map/all_to_all | solution.py:431
  10.8 1.7 %shard_map.103.refs_3_.w_out = bf16[128,1024]{1,0:T(8,128)(2,1)} custom-call(s32[1]{0:T(128)} %bitcast.ctx.refs_0_, bf16[1024,1024]{1,0:T(8,128)(2,1)} %w_out.1), custom_call_target="tpu_custom_call" | custom-call | tf_op jit(solution)/shard_map/pallas_call | solution.py:397
  12.5 3.7 %shard_map.102.refs_2_.wt = bf16[512,1024]{1,0:T(8,128)(2,1)} custom-call(s32[1]{0:T(128)} %bitcast.ctx.refs_0_, bf16[1024,4096]{1,0:T(8,128)(2,1)} %w.3), custom_call_target="tpu_custom_call" | custom-call | tf_op jit(solution)/shard_map/pallas_call | solution.py:383
  16.2 3.9 %all-to-all-done = bf16[16,16,1024]{2,1,0:T(8,128)(2,1)S(1)} async-done(((bf16[16,16,1024]{2,1,0:T(8,128)(2,1)}), bf16[16,16,1024]{2,1,0:T(8,128)(2,1)S(1)}, u32[]{:S(2)}, u32[]{:S(2)}) %all-to-all-start) | async-done | bytes 524320 | tf_op jit(solution)/shard_map/all_to_all | solution.py:431
  20.1 1.2 copy-done
  21.3 1.1 shard_map.105
  22.4 1.5 %collective-permute-start.5 = (bf16[1024,128]{1,0:T(8,128)(2,1)}, bf16[1024,128]{1,0:T(8,128)(2,1)S(1)}, u32[]{:S(2)}, u32[]{:S(2)}) collective-permute-start(bf16[1024,128]{1,0:T(8,128)(2,1)} %get-tuple-element.28.refs_0_.refs_8_), channel_id=1, source_target_pairs={{0,2},{1,3},{2,4},{3,5},{4,6},{5,7},{6,0},{7,1},{8,10},{9,11},{10,... | collective-permute-start | bytes 786440 | tf_op jit(solution)/shard_map/ppermute | solution.py:80
  23.9 0.5 collective-permute-start.1
  24.4 1.5 %collective-permute-start.10 = (bf16[1024,128]{1,0:T(8,128)(2,1)}, bf16[1024,128]{1,0:T(8,128)(2,1)S(1)}, u32[]{:S(2)}, u32[]{:S(2)}) collective-permute-start(bf16[1024,128]{1,0:T(8,128)(2,1)} %get-tuple-element.29.refs_8_.refs_16_), channel_id=1, source_target_pairs={{0,2},{1,3},{2,4},{3,5},{4,6},{5,7},{6,0},{7,1},{8,10},{9,11},{10,... | collective-permute-start | bytes 786440 | tf_op jit(solution)/shard_map/ppermute | solution.py:80
  25.9 0.5 collective-permute-start.8
  26.5 4.8 %collective-permute-done.5.refs_6_.refs_14_ = bf16[1024,128]{1,0:T(8,128)(2,1)S(1)} collective-permute-done((bf16[1024,128]{1,0:T(8,128)(2,1)}, bf16[1024,128]{1,0:T(8,128)(2,1)S(1)}, u32[]{:S(2)}, u32[]{:S(2)}) %collective-permute-start.5) | collective-permute-done | bytes 262176 | tf_op jit(solution)/shard_map/ppermute | solution.py:80
  31.3 1.2 collective-permute-done.1.refs_2_.refs_10_
  32.5 0.6 collective-permute-start.3
  33.1 2.0 %collective-permute-done.10.refs_14_.refs_22_ = bf16[1024,128]{1,0:T(8,128)(2,1)S(1)} collective-permute-done((bf16[1024,128]{1,0:T(8,128)(2,1)}, bf16[1024,128]{1,0:T(8,128)(2,1)S(1)}, u32[]{:S(2)}, u32[]{:S(2)}) %collective-permute-start.10) | collective-permute-done | bytes 262176 | tf_op jit(solution)/shard_map/ppermute | solution.py:80
  35.2 1.5 %collective-permute-start.11 = (bf16[1024,128]{1,0:T(8,128)(2,1)S(1)}, bf16[1024,128]{1,0:T(8,128)(2,1)S(1)}, u32[]{:S(2)}, u32[]{:S(2)}) collective-permute-start(bf16[1024,128]{1,0:T(8,128)(2,1)S(1)} %collective-permute-done.10.refs_14_.refs_22_), channel_id=1, source_target_pairs={{0,2},{1,3},{2,4},{3,5},{4,6},{5,7},{6,0},{7,1},{8,10},{9,11},{10,... | collective-permute-start | bytes 786440 | tf_op jit(solution)/shard_map/ppermute | solution.py:80
  36.6 0.4 collective-permute-done.8.refs_10_.refs_18_
  37.1 0.5 collective-permute-start.13
  37.6 0.1 collective-permute-start.9
  37.7 4.3 %collective-permute-done.3.refs_4_.refs_12_ = bf16[1024,128]{1,0:T(8,128)(2,1)S(1)} collective-permute-done((bf16[1024,128]{1,0:T(8,128)(2,1)S(1)}, bf16[1024,128]{1,0:T(8,128)(2,1)S(1)}, u32[]{:S(2)}, u32[]{:S(2)}) %collective-permute-start.3) | collective-permute-done | bytes 262176 | tf_op jit(solution)/shard_map/ppermute | solution.py:80
  42.0 1.0 collective-permute-done.11.refs_12_.refs_20_
  43.0 0.5 collective-permute-done.4.refs_5_.refs_13_
  43.5 1.0 collective-permute-done.12.refs_13_.refs_21_
  44.6 0.7 copy-done.26
  45.3 8.2 %shard_map.106 = (bf16[512,1024]{1,0:T(8,128)(2,1)}, bf16[512,1024]{1,0:T(8,128)(2,1)}, f32[128,1024]{1,0:T(8,128)}, f32[128,1024]{1,0:T(8,128)}, f32[8,1024]{1,0:T(8,128)}) custom-call(s32[1,4]{1,0:T(1,128)S(1)} %copy-done.9, s32[1]{0:T(128)} %bitcast.ctx.refs_0_, bf16[512,1024]{1,0:T(8,128)(2,1)S(1)} %copy-done.1, bf16[128,1024]{1,0:T(8,128)(2,1)S(1)} %copy-done.3, ...), custom_call_target="tpu_custom_call" | custom-call | tf_op jit(solution)/shard_map/pallas_call | solution.py:59
  53.5 3.0 %collective-permute-start.16 = (f32[8,1024]{1,0:T(8,128)}, f32[8,1024]{1,0:T(8,128)S(1)}, u32[]{:S(2)}, u32[]{:S(2)}) collective-permute-start(f32[8,1024]{1,0:T(8,128)} %get-tuple-element.34.refs_0_), channel_id=1, source_target_pairs={{0,6},{1,7},{2,0},{3,1},{4,2},{5,3},{6,4},{7,5},{8,14},{9,15},{10,... | collective-permute-start | bytes 98312 | tf_op jit(solution)/shard_map/ppermute | solution.py:80
  56.5 2.2 %collective-permute-start.14 = (f32[8,1024]{1,0:T(8,128)}, f32[8,1024]{1,0:T(8,128)S(1)}, u32[]{:S(2)}, u32[]{:S(2)}) collective-permute-start(f32[8,1024]{1,0:T(8,128)} %get-tuple-element.34.refs_0_), channel_id=1, source_target_pairs={{0,4},{1,5},{2,6},{3,7},{4,0},{5,1},{6,2},{7,3},{8,12},{9,13},{10,... | collective-permute-start | bytes 98312 | tf_op jit(solution)/shard_map/ppermute | solution.py:80
  58.7 0.5 collective-permute-start.20
  59.2 1.4 %collective-permute-done.15.refs_2_ = f32[8,1024]{1,0:T(8,128)S(1)} collective-permute-done((f32[8,1024]{1,0:T(8,128)}, f32[8,1024]{1,0:T(8,128)S(1)}, u32[]{:S(2)}, u32[]{:S(2)}) %collective-permute-start.15) | collective-permute-done | bytes 32800 | tf_op jit(solution)/shard_map/ppermute | solution.py:80
  60.7 1.5 %collective-permute-done.14.refs_1_ = f32[8,1024]{1,0:T(8,128)S(1)} collective-permute-done((f32[8,1024]{1,0:T(8,128)}, f32[8,1024]{1,0:T(8,128)S(1)}, u32[]{:S(2)}, u32[]{:S(2)}) %collective-permute-start.14) | collective-permute-done | bytes 32800 | tf_op jit(solution)/shard_map/ppermute | solution.py:80
  62.2 1.2 collective-permute-done.18.refs_5_
  63.4 0.8 copy-done.7
  64.1 10.7 %shard_map.107 = (bf16[640,128]{1,0:T(8,128)(2,1)}, bf16[640,128]{1,0:T(8,128)(2,1)}, bf16[1280,128]{1,0:T(8,128)(2,1)}, bf16[1280,128]{1,0:T(8,128)(2,1)}, bf16...) custom-call(s32[1,4]{1,0:T(1,128)S(1)} %copy-done.9, s32[1]{0:T(128)} %bitcast.ctx.refs_0_, ...), custom_call_target="tpu_custom_call" | custom-call | tf_op jit(solution)/shard_map/pallas_call | solution.py:59
  74.9 6.1 %all-to-all-start.2 = ((bf16[16,80,512]{2,1,0:T(8,128)(2,1)}), bf16[16,80,512]{2,1,0:T(8,128)(2,1)S(1)}, u32[]{:S(2)}, u32[]{:S(2)}) async-start(bf16[16,80,512]{2,1,0:T(8,128)(2,1)} %get-tuple-element.43), calls=%async_computation.2 | async-start | bytes 2621440 | tf_op jit(solution)/shard_map/all_to_all | solution.py:431
  81.0 0.4 collective-permute-start.22
  81.4 1.8 %collective-permute-start.24 = (bf16[1280,128]{1,0:T(8,128)(2,1)S(1)}, bf16[1280,128]{1,0:T(8,128)(2,1)S(1)}, u32[]{:S(2)}, u32[]{:S(2)}) collective-permute-start(bf16[1280,128]{1,0:T(8,128)(2,1)S(1)} %copy-done.27), channel_id=1, source_target_pairs={{0,6},{1,7},{2,0},{3,1},{4,2},{5,3},{6,4},{7,5},{8,14},{9,15},{10,... | collective-permute-start | bytes 983048 | tf_op jit(solution)/shard_map/ppermute | solution.py:80
  83.2 0.7 collective-permute-start.26
  83.9 2.5 %collective-permute-start.29 = (bf16[640,128]{1,0:T(8,128)(2,1)S(1)}, bf16[640,128]{1,0:T(8,128)(2,1)S(1)}, u32[]{:S(2)}, u32[]{:S(2)}) collective-permute-start(bf16[640,128]{1,0:T(8,128)(2,1)S(1)} %copy-done.30), channel_id=1, source_target_pairs={{0,6},{1,7},{2,0},{3,1},{4,2},{5,3},{6,4},{7,5},{8,14},{9,15},{10,... | collective-permute-start | bytes 491528 | tf_op jit(solution)/shard_map/ppermute | solution.py:80
  86.4 7.9 %collective-permute-done.26 = bf16[640,128]{1,0:T(8,128)(2,1)S(1)} collective-permute-done((bf16[640,128]{1,0:T(8,128)(2,1)S(1)}, bf16[640,128]{1,0:T(8,128)(2,1)S(1)}, u32[]{:S(2)}, u32[]{:S(2)}) %collective-permute-start.26) | collective-permute-done | bytes 163872 | tf_op jit(solution)/shard_map/ppermute | solution.py:80
  94.4 0.4 collective-permute-done.29
  94.8 2.5 %collective-permute-start.30 = (bf16[640,128]{1,0:T(8,128)(2,1)S(1)}, bf16[640,128]{1,0:T(8,128)(2,1)S(1)}, u32[]{:S(2)}, u32[]{:S(2)}) collective-permute-start(bf16[640,128]{1,0:T(8,128)(2,1)S(1)} %collective-permute-done.29), channel_id=1, source_target_pairs={{0,6},{1,7},{2,0},{3,1},{4,2},{5,3},{6,4},{7,5},{8,14},{9,15},{10,... | collective-permute-start | bytes 491528 | tf_op jit(solution)/shard_map/ppermute | solution.py:80
  97.3 0.5 collective-permute-start.25
  97.9 0.1 collective-permute-start.21
  97.9 2.8 %collective-permute-done.27.refs_6_ = bf16[640,128]{1,0:T(8,128)(2,1)S(1)} collective-permute-done((bf16[640,128]{1,0:T(8,128)(2,1)S(1)}, bf16[640,128]{1,0:T(8,128)(2,1)S(1)}, u32[]{:S(2)}, u32[]{:S(2)}) %collective-permute-start.27) | collective-permute-done | bytes 163872 | tf_op jit(solution)/shard_map/ppermute | solution.py:80
  100.7 0.5 collective-permute-start.31
  101.2 0.9 collective-permute-done.28.refs_7_
  102.1 0.2 collective-permute-done.31.refs_9_
  102.3 6.8 %shard_map.108.refs_2_ = bf16[256,1024]{1,0:T(8,128)(2,1)} custom-call(s32[1]{0:T(128)} %bitcast.ctx.refs_0_, s32[1,128]{1,0:T(1,128)S(1)} %bitcast.13, bf16[1024,4096]{1,0:T(8,128)(2,1)} %w.3, bf16[1024,1024]{1,0:T(8,128)(2,1)} %w_out.1, bf16[640,128]{1,0:T(8,128)(2,1)S(1)} %copy-done.6, bf16[640,128]{1,0:T(8,128)(2,1)S(1)} %collective-permute-done.21.refs_1_, ...), custom_call_target="tpu_custom_call" | custom-call | tf_op jit(solution)/shard_map/pallas_call | solution.py:413
  109.2 7.4 %all-to-all-start.1 = ((bf16[16,16,1024]{2,1,0:T(8,128)(2,1)}), bf16[16,16,1024]{2,1,0:T(8,128)(2,1)S(1)}, u32[]{:S(2)}, u32[]{:S(2)}) async-start(bf16[16,16,1024]{2,1,0:T(8,128)(2,1)} %bitcast.7), calls=%async_computation.1 | async-start | bytes 1048576 | tf_op jit(solution)/shard_map/all_to_all | solution.py:431
  116.5 1.1 copy-done.2
  117.6 0.8 shard_map.110
  118.4 2.3 %collective-permute-start.34 = (f32[16,512]{1,0:T(8,128)}, f32[16,512]{1,0:T(8,128)S(1)}, u32[]{:S(2)}, u32[]{:S(2)}) collective-permute-start(f32[16,512]{1,0:T(8,128)} %get-tuple-element.47), channel_id=1, source_target_pairs={{0,2},{1,3},{2,4},{3,5},{4,6},{5,7},{6,0},{7,1},{8,10},{9,11},{10,... | collective-permute-start | bytes 98312 | tf_op jit(solution)/shard_map/ppermute | solution.py:80
  120.7 2.9 %collective-permute-start.36 = (f32[16,512]{1,0:T(8,128)}, f32[16,512]{1,0:T(8,128)S(1)}, u32[]{:S(2)}, u32[]{:S(2)}) collective-permute-start(f32[16,512]{1,0:T(8,128)} %get-tuple-element.48), channel_id=1, source_target_pairs={{0,4},{1,5},{2,6},{3,7},{4,0},{5,1},{6,2},{7,3},{8,12},{9,13},{10,... | collective-permute-start | bytes 98312 | tf_op jit(solution)/shard_map/ppermute | solution.py:80
  123.6 2.4 %collective-permute-start.38 = (f32[16,512]{1,0:T(8,128)}, f32[16,512]{1,0:T(8,128)S(1)}, u32[]{:S(2)}, u32[]{:S(2)}) collective-permute-start(f32[16,512]{1,0:T(8,128)} %get-tuple-element.49), channel_id=1, source_target_pairs={{0,6},{1,7},{2,0},{3,1},{4,2},{5,3},{6,4},{7,5},{8,14},{9,15},{10,... | collective-permute-start | bytes 98312 | tf_op jit(solution)/shard_map/ppermute | solution.py:80
  126.1 3.3 %collective-permute-start.32 = (f32[8,1024]{1,0:T(8,128)}, f32[8,1024]{1,0:T(8,128)S(1)}, u32[]{:S(2)}, u32[]{:S(2)}) collective-permute-start(f32[8,1024]{1,0:T(8,128)} %get-tuple-element.44), channel_id=1, source_target_pairs={{0,0},{1,16},{2,32},{3,48},{4,64},{5,80},{6,96},{7,112},{8,1},{9,1... | collective-permute-start | bytes 98312 | tf_op jit(solution)/shard_map/ppermute | solution.py:517
  129.4 1.4 %collective-permute-start.35 = (f32[16,512]{1,0:T(8,128)S(1)}, f32[16,512]{1,0:T(8,128)S(1)}, u32[]{:S(2)}, u32[]{:S(2)}) collective-permute-start(f32[16,512]{1,0:T(8,128)S(1)} %collective-permute-done.34.refs_2_), channel_id=1, source_target_pairs={{0,1},{1,0},{2,3},{3,2},{4,5},{5,4},{6,7},{7,6},{8,9},{9,8},{10,11... | collective-permute-start | bytes 98312 | tf_op jit(solution)/shard_map/ppermute | solution.py:80
  130.8 0.1 collective-permute-start.37
  130.9 0.4 collective-permute-start.39
  131.3 0.1 collective-permute-start.33
  131.4 1.3 shard_map.109
  132.7 5.4 %collective-permute-done.32.mixing = f32[8,1024]{1,0:T(8,128)S(1)} collective-permute-done((f32[8,1024]{1,0:T(8,128)}, f32[8,1024]{1,0:T(8,128)S(1)}, u32[]{:S(2)}, u32[]{:S(2)}) %collective-permute-start.32) | collective-permute-done | bytes 32800 | tf_op jit(solution)/shard_map/ppermute | solution.py:517
  138.1 0.7 copy-done.8
  138.8 0.7 shard_map.111
  (96 shorter events, 0.2 us)
Async XLA Ops:
  3.6 16.4 %all-to-all-start = ((bf16[16,16,1024]{2,1,0:T(8,128)(2,1)}), bf16[16,16,1024]{2,1,0:T(8,128)(2,1)S(1)}, u32[]{:S(2)}, u32[]{:S(2)}) async-start(bf16[16,16,1024]{2,1,0:T(8,128)(2,1)} %bitcast.14), calls=%async_computation | async-start | bytes 1048576 | tf_op jit(solution)/shard_map/all_to_all | solution.py:431
  12.5 7.6 %copy-start.3 = (bf16[128,1024]{1,0:T(8,128)(2,1)S(1)}, bf16[128,1024]{1,0:T(8,128)(2,1)}, u32[]{:S(2)}) copy-start(bf16[128,1024]{1,0:T(8,128)(2,1)} %shard_map.103.refs_3_.w_out) | copy-start | bytes 786436
  12.5 7.6 %copy-start.12 = (s32[128]{0:T(128)S(1)}, s32[128]{0:T(128)}, u32[]{:S(2)}) copy-start(s32[128]{0:T(128)} %param.11) | copy-start | bytes 1540
  12.5 32.9 %copy-start.9 = (s32[1,4]{1,0:T(1,128)S(1)}, s32[1,4]{1,0:T(1,128)}, u32[]{:S(2)}) copy-start(s32[1,4]{1,0:T(1,128)} %lengths.3) | copy-start | bytes 52
  21.3 24.1 %copy-start.1 = (bf16[512,1024]{1,0:T(8,128)(2,1)S(1)}, bf16[512,1024]{1,0:T(8,128)(2,1)}, u32[]{:S(2)}) copy-start(bf16[512,1024]{1,0:T(8,128)(2,1)} %shard_map.102.refs_2_.wt) | copy-start | bytes 3145732
  22.4 8.8 %collective-permute-start.5 = (bf16[1024,128]{1,0:T(8,128)(2,1)}, bf16[1024,128]{1,0:T(8,128)(2,1)S(1)}, u32[]{:S(2)}, u32[]{:S(2)}) collective-permute-start(bf16[1024,128]{1,0:T(8,128)(2,1)} %get-tuple-element.28.refs_0_.refs_8_), channel_id=1, source_target_pairs={{0,2},{1,3},{2,4},{3,5},{4,6},{5,7},{6,0},{7,1},{8,10},{9,11},{10,... | collective-permute-start | bytes 786440 | tf_op jit(solution)/shard_map/ppermute | solution.py:80
  23.9 8.5 %collective-permute-start.1 = (bf16[1024,128]{1,0:T(8,128)(2,1)}, bf16[1024,128]{1,0:T(8,128)(2,1)S(1)}, u32[]{:S(2)}, u32[]{:S(2)}) collective-permute-start(bf16[1024,128]{1,0:T(8,128)(2,1)} %get-tuple-element.28.refs_0_.refs_8_), channel_id=1, source_target_pairs={{0,6},{1,7},{2,0},{3,1},{4,2},{5,3},{6,4},{7,5},{8,14},{9,15},{10,... | collective-permute-start | bytes 786440 | tf_op jit(solution)/shard_map/ppermute | solution.py:80
  24.4 8.0 %collective-permute-start = (bf16[1024,128]{1,0:T(8,128)(2,1)}, bf16[1024,128]{1,0:T(8,128)(2,1)S(1)}, u32[]{:S(2)}, u32[]{:S(2)}) collective-permute-start(bf16[1024,128]{1,0:T(8,128)(2,1)} %get-tuple-element.28.refs_0_.refs_8_), channel_id=1, source_target_pairs={{0,1},{1,0},{2,3},{3,2},{4,5},{5,4},{6,7},{7,6},{8,9},{9,8},{10,11... | collective-permute-start | bytes 786440 | tf_op jit(solution)/shard_map/ppermute | solution.py:80
  24.4 10.7 %collective-permute-start.10 = (bf16[1024,128]{1,0:T(8,128)(2,1)}, bf16[1024,128]{1,0:T(8,128)(2,1)S(1)}, u32[]{:S(2)}, u32[]{:S(2)}) collective-permute-start(bf16[1024,128]{1,0:T(8,128)(2,1)} %get-tuple-element.29.refs_8_.refs_16_), channel_id=1, source_target_pairs={{0,2},{1,3},{2,4},{3,5},{4,6},{5,7},{6,0},{7,1},{8,10},{9,11},{10,... | collective-permute-start | bytes 786440 | tf_op jit(solution)/shard_map/ppermute | solution.py:80
  25.9 11.1 %collective-permute-start.8 = (bf16[1024,128]{1,0:T(8,128)(2,1)}, bf16[1024,128]{1,0:T(8,128)(2,1)S(1)}, u32[]{:S(2)}, u32[]{:S(2)}) collective-permute-start(bf16[1024,128]{1,0:T(8,128)(2,1)} %get-tuple-element.29.refs_8_.refs_16_), channel_id=1, source_target_pairs={{0,6},{1,7},{2,0},{3,1},{4,2},{5,3},{6,4},{7,5},{8,14},{9,15},{10,... | collective-permute-start | bytes 786440 | tf_op jit(solution)/shard_map/ppermute | solution.py:80
  31.3 13.3 %copy-start.13 = (bf16[1024,128]{1,0:T(8,128)(2,1)}, bf16[1024,128]{1,0:T(8,128)(2,1)S(1)}, u32[]{:S(2)}) copy-start(bf16[1024,128]{1,0:T(8,128)(2,1)S(1)} %collective-permute-done.5.refs_6_.refs_14_) | copy-start | bytes 786436
  31.3 5.8 %collective-permute-start.7 = (bf16[1024,128]{1,0:T(8,128)(2,1)}, bf16[1024,128]{1,0:T(8,128)(2,1)S(1)}, u32[]{:S(2)}, u32[]{:S(2)}) collective-permute-start(bf16[1024,128]{1,0:T(8,128)(2,1)} %get-tuple-element.29.refs_8_.refs_16_), channel_id=1, source_target_pairs={{0,1},{1,0},{2,3},{3,2},{4,5},{5,4},{6,7},{7,6},{8,9},{9,8},{10,11... | collective-permute-start | bytes 786440 | tf_op jit(solution)/shard_map/ppermute | solution.py:80
  32.5 12.1 %copy-start.14 = (bf16[1024,128]{1,0:T(8,128)(2,1)}, bf16[1024,128]{1,0:T(8,128)(2,1)S(1)}, u32[]{:S(2)}) copy-start(bf16[1024,128]{1,0:T(8,128)(2,1)S(1)} %collective-permute-done.1.refs_2_.refs_10_) | copy-start | bytes 786436
  32.5 5.1 %collective-permute-start.6 = (bf16[1024,128]{1,0:T(8,128)(2,1)S(1)}, bf16[1024,128]{1,0:T(8,128)(2,1)S(1)}, u32[]{:S(2)}, u32[]{:S(2)}) collective-permute-start(bf16[1024,128]{1,0:T(8,128)(2,1)S(1)} %collective-permute-done.5.refs_6_.refs_14_), channel_id=1, source_target_pairs={{0,1},{1,0},{2,3},{3,2},{4,5},{5,4},{6,7},{7,6},{8,9},{9,8},{10,11... | collective-permute-start | bytes 786440 | tf_op jit(solution)/shard_map/ppermute | solution.py:80
  32.5 12.0 %copy-start.15 = (bf16[1024,128]{1,0:T(8,128)(2,1)}, bf16[1024,128]{1,0:T(8,128)(2,1)S(1)}, u32[]{:S(2)}) copy-start(bf16[1024,128]{1,0:T(8,128)(2,1)S(1)} %collective-permute-done.refs_1_.refs_9_) | copy-start | bytes 786436
  32.5 9.5 %collective-permute-start.3 = (bf16[1024,128]{1,0:T(8,128)(2,1)S(1)}, bf16[1024,128]{1,0:T(8,128)(2,1)S(1)}, u32[]{:S(2)}, u32[]{:S(2)}) collective-permute-start(bf16[1024,128]{1,0:T(8,128)(2,1)S(1)} %collective-permute-done.1.refs_2_.refs_10_), channel_id=1, source_target_pairs={{0,6},{1,7},{2,0},{3,1},{4,2},{5,3},{6,4},{7,5},{8,14},{9,15},{10,... | collective-permute-start | bytes 786440 | tf_op jit(solution)/shard_map/ppermute | solution.py:80
  35.2 9.4 %copy-start.16 = (bf16[1024,128]{1,0:T(8,128)(2,1)}, bf16[1024,128]{1,0:T(8,128)(2,1)S(1)}, u32[]{:S(2)}) copy-start(bf16[1024,128]{1,0:T(8,128)(2,1)S(1)} %collective-permute-done.10.refs_14_.refs_22_) | copy-start | bytes 786436
  35.2 7.8 %collective-permute-start.11 = (bf16[1024,128]{1,0:T(8,128)(2,1)S(1)}, bf16[1024,128]{1,0:T(8,128)(2,1)S(1)}, u32[]{:S(2)}, u32[]{:S(2)}) collective-permute-start(bf16[1024,128]{1,0:T(8,128)(2,1)S(1)} %collective-permute-done.10.refs_14_.refs_22_), channel_id=1, source_target_pairs={{0,2},{1,3},{2,4},{3,5},{4,6},{5,7},{6,0},{7,1},{8,10},{9,11},{10,... | collective-permute-start | bytes 786440 | tf_op jit(solution)/shard_map/ppermute | solution.py:80
  37.1 7.5 %copy-start.17 = (bf16[1024,128]{1,0:T(8,128)(2,1)}, bf16[1024,128]{1,0:T(8,128)(2,1)S(1)}, u32[]{:S(2)}) copy-start(bf16[1024,128]{1,0:T(8,128)(2,1)S(1)} %collective-permute-done.8.refs_10_.refs_18_) | copy-start | bytes 786436
  37.1 5.9 %collective-permute-start.2 = (bf16[1024,128]{1,0:T(8,128)(2,1)S(1)}, bf16[1024,128]{1,0:T(8,128)(2,1)S(1)}, u32[]{:S(2)}, u32[]{:S(2)}) collective-permute-start(bf16[1024,128]{1,0:T(8,128)(2,1)S(1)} %collective-permute-done.1.refs_2_.refs_10_), channel_id=1, source_target_pairs={{0,1},{1,0},{2,3},{3,2},{4,5},{5,4},{6,7},{7,6},{8,9},{9,8},{10,11... | collective-permute-start | bytes 786440 | tf_op jit(solution)/shard_map/ppermute | solution.py:80
  37.1 7.5 %copy-start.18 = (bf16[1024,128]{1,0:T(8,128)(2,1)}, bf16[1024,128]{1,0:T(8,128)(2,1)S(1)}, u32[]{:S(2)}) copy-start(bf16[1024,128]{1,0:T(8,128)(2,1)S(1)} %collective-permute-done.7.refs_9_.refs_17_) | copy-start | bytes 786436
  37.1 5.9 %collective-permute-start.13 = (bf16[1024,128]{1,0:T(8,128)(2,1)S(1)}, bf16[1024,128]{1,0:T(8,128)(2,1)S(1)}, u32[]{:S(2)}, u32[]{:S(2)}) collective-permute-start(bf16[1024,128]{1,0:T(8,128)(2,1)S(1)} %collective-permute-done.10.refs_14_.refs_22_), channel_id=1, source_target_pairs={{0,1},{1,0},{2,3},{3,2},{4,5},{5,4},{6,7},{7,6},{8,9},{9,8},{10,11... | collective-permute-start | bytes 786440 | tf_op jit(solution)/shard_map/ppermute | solution.py:80
  37.6 7.0 %copy-start.19 = (bf16[1024,128]{1,0:T(8,128)(2,1)}, bf16[1024,128]{1,0:T(8,128)(2,1)S(1)}, u32[]{:S(2)}) copy-start(bf16[1024,128]{1,0:T(8,128)(2,1)S(1)} %collective-permute-done.6.refs_7_.refs_15_) | copy-start | bytes 786436
  37.6 5.4 %collective-permute-start.9 = (bf16[1024,128]{1,0:T(8,128)(2,1)S(1)}, bf16[1024,128]{1,0:T(8,128)(2,1)S(1)}, u32[]{:S(2)}, u32[]{:S(2)}) collective-permute-start(bf16[1024,128]{1,0:T(8,128)(2,1)S(1)} %collective-permute-done.8.refs_10_.refs_18_), channel_id=1, source_target_pairs={{0,1},{1,0},{2,3},{3,2},{4,5},{5,4},{6,7},{7,6},{8,9},{9,8},{10,11... | collective-permute-start | bytes 786440 | tf_op jit(solution)/shard_map/ppermute | solution.py:80
  42.0 2.6 %copy-start.20 = (bf16[1024,128]{1,0:T(8,128)(2,1)}, bf16[1024,128]{1,0:T(8,128)(2,1)S(1)}, u32[]{:S(2)}) copy-start(bf16[1024,128]{1,0:T(8,128)(2,1)S(1)} %collective-permute-done.3.refs_4_.refs_12_) | copy-start | bytes 786436
  42.0 1.5 %collective-permute-start.4 = (bf16[1024,128]{1,0:T(8,128)(2,1)S(1)}, bf16[1024,128]{1,0:T(8,128)(2,1)S(1)}, u32[]{:S(2)}, u32[]{:S(2)}) collective-permute-start(bf16[1024,128]{1,0:T(8,128)(2,1)S(1)} %collective-permute-done.3.refs_4_.refs_12_), channel_id=1, source_target_pairs={{0,1},{1,0},{2,3},{3,2},{4,5},{5,4},{6,7},{7,6},{8,9},{9,8},{10,11... | collective-permute-start | bytes 786440 | tf_op jit(solution)/shard_map/ppermute | solution.py:80
  43.0 1.5 %collective-permute-start.12 = (bf16[1024,128]{1,0:T(8,128)(2,1)S(1)}, bf16[1024,128]{1,0:T(8,128)(2,1)S(1)}, u32[]{:S(2)}, u32[]{:S(2)}) collective-permute-start(bf16[1024,128]{1,0:T(8,128)(2,1)S(1)} %collective-permute-done.11.refs_12_.refs_20_), channel_id=1, source_target_pairs={{0,1},{1,0},{2,3},{3,2},{4,5},{5,4},{6,7},{7,6},{8,9},{9,8},{10,11... | collective-permute-start | bytes 786440 | tf_op jit(solution)/shard_map/ppermute | solution.py:80
  53.5 5.2 %collective-permute-start.16 = (f32[8,1024]{1,0:T(8,128)}, f32[8,1024]{1,0:T(8,128)S(1)}, u32[]{:S(2)}, u32[]{:S(2)}) collective-permute-start(f32[8,1024]{1,0:T(8,128)} %get-tuple-element.34.refs_0_), channel_id=1, source_target_pairs={{0,6},{1,7},{2,0},{3,1},{4,2},{5,3},{6,4},{7,5},{8,14},{9,15},{10,... | collective-permute-start | bytes 98312 | tf_op jit(solution)/shard_map/ppermute | solution.py:80
  56.5 4.1 %collective-permute-start.15 = (f32[8,1024]{1,0:T(8,128)}, f32[8,1024]{1,0:T(8,128)S(1)}, u32[]{:S(2)}, u32[]{:S(2)}) collective-permute-start(f32[8,1024]{1,0:T(8,128)} %get-tuple-element.34.refs_0_), channel_id=1, source_target_pairs={{0,2},{1,3},{2,4},{3,5},{4,6},{5,7},{6,0},{7,1},{8,10},{9,11},{10,... | collective-permute-start | bytes 98312 | tf_op jit(solution)/shard_map/ppermute | solution.py:80
  56.5 5.6 %collective-permute-start.14 = (f32[8,1024]{1,0:T(8,128)}, f32[8,1024]{1,0:T(8,128)S(1)}, u32[]{:S(2)}, u32[]{:S(2)}) collective-permute-start(f32[8,1024]{1,0:T(8,128)} %get-tuple-element.34.refs_0_), channel_id=1, source_target_pairs={{0,4},{1,5},{2,6},{3,7},{4,0},{5,1},{6,2},{7,3},{8,12},{9,13},{10,... | collective-permute-start | bytes 98312 | tf_op jit(solution)/shard_map/ppermute | solution.py:80
  58.7 3.5 %collective-permute-start.17 = (f32[8,1024]{1,0:T(8,128)}, f32[8,1024]{1,0:T(8,128)S(1)}, u32[]{:S(2)}, u32[]{:S(2)}) collective-permute-start(f32[8,1024]{1,0:T(8,128)} %get-tuple-element.34.refs_0_), channel_id=1, source_target_pairs={{0,1},{1,0},{2,3},{3,2},{4,5},{5,4},{6,7},{7,6},{8,9},{9,8},{10,11... | collective-permute-start | bytes 98312 | tf_op jit(solution)/shard_map/ppermute | solution.py:80
  58.7 3.5 %collective-permute-start.20 = (f32[8,1024]{1,0:T(8,128)S(1)}, f32[8,1024]{1,0:T(8,128)S(1)}, u32[]{:S(2)}, u32[]{:S(2)}) collective-permute-start(f32[8,1024]{1,0:T(8,128)S(1)} %collective-permute-done.16.refs_3_), channel_id=1, source_target_pairs={{0,1},{1,0},{2,3},{3,2},{4,5},{5,4},{6,7},{7,6},{8,9},{9,8},{10,11... | collective-permute-start | bytes 98312 | tf_op jit(solution)/shard_map/ppermute | solution.py:80
  60.7 1.5 %collective-permute-start.19 = (f32[8,1024]{1,0:T(8,128)S(1)}, f32[8,1024]{1,0:T(8,128)S(1)}, u32[]{:S(2)}, u32[]{:S(2)}) collective-permute-start(f32[8,1024]{1,0:T(8,128)S(1)} %collective-permute-done.15.refs_2_), channel_id=1, source_target_pairs={{0,1},{1,0},{2,3},{3,2},{4,5},{5,4},{6,7},{7,6},{8,9},{9,8},{10,11... | collective-permute-start | bytes 98312 | tf_op jit(solution)/shard_map/ppermute | solution.py:80
  62.2 1.2 collective-permute-start.18
  74.9 6.1 %copy-start.28 = (bf16[1280,128]{1,0:T(8,128)(2,1)S(1)}, bf16[1280,128]{1,0:T(8,128)(2,1)}, u32[]{:S(2)}) copy-start(bf16[1280,128]{1,0:T(8,128)(2,1)} %get-tuple-element.37) | copy-start | bytes 983044
  74.9 6.5 %copy-start.27 = (bf16[1280,128]{1,0:T(8,128)(2,1)S(1)}, bf16[1280,128]{1,0:T(8,128)(2,1)}, u32[]{:S(2)}) copy-start(bf16[1280,128]{1,0:T(8,128)(2,1)} %get-tuple-element.38) | copy-start | bytes 983044
  74.9 8.3 %copy-start.31 = (bf16[640,128]{1,0:T(8,128)(2,1)S(1)}, bf16[640,128]{1,0:T(8,128)(2,1)}, u32[]{:S(2)}) copy-start(bf16[640,128]{1,0:T(8,128)(2,1)} %get-tuple-element.39) | copy-start | bytes 491524
  74.9 9.0 %copy-start.30 = (bf16[640,128]{1,0:T(8,128)(2,1)S(1)}, bf16[640,128]{1,0:T(8,128)(2,1)}, u32[]{:S(2)}) copy-start(bf16[640,128]{1,0:T(8,128)(2,1)} %get-tuple-element.40) | copy-start | bytes 491524
  74.9 22.9 %copy-start.29 = (bf16[640,128]{1,0:T(8,128)(2,1)S(1)}, bf16[640,128]{1,0:T(8,128)(2,1)}, u32[]{:S(2)}) copy-start(bf16[640,128]{1,0:T(8,128)(2,1)} %get-tuple-element.36) | copy-start | bytes 491524
  74.9 27.4 %copy-start.6 = (bf16[640,128]{1,0:T(8,128)(2,1)S(1)}, bf16[640,128]{1,0:T(8,128)(2,1)}, u32[]{:S(2)}) copy-start(bf16[640,128]{1,0:T(8,128)(2,1)} %get-tuple-element.35.refs_0_) | copy-start | bytes 491524
  74.9 34.2 %all-to-all-start.2 = ((bf16[16,80,512]{2,1,0:T(8,128)(2,1)}), bf16[16,80,512]{2,1,0:T(8,128)(2,1)S(1)}, u32[]{:S(2)}, u32[]{:S(2)}) async-start(bf16[16,80,512]{2,1,0:T(8,128)(2,1)} %get-tuple-element.43), calls=%async_computation.2 | async-start | bytes 2621440 | tf_op jit(solution)/shard_map/all_to_all | solution.py:431
  81.0 16.3 %collective-permute-start.22 = (bf16[1280,128]{1,0:T(8,128)(2,1)S(1)}, bf16[1280,128]{1,0:T(8,128)(2,1)S(1)}, u32[]{:S(2)}, u32[]{:S(2)}) collective-permute-start(bf16[1280,128]{1,0:T(8,128)(2,1)S(1)} %copy-done.28), channel_id=1, source_target_pairs={{0,2},{1,3},{2,4},{3,5},{4,6},{5,7},{6,0},{7,1},{8,10},{9,11},{10,... | collective-permute-start | bytes 983048 | tf_op jit(solution)/shard_map/ppermute | solution.py:80
  81.4 16.0 %collective-permute-start.24 = (bf16[1280,128]{1,0:T(8,128)(2,1)S(1)}, bf16[1280,128]{1,0:T(8,128)(2,1)S(1)}, u32[]{:S(2)}, u32[]{:S(2)}) collective-permute-start(bf16[1280,128]{1,0:T(8,128)(2,1)S(1)} %copy-done.27), channel_id=1, source_target_pairs={{0,6},{1,7},{2,0},{3,1},{4,2},{5,3},{6,4},{7,5},{8,14},{9,15},{10,... | collective-permute-start | bytes 983048 | tf_op jit(solution)/shard_map/ppermute | solution.py:80
  83.2 11.2 %collective-permute-start.26 = (bf16[640,128]{1,0:T(8,128)(2,1)S(1)}, bf16[640,128]{1,0:T(8,128)(2,1)S(1)}, u32[]{:S(2)}, u32[]{:S(2)}) collective-permute-start(bf16[640,128]{1,0:T(8,128)(2,1)S(1)} %copy-done.31), channel_id=1, source_target_pairs={{0,2},{1,3},{2,4},{3,5},{4,6},{5,7},{6,0},{7,1},{8,10},{9,11},{10,... | collective-permute-start | bytes 491528 | tf_op jit(solution)/shard_map/ppermute | solution.py:80
  83.9 10.9 %collective-permute-start.29 = (bf16[640,128]{1,0:T(8,128)(2,1)S(1)}, bf16[640,128]{1,0:T(8,128)(2,1)S(1)}, u32[]{:S(2)}, u32[]{:S(2)}) collective-permute-start(bf16[640,128]{1,0:T(8,128)(2,1)S(1)} %copy-done.30), channel_id=1, source_target_pairs={{0,6},{1,7},{2,0},{3,1},{4,2},{5,3},{6,4},{7,5},{8,14},{9,15},{10,... | collective-permute-start | bytes 491528 | tf_op jit(solution)/shard_map/ppermute | solution.py:80
  94.4 6.3 %collective-permute-start.27 = (bf16[640,128]{1,0:T(8,128)(2,1)S(1)}, bf16[640,128]{1,0:T(8,128)(2,1)S(1)}, u32[]{:S(2)}, u32[]{:S(2)}) collective-permute-start(bf16[640,128]{1,0:T(8,128)(2,1)S(1)} %collective-permute-done.26), channel_id=1, source_target_pairs={{0,2},{1,3},{2,4},{3,5},{4,6},{5,7},{6,0},{7,1},{8,10},{9,11},{10,... | collective-permute-start | bytes 491528 | tf_op jit(solution)/shard_map/ppermute | solution.py:80
  94.8 5.9 %collective-permute-start.30 = (bf16[640,128]{1,0:T(8,128)(2,1)S(1)}, bf16[640,128]{1,0:T(8,128)(2,1)S(1)}, u32[]{:S(2)}, u32[]{:S(2)}) collective-permute-start(bf16[640,128]{1,0:T(8,128)(2,1)S(1)} %collective-permute-done.29), channel_id=1, source_target_pairs={{0,6},{1,7},{2,0},{3,1},{4,2},{5,3},{6,4},{7,5},{8,14},{9,15},{10,... | collective-permute-start | bytes 491528 | tf_op jit(solution)/shard_map/ppermute | solution.py:80
  97.3 5.0 %collective-permute-start.23 = (bf16[1280,128]{1,0:T(8,128)(2,1)S(1)}, bf16[1280,128]{1,0:T(8,128)(2,1)S(1)}, u32[]{:S(2)}, u32[]{:S(2)}) collective-permute-start(bf16[1280,128]{1,0:T(8,128)(2,1)S(1)} %collective-permute-done.22.refs_2_), channel_id=1, source_target_pairs={{0,1},{1,0},{2,3},{3,2},{4,5},{5,4},{6,7},{7,6},{8,9},{9,8},{10,11... | collective-permute-start | bytes 983048 | tf_op jit(solution)/shard_map/ppermute | solution.py:80
  97.3 5.0 %collective-permute-start.25 = (bf16[1280,128]{1,0:T(8,128)(2,1)S(1)}, bf16[1280,128]{1,0:T(8,128)(2,1)S(1)}, u32[]{:S(2)}, u32[]{:S(2)}) collective-permute-start(bf16[1280,128]{1,0:T(8,128)(2,1)S(1)} %collective-permute-done.24.refs_4_), channel_id=1, source_target_pairs={{0,1},{1,0},{2,3},{3,2},{4,5},{5,4},{6,7},{7,6},{8,9},{9,8},{10,11... | collective-permute-start | bytes 983048 | tf_op jit(solution)/shard_map/ppermute | solution.py:80
  97.9 3.4 %collective-permute-start.21 = (bf16[640,128]{1,0:T(8,128)(2,1)S(1)}, bf16[640,128]{1,0:T(8,128)(2,1)S(1)}, u32[]{:S(2)}, u32[]{:S(2)}) collective-permute-start(bf16[640,128]{1,0:T(8,128)(2,1)S(1)} %copy-done.29), channel_id=1, source_target_pairs={{0,1},{1,0},{2,3},{3,2},{4,5},{5,4},{6,7},{7,6},{8,9},{9,8},{10,11... | collective-permute-start | bytes 491528 | tf_op jit(solution)/shard_map/ppermute | solution.py:80
  100.7 1.4 %collective-permute-start.28 = (bf16[640,128]{1,0:T(8,128)(2,1)S(1)}, bf16[640,128]{1,0:T(8,128)(2,1)S(1)}, u32[]{:S(2)}, u32[]{:S(2)}) collective-permute-start(bf16[640,128]{1,0:T(8,128)(2,1)S(1)} %collective-permute-done.27.refs_6_), channel_id=1, source_target_pairs={{0,1},{1,0},{2,3},{3,2},{4,5},{5,4},{6,7},{7,6},{8,9},{9,8},{10,11... | collective-permute-start | bytes 491528 | tf_op jit(solution)/shard_map/ppermute | solution.py:80
  100.7 1.6 %collective-permute-start.31 = (bf16[640,128]{1,0:T(8,128)(2,1)S(1)}, bf16[640,128]{1,0:T(8,128)(2,1)S(1)}, u32[]{:S(2)}, u32[]{:S(2)}) collective-permute-start(bf16[640,128]{1,0:T(8,128)(2,1)S(1)} %collective-permute-done.30.refs_8_), channel_id=1, source_target_pairs={{0,1},{1,0},{2,3},{3,2},{4,5},{5,4},{6,7},{7,6},{8,9},{9,8},{10,11... | collective-permute-start | bytes 491528 | tf_op jit(solution)/shard_map/ppermute | solution.py:80
  109.1 22.3 %copy-start.4 = (bf16[128,1024]{1,0:T(8,128)(2,1)S(1)}, bf16[128,1024]{1,0:T(8,128)(2,1)}, u32[]{:S(2)}) copy-start(bf16[128,1024]{1,0:T(8,128)(2,1)} %hist.3) | copy-start | bytes 786436
  109.1 22.3 %copy-start.5 = (bf16[128,1024]{1,0:T(8,128)(2,1)S(1)}, bf16[128,1024]{1,0:T(8,128)(2,1)}, u32[]{:S(2)}) copy-start(bf16[128,1024]{1,0:T(8,128)(2,1)} %gout.3) | copy-start | bytes 786436
  109.1 22.3 %copy-start.11 = (s32[128]{0:T(128)S(1)}, s32[128]{0:T(128)}, u32[]{:S(2)}) copy-start(s32[128]{0:T(128)} %param.10) | copy-start | bytes 1540
  109.2 22.3 %all-to-all-start.1 = ((bf16[16,16,1024]{2,1,0:T(8,128)(2,1)}), bf16[16,16,1024]{2,1,0:T(8,128)(2,1)S(1)}, u32[]{:S(2)}, u32[]{:S(2)}) async-start(bf16[16,16,1024]{2,1,0:T(8,128)(2,1)} %bitcast.7), calls=%async_computation.1 | async-start | bytes 1048576 | tf_op jit(solution)/shard_map/all_to_all | solution.py:431
  118.4 11.0 %collective-permute-start.34 = (f32[16,512]{1,0:T(8,128)}, f32[16,512]{1,0:T(8,128)S(1)}, u32[]{:S(2)}, u32[]{:S(2)}) collective-permute-start(f32[16,512]{1,0:T(8,128)} %get-tuple-element.47), channel_id=1, source_target_pairs={{0,2},{1,3},{2,4},{3,5},{4,6},{5,7},{6,0},{7,1},{8,10},{9,11},{10,... | collective-permute-start | bytes 98312 | tf_op jit(solution)/shard_map/ppermute | solution.py:80
  120.7 10.0 %collective-permute-start.36 = (f32[16,512]{1,0:T(8,128)}, f32[16,512]{1,0:T(8,128)S(1)}, u32[]{:S(2)}, u32[]{:S(2)}) collective-permute-start(f32[16,512]{1,0:T(8,128)} %get-tuple-element.48), channel_id=1, source_target_pairs={{0,4},{1,5},{2,6},{3,7},{4,0},{5,1},{6,2},{7,3},{8,12},{9,13},{10,... | collective-permute-start | bytes 98312 | tf_op jit(solution)/shard_map/ppermute | solution.py:80
  123.6 7.2 %collective-permute-start.38 = (f32[16,512]{1,0:T(8,128)}, f32[16,512]{1,0:T(8,128)S(1)}, u32[]{:S(2)}, u32[]{:S(2)}) collective-permute-start(f32[16,512]{1,0:T(8,128)} %get-tuple-element.49), channel_id=1, source_target_pairs={{0,6},{1,7},{2,0},{3,1},{4,2},{5,3},{6,4},{7,5},{8,14},{9,15},{10,... | collective-permute-start | bytes 98312 | tf_op jit(solution)/shard_map/ppermute | solution.py:80
  126.1 12.0 %collective-permute-start.32 = (f32[8,1024]{1,0:T(8,128)}, f32[8,1024]{1,0:T(8,128)S(1)}, u32[]{:S(2)}, u32[]{:S(2)}) collective-permute-start(f32[8,1024]{1,0:T(8,128)} %get-tuple-element.44), channel_id=1, source_target_pairs={{0,0},{1,16},{2,32},{3,48},{4,64},{5,80},{6,96},{7,112},{8,1},{9,1... | collective-permute-start | bytes 98312 | tf_op jit(solution)/shard_map/ppermute | solution.py:517
  129.4 8.7 %collective-permute-start.35 = (f32[16,512]{1,0:T(8,128)S(1)}, f32[16,512]{1,0:T(8,128)S(1)}, u32[]{:S(2)}, u32[]{:S(2)}) collective-permute-start(f32[16,512]{1,0:T(8,128)S(1)} %collective-permute-done.34.refs_2_), channel_id=1, source_target_pairs={{0,1},{1,0},{2,3},{3,2},{4,5},{5,4},{6,7},{7,6},{8,9},{9,8},{10,11... | collective-permute-start | bytes 98312 | tf_op jit(solution)/shard_map/ppermute | solution.py:80
  130.8 7.3 %collective-permute-start.37 = (f32[16,512]{1,0:T(8,128)S(1)}, f32[16,512]{1,0:T(8,128)S(1)}, u32[]{:S(2)}, u32[]{:S(2)}) collective-permute-start(f32[16,512]{1,0:T(8,128)S(1)} %collective-permute-done.36.refs_4_), channel_id=1, source_target_pairs={{0,1},{1,0},{2,3},{3,2},{4,5},{5,4},{6,7},{7,6},{8,9},{9,8},{10,11... | collective-permute-start | bytes 98312 | tf_op jit(solution)/shard_map/ppermute | solution.py:80
  130.9 7.2 %collective-permute-start.39 = (f32[16,512]{1,0:T(8,128)S(1)}, f32[16,512]{1,0:T(8,128)S(1)}, u32[]{:S(2)}, u32[]{:S(2)}) collective-permute-start(f32[16,512]{1,0:T(8,128)S(1)} %collective-permute-done.38.refs_6_), channel_id=1, source_target_pairs={{0,1},{1,0},{2,3},{3,2},{4,5},{5,4},{6,7},{7,6},{8,9},{9,8},{10,11... | collective-permute-start | bytes 98312 | tf_op jit(solution)/shard_map/ppermute | solution.py:80
  131.3 1.4 collective-permute-start.33
  (11 other events, 12.6 us)

commit v5 on v4

--- a/solution.py
+++ b/solution.py
@@ -91,7 +91,7 @@
 
 
 def relay(own, other, near, far):
-    far = [send(send(far[0], 1, 0), 1, 0), send(send(far[1], 3, 0), 3, 0)]
+    far = [send(send(far[0], 1, 0), 1, 0), send(far[1], 2, 0)]
     near = [send(near[0], 1, 0), send(near[1], 3, 0)]
     got = [own, send(other, 0, 1)]
     for v in near + far:
@@ -434,7 +434,7 @@
 def local(history, grad_output, lengths, send_order, place_order, w_project, w_out):
     ctx_s = lax.axis_index("ctx").astype(jnp.int32).reshape(1)
     w_project, w_out = hbm(w_project), hbm(w_out)
-    order = send_order.reshape(1, R)
+    order = hbm(send_order.reshape(1, R))
     place = place_order.reshape(1, R)
 
     (packed,) = call(pack_kernel, [((2 * R, D), BF)], hbm(history), hbm(grad_output), order)

time: 140 us -> 141 us (level)
  the two profiles are of different devices: /device:TPU:98 before, /device:TPU:6 now
where the time goes in v5:
time: 141 us; the launch traced here: 139 us
  starting transfers between devices  57 us (40%)
  Pallas kernels  38 us (27%)
  waiting for transfers between devices  38 us (27%)
  local copies, waits for them, and re-layouts  4.79 us (3%)
    ppermute x38, waiting for transfers between devices, send(): return lax.ppermute(x, 'ctx', pairs)  31.8 us
    ppermute x38, starting transfers between devices, send(): return lax.ppermute(x, 'ctx', pairs)  31.6 us
    pallas_call x7, Pallas kernels, call(): pl.pallas_call(skip(body, len(args), len(late)), out_shape=[pltpu.HBM(s,...  25.8 us
    all_to_all x3, starting transfers between devices, across(): return lax.all_to_all(x, axis, split_axis=0, concat_axis=0, tiled=True)  18.6 us
    pallas_call x1, Pallas kernels, rows_back(): pl.pallas_call(rows_kernel, grid=(D // cols,), in_specs=[pl.BlockSpec(mem...  6.81 us
    ppermute x1, starting transfers between devices, local(): mixing = lax.ppermute(mixing, ('dp', 'ctx'), owners)  6.8 us
    all_to_all x3, waiting for transfers between devices, across(): return lax.all_to_all(x, axis, split_axis=0, concat_axis=0, tiled=True)  6.14 us
    unnamed x60, local copies, waits for them, and re-layouts  4.79 us
  transfers between devices with their start and end apart: 42, of which 15 were waited for; matrix products, arithmetic and copies ran while one was open for 0% of the time, Pallas kernels for 11%

profile of v5, /device:TPU:6, one launch (start us, length us, event | category | flops | bytes accessed | tf_op | source)
XLA Modules:
  0.0 138.7 jit_solution(16409729145089501678)
XLA Ops:
  0.6 2.4 %shard_map.104 = bf16[256,1024]{1,0:T(8,128)(2,1)} custom-call(bf16[128,1024]{1,0:T(8,128)(2,1)} %hist.3, bf16[128,1024]{1,0:T(8,128)(2,1)} %gout.3, s32[1,128]{1,0:T(1,128)} %bitcast.13), custom_call_target="tpu_custom_call" | custom-call | tf_op jit(solution)/shard_map/pallas_call | solution.py:59
  3.0 8.0 %all-to-all-start = ((bf16[16,16,1024]{2,1,0:T(8,128)(2,1)}), bf16[16,16,1024]{2,1,0:T(8,128)(2,1)S(1)}, u32[]{:S(2)}, u32[]{:S(2)}) async-start(bf16[16,16,1024]{2,1,0:T(8,128)(2,1)} %bitcast.12), calls=%async_computation | async-start | bytes 1048576 | tf_op jit(solution)/shard_map/all_to_all | solution.py:431
  11.1 1.7 %shard_map.103.refs_3_.w_out = bf16[128,1024]{1,0:T(8,128)(2,1)} custom-call(s32[1]{0:T(128)} %bitcast.ctx.refs_0_, bf16[1024,1024]{1,0:T(8,128)(2,1)} %w_out.1), custom_call_target="tpu_custom_call" | custom-call | tf_op jit(solution)/shard_map/pallas_call | solution.py:397
  12.7 3.7 %shard_map.102.refs_2_.wt = bf16[512,1024]{1,0:T(8,128)(2,1)} custom-call(s32[1]{0:T(128)} %bitcast.ctx.refs_0_, bf16[1024,4096]{1,0:T(8,128)(2,1)} %w.3), custom_call_target="tpu_custom_call" | custom-call | tf_op jit(solution)/shard_map/pallas_call | solution.py:383
  16.5 6.1 %all-to-all-done = bf16[16,16,1024]{2,1,0:T(8,128)(2,1)S(1)} async-done(((bf16[16,16,1024]{2,1,0:T(8,128)(2,1)}), bf16[16,16,1024]{2,1,0:T(8,128)(2,1)S(1)}, u32[]{:S(2)}, u32[]{:S(2)}) %all-to-all-start) | async-done | bytes 524320 | tf_op jit(solution)/shard_map/all_to_all | solution.py:431
  22.6 1.2 copy-done
  23.8 1.1 shard_map.105
  25.0 0.5 collective-permute-start.5
  25.4 1.5 %collective-permute-start.1 = (bf16[1024,128]{1,0:T(8,128)(2,1)}, bf16[1024,128]{1,0:T(8,128)(2,1)S(1)}, u32[]{:S(2)}, u32[]{:S(2)}) collective-permute-start(bf16[1024,128]{1,0:T(8,128)(2,1)} %get-tuple-element.28.refs_0_.refs_8_), channel_id=1, source_target_pairs={{0,6},{1,7},{2,0},{3,1},{4,2},{5,3},{6,4},{7,5},{8,14},{9,15},{10,... | collective-permute-start | bytes 786440 | tf_op jit(solution)/shard_map/ppermute | solution.py:80
  27.0 0.0 collective-permute-start
  27.0 1.7 %collective-permute-start.10 = (bf16[1024,128]{1,0:T(8,128)(2,1)}, bf16[1024,128]{1,0:T(8,128)(2,1)S(1)}, u32[]{:S(2)}, u32[]{:S(2)}) collective-permute-start(bf16[1024,128]{1,0:T(8,128)(2,1)} %get-tuple-element.29.refs_8_.refs_16_), channel_id=1, source_target_pairs={{0,2},{1,3},{2,4},{3,5},{4,6},{5,7},{6,0},{7,1},{8,10},{9,11},{10,... | collective-permute-start | bytes 786440 | tf_op jit(solution)/shard_map/ppermute | solution.py:80
  28.7 0.3 collective-permute-start.8
  29.0 4.4 %collective-permute-done.5.refs_6_.refs_14_ = bf16[1024,128]{1,0:T(8,128)(2,1)S(1)} collective-permute-done((bf16[1024,128]{1,0:T(8,128)(2,1)}, bf16[1024,128]{1,0:T(8,128)(2,1)S(1)}, u32[]{:S(2)}, u32[]{:S(2)}) %collective-permute-start.5) | collective-permute-done | bytes 262176 | tf_op jit(solution)/shard_map/ppermute | solution.py:80
  33.5 0.2 collective-permute-done.1.refs_2_.refs_10_
  33.7 0.3 collective-permute-start.6
  34.0 1.3 collective-permute-start.3
  35.3 2.2 %collective-permute-done.10.refs_14_.refs_22_ = bf16[1024,128]{1,0:T(8,128)(2,1)S(1)} collective-permute-done((bf16[1024,128]{1,0:T(8,128)(2,1)}, bf16[1024,128]{1,0:T(8,128)(2,1)S(1)}, u32[]{:S(2)}, u32[]{:S(2)}) %collective-permute-start.10) | collective-permute-done | bytes 262176 | tf_op jit(solution)/shard_map/ppermute | solution.py:80
  37.5 1.7 %collective-permute-start.11 = (bf16[1024,128]{1,0:T(8,128)(2,1)S(1)}, bf16[1024,128]{1,0:T(8,128)(2,1)S(1)}, u32[]{:S(2)}, u32[]{:S(2)}) collective-permute-start(bf16[1024,128]{1,0:T(8,128)(2,1)S(1)} %collective-permute-done.10.refs_14_.refs_22_), channel_id=1, source_target_pairs={{0,2},{1,3},{2,4},{3,5},{4,6},{5,7},{6,0},{7,1},{8,10},{9,11},{10,... | collective-permute-start | bytes 786440 | tf_op jit(solution)/shard_map/ppermute | solution.py:80
  39.2 0.1 collective-permute-done.8.refs_10_.refs_18_
  39.3 0.5 collective-permute-start.13
  39.8 0.1 collective-permute-start.9
  39.9 4.7 %collective-permute-done.3.refs_4_.refs_12_ = bf16[1024,128]{1,0:T(8,128)(2,1)S(1)} collective-permute-done((bf16[1024,128]{1,0:T(8,128)(2,1)S(1)}, bf16[1024,128]{1,0:T(8,128)(2,1)S(1)}, u32[]{:S(2)}, u32[]{:S(2)}) %collective-permute-start.3) | collective-permute-done | bytes 262176 | tf_op jit(solution)/shard_map/ppermute | solution.py:80
  44.6 0.2 collective-permute-done.11.refs_12_.refs_20_
  44.7 0.3 collective-permute-start.12
  45.1 1.0 collective-permute-done.4.refs_5_.refs_13_
  46.1 0.4 collective-permute-done.12.refs_13_.refs_21_
  46.6 0.2 copy-done.23
  46.8 0.7 copy-done.24
  47.5 8.1 %shard_map.106 = (bf16[512,1024]{1,0:T(8,128)(2,1)}, bf16[512,1024]{1,0:T(8,128)(2,1)}, f32[128,1024]{1,0:T(8,128)}, f32[128,1024]{1,0:T(8,128)}, f32[8,1024]{1,0:T(8,128)}) custom-call(s32[1,4]{1,0:T(1,128)S(1)} %copy-done.9, s32[1]{0:T(128)} %bitcast.ctx.refs_0_, bf16[512,1024]{1,0:T(8,128)(2,1)S(1)} %copy-done.1, bf16[128,1024]{1,0:T(8,128)(2,1)S(1)} %copy-done.3, ...), custom_call_target="tpu_custom_call" | custom-call | tf_op jit(solution)/shard_map/pallas_call | solution.py:59
  55.7 0.4 collective-permute-start.16
  56.1 3.0 %collective-permute-start.15 = (f32[8,1024]{1,0:T(8,128)}, f32[8,1024]{1,0:T(8,128)S(1)}, u32[]{:S(2)}, u32[]{:S(2)}) collective-permute-start(f32[8,1024]{1,0:T(8,128)} %get-tuple-element.34.refs_0_), channel_id=1, source_target_pairs={{0,2},{1,3},{2,4},{3,5},{4,6},{5,7},{6,0},{7,1},{8,10},{9,11},{10,... | collective-permute-start | bytes 98312 | tf_op jit(solution)/shard_map/ppermute | solution.py:80
  59.1 1.4 collective-permute-start.14
  60.5 0.6 collective-permute-done.16.refs_3_
  61.1 0.5 collective-permute-start.19
  61.6 3.1 %collective-permute-done.14.refs_1_ = f32[8,1024]{1,0:T(8,128)S(1)} collective-permute-done((f32[8,1024]{1,0:T(8,128)}, f32[8,1024]{1,0:T(8,128)S(1)}, u32[]{:S(2)}, u32[]{:S(2)}) %collective-permute-start.14) | collective-permute-done | bytes 32800 | tf_op jit(solution)/shard_map/ppermute | solution.py:80
  64.7 0.0 collective-permute-start.18
  64.7 1.2 collective-permute-done.18.refs_5_
  65.9 0.8 copy-done.7
  66.7 10.8 %shard_map.107 = (bf16[640,128]{1,0:T(8,128)(2,1)}, bf16[640,128]{1,0:T(8,128)(2,1)}, bf16[1280,128]{1,0:T(8,128)(2,1)}, bf16[1280,128]{1,0:T(8,128)(2,1)}, bf16...) custom-call(s32[1,4]{1,0:T(1,128)S(1)} %copy-done.9, s32[1]{0:T(128)} %bitcast.ctx.refs_0_, ...), custom_call_target="tpu_custom_call" | custom-call | tf_op jit(solution)/shard_map/pallas_call | solution.py:59
  77.5 3.8 %all-to-all-start.2 = ((bf16[16,80,512]{2,1,0:T(8,128)(2,1)}), bf16[16,80,512]{2,1,0:T(8,128)(2,1)S(1)}, u32[]{:S(2)}, u32[]{:S(2)}) async-start(bf16[16,80,512]{2,1,0:T(8,128)(2,1)} %get-tuple-element.43), calls=%async_computation.2 | async-start | bytes 2621440 | tf_op jit(solution)/shard_map/all_to_all | solution.py:431
  81.4 2.0 %collective-permute-start.22 = (bf16[1280,128]{1,0:T(8,128)(2,1)S(1)}, bf16[1280,128]{1,0:T(8,128)(2,1)S(1)}, u32[]{:S(2)}, u32[]{:S(2)}) collective-permute-start(bf16[1280,128]{1,0:T(8,128)(2,1)S(1)} %copy-done.26), channel_id=1, source_target_pairs={{0,2},{1,3},{2,4},{3,5},{4,6},{5,7},{6,0},{7,1},{8,10},{9,11},{10,... | collective-permute-start | bytes 983048 | tf_op jit(solution)/shard_map/ppermute | solution.py:80
  83.4 0.1 collective-permute-start.24
  83.5 3.2 %collective-permute-start.26 = (bf16[640,128]{1,0:T(8,128)(2,1)S(1)}, bf16[640,128]{1,0:T(8,128)(2,1)S(1)}, u32[]{:S(2)}, u32[]{:S(2)}) collective-permute-start(bf16[640,128]{1,0:T(8,128)(2,1)S(1)} %copy-done.29), channel_id=1, source_target_pairs={{0,2},{1,3},{2,4},{3,5},{4,6},{5,7},{6,0},{7,1},{8,10},{9,11},{10,... | collective-permute-start | bytes 491528 | tf_op jit(solution)/shard_map/ppermute | solution.py:80
  86.6 10.6 %collective-permute-done.26 = bf16[640,128]{1,0:T(8,128)(2,1)S(1)} collective-permute-done((bf16[640,128]{1,0:T(8,128)(2,1)S(1)}, bf16[640,128]{1,0:T(8,128)(2,1)S(1)}, u32[]{:S(2)}, u32[]{:S(2)}) %collective-permute-start.26) | collective-permute-done | bytes 163872 | tf_op jit(solution)/shard_map/ppermute | solution.py:80
  97.2 3.8 %collective-permute-start.27 = (bf16[640,128]{1,0:T(8,128)(2,1)S(1)}, bf16[640,128]{1,0:T(8,128)(2,1)S(1)}, u32[]{:S(2)}, u32[]{:S(2)}) collective-permute-start(bf16[640,128]{1,0:T(8,128)(2,1)S(1)} %collective-permute-done.26), channel_id=1, source_target_pairs={{0,2},{1,3},{2,4},{3,5},{4,6},{5,7},{6,0},{7,1},{8,10},{9,11},{10,... | collective-permute-start | bytes 491528 | tf_op jit(solution)/shard_map/ppermute | solution.py:80
  101.1 0.5 collective-permute-start.25
  101.6 0.1 collective-permute-start.21
  101.7 0.4 collective-permute-start.30
  102.1 1.8 %collective-permute-done.27.refs_6_ = bf16[640,128]{1,0:T(8,128)(2,1)S(1)} collective-permute-done((bf16[640,128]{1,0:T(8,128)(2,1)S(1)}, bf16[640,128]{1,0:T(8,128)(2,1)S(1)}, u32[]{:S(2)}, u32[]{:S(2)}) %collective-permute-start.27) | collective-permute-done | bytes 163872 | tf_op jit(solution)/shard_map/ppermute | solution.py:80
  103.9 1.4 collective-permute-done.28.refs_7_
  105.3 6.8 %shard_map.108.refs_2_ = bf16[256,1024]{1,0:T(8,128)(2,1)} custom-call(s32[1]{0:T(128)} %bitcast.ctx.refs_0_, s32[1,128]{1,0:T(1,128)S(1)} %bitcast.11, bf16[1024,4096]{1,0:T(8,128)(2,1)} %w.3, bf16[1024,1024]{1,0:T(8,128)(2,1)} %w_out.1, bf16[640,128]{1,0:T(8,128)(2,1)S(1)} %copy-done.6, bf16[640,128]{1,0:T(8,128)(2,1)S(1)} %collective-permute-done.21.refs_1_, ...), custom_call_target="tpu_custom_call" | custom-call | tf_op jit(solution)/shard_map/pallas_call | solution.py:413
  112.1 6.7 %all-to-all-start.1 = ((bf16[16,16,1024]{2,1,0:T(8,128)(2,1)}), bf16[16,16,1024]{2,1,0:T(8,128)(2,1)S(1)}, u32[]{:S(2)}, u32[]{:S(2)}) async-start(bf16[16,16,1024]{2,1,0:T(8,128)(2,1)} %bitcast.7), calls=%async_computation.1 | async-start | bytes 1048576 | tf_op jit(solution)/shard_map/all_to_all | solution.py:431
  118.8 1.1 copy-done.2
  119.9 0.8 shard_map.110
  120.7 3.7 %collective-permute-start.33 = (f32[16,512]{1,0:T(8,128)}, f32[16,512]{1,0:T(8,128)S(1)}, u32[]{:S(2)}, u32[]{:S(2)}) collective-permute-start(f32[16,512]{1,0:T(8,128)} %get-tuple-element.47), channel_id=1, source_target_pairs={{0,2},{1,3},{2,4},{3,5},{4,6},{5,7},{6,0},{7,1},{8,10},{9,11},{10,... | collective-permute-start | bytes 98312 | tf_op jit(solution)/shard_map/ppermute | solution.py:80
  124.4 0.9 collective-permute-start.37
  125.3 6.8 %collective-permute-start.31 = (f32[8,1024]{1,0:T(8,128)}, f32[8,1024]{1,0:T(8,128)S(1)}, u32[]{:S(2)}, u32[]{:S(2)}) collective-permute-start(f32[8,1024]{1,0:T(8,128)} %get-tuple-element.44), channel_id=1, source_target_pairs={{0,0},{1,16},{2,32},{3,48},{4,64},{5,80},{6,96},{7,112},{8,1},{9,1... | collective-permute-start | bytes 98312 | tf_op jit(solution)/shard_map/ppermute | solution.py:517
  132.1 2.6 %collective-permute-start.34 = (f32[16,512]{1,0:T(8,128)S(1)}, f32[16,512]{1,0:T(8,128)S(1)}, u32[]{:S(2)}, u32[]{:S(2)}) collective-permute-start(f32[16,512]{1,0:T(8,128)S(1)} %collective-permute-done.33.refs_2_), channel_id=1, source_target_pairs={{0,1},{1,0},{2,3},{3,2},{4,5},{5,4},{6,7},{7,6},{8,9},{9,8},{10,11... | collective-permute-start | bytes 98312 | tf_op jit(solution)/shard_map/ppermute | solution.py:80
  134.7 0.1 collective-permute-start.36
  134.8 0.4 collective-permute-start.38
  135.3 0.1 collective-permute-start.32
  135.4 1.9 %shard_map.109 = (bf16[128,1024]{1,0:T(8,128)(2,1)}, bf16[128,1024]{1,0:T(8,128)(2,1)}) custom-call(bf16[256,1024]{1,0:T(8,128)(2,1)S(1)} %bitcast.8, bf16[128,1024]{1,0:T(8,128)(2,1)S(1)} %copy-done.4, bf16[128,1024]{1,0:T(8,128)(2,1)S(1)} %copy-done.5, s32[1,128]{1,0:T(1,128)} %bitcast.14), custom_call_target="tpu_custom_call" | custom-call | tf_op jit(solution)/shard_map/pallas_call | solution.py:59
  137.3 0.7 copy-done.8
  138.0 0.7 shard_map.111
  (90 shorter events, 0.2 us)
Async XLA Ops:
  3.0 19.6 %all-to-all-start = ((bf16[16,16,1024]{2,1,0:T(8,128)(2,1)}), bf16[16,16,1024]{2,1,0:T(8,128)(2,1)S(1)}, u32[]{:S(2)}, u32[]{:S(2)}) async-start(bf16[16,16,1024]{2,1,0:T(8,128)(2,1)} %bitcast.12), calls=%async_computation | async-start | bytes 1048576 | tf_op jit(solution)/shard_map/all_to_all | solution.py:431
  12.7 9.9 %copy-start.3 = (bf16[128,1024]{1,0:T(8,128)(2,1)S(1)}, bf16[128,1024]{1,0:T(8,128)(2,1)}, u32[]{:S(2)}) copy-start(bf16[128,1024]{1,0:T(8,128)(2,1)} %shard_map.103.refs_3_.w_out) | copy-start | bytes 786436
  12.7 9.9 %copy-start.10 = (s32[128]{0:T(128)S(1)}, s32[128]{0:T(128)}, u32[]{:S(2)}) copy-start(s32[128]{0:T(128)} %param.11) | copy-start | bytes 1540
  12.7 34.8 %copy-start.9 = (s32[1,4]{1,0:T(1,128)S(1)}, s32[1,4]{1,0:T(1,128)}, u32[]{:S(2)}) copy-start(s32[1,4]{1,0:T(1,128)} %lengths.3) | copy-start | bytes 52
  23.8 23.7 %copy-start.1 = (bf16[512,1024]{1,0:T(8,128)(2,1)S(1)}, bf16[512,1024]{1,0:T(8,128)(2,1)}, u32[]{:S(2)}) copy-start(bf16[512,1024]{1,0:T(8,128)(2,1)} %shard_map.102.refs_2_.wt) | copy-start | bytes 3145732
  25.0 8.5 %collective-permute-start.5 = (bf16[1024,128]{1,0:T(8,128)(2,1)}, bf16[1024,128]{1,0:T(8,128)(2,1)S(1)}, u32[]{:S(2)}, u32[]{:S(2)}) collective-permute-start(bf16[1024,128]{1,0:T(8,128)(2,1)} %get-tuple-element.28.refs_0_.refs_8_), channel_id=1, source_target_pairs={{0,2},{1,3},{2,4},{3,5},{4,6},{5,7},{6,0},{7,1},{8,10},{9,11},{10,... | collective-permute-start | bytes 786440 | tf_op jit(solution)/shard_map/ppermute | solution.py:80
  25.4 8.2 %collective-permute-start.1 = (bf16[1024,128]{1,0:T(8,128)(2,1)}, bf16[1024,128]{1,0:T(8,128)(2,1)S(1)}, u32[]{:S(2)}, u32[]{:S(2)}) collective-permute-start(bf16[1024,128]{1,0:T(8,128)(2,1)} %get-tuple-element.28.refs_0_.refs_8_), channel_id=1, source_target_pairs={{0,6},{1,7},{2,0},{3,1},{4,2},{5,3},{6,4},{7,5},{8,14},{9,15},{10,... | collective-permute-start | bytes 786440 | tf_op jit(solution)/shard_map/ppermute | solution.py:80
  27.0 7.0 %collective-permute-start = (bf16[1024,128]{1,0:T(8,128)(2,1)}, bf16[1024,128]{1,0:T(8,128)(2,1)S(1)}, u32[]{:S(2)}, u32[]{:S(2)}) collective-permute-start(bf16[1024,128]{1,0:T(8,128)(2,1)} %get-tuple-element.28.refs_0_.refs_8_), channel_id=1, source_target_pairs={{0,1},{1,0},{2,3},{3,2},{4,5},{5,4},{6,7},{7,6},{8,9},{9,8},{10,11... | collective-permute-start | bytes 786440 | tf_op jit(solution)/shard_map/ppermute | solution.py:80
  27.0 10.5 %collective-permute-start.10 = (bf16[1024,128]{1,0:T(8,128)(2,1)}, bf16[1024,128]{1,0:T(8,128)(2,1)S(1)}, u32[]{:S(2)}, u32[]{:S(2)}) collective-permute-start(bf16[1024,128]{1,0:T(8,128)(2,1)} %get-tuple-element.29.refs_8_.refs_16_), channel_id=1, source_target_pairs={{0,2},{1,3},{2,4},{3,5},{4,6},{5,7},{6,0},{7,1},{8,10},{9,11},{10,... | collective-permute-start | bytes 786440 | tf_op jit(solution)/shard_map/ppermute | solution.py:80
  28.7 10.6 %collective-permute-start.8 = (bf16[1024,128]{1,0:T(8,128)(2,1)}, bf16[1024,128]{1,0:T(8,128)(2,1)S(1)}, u32[]{:S(2)}, u32[]{:S(2)}) collective-permute-start(bf16[1024,128]{1,0:T(8,128)(2,1)} %get-tuple-element.29.refs_8_.refs_16_), channel_id=1, source_target_pairs={{0,6},{1,7},{2,0},{3,1},{4,2},{5,3},{6,4},{7,5},{8,14},{9,15},{10,... | collective-permute-start | bytes 786440 | tf_op jit(solution)/shard_map/ppermute | solution.py:80
  33.5 13.0 %copy-start.11 = (bf16[1024,128]{1,0:T(8,128)(2,1)}, bf16[1024,128]{1,0:T(8,128)(2,1)S(1)}, u32[]{:S(2)}) copy-start(bf16[1024,128]{1,0:T(8,128)(2,1)S(1)} %collective-permute-done.5.refs_6_.refs_14_) | copy-start | bytes 786436
  33.5 5.8 %collective-permute-start.7 = (bf16[1024,128]{1,0:T(8,128)(2,1)}, bf16[1024,128]{1,0:T(8,128)(2,1)S(1)}, u32[]{:S(2)}, u32[]{:S(2)}) collective-permute-start(bf16[1024,128]{1,0:T(8,128)(2,1)} %get-tuple-element.29.refs_8_.refs_16_), channel_id=1, source_target_pairs={{0,1},{1,0},{2,3},{3,2},{4,5},{5,4},{6,7},{7,6},{8,9},{9,8},{10,11... | collective-permute-start | bytes 786440 | tf_op jit(solution)/shard_map/ppermute | solution.py:80
  33.7 12.8 %copy-start.12 = (bf16[1024,128]{1,0:T(8,128)(2,1)}, bf16[1024,128]{1,0:T(8,128)(2,1)S(1)}, u32[]{:S(2)}) copy-start(bf16[1024,128]{1,0:T(8,128)(2,1)S(1)} %collective-permute-done.1.refs_2_.refs_10_) | copy-start | bytes 786436
  33.7 6.1 %collective-permute-start.6 = (bf16[1024,128]{1,0:T(8,128)(2,1)S(1)}, bf16[1024,128]{1,0:T(8,128)(2,1)S(1)}, u32[]{:S(2)}, u32[]{:S(2)}) collective-permute-start(bf16[1024,128]{1,0:T(8,128)(2,1)S(1)} %collective-permute-done.5.refs_6_.refs_14_), channel_id=1, source_target_pairs={{0,1},{1,0},{2,3},{3,2},{4,5},{5,4},{6,7},{7,6},{8,9},{9,8},{10,11... | collective-permute-start | bytes 786440 | tf_op jit(solution)/shard_map/ppermute | solution.py:80
  34.0 12.5 %copy-start.13 = (bf16[1024,128]{1,0:T(8,128)(2,1)}, bf16[1024,128]{1,0:T(8,128)(2,1)S(1)}, u32[]{:S(2)}) copy-start(bf16[1024,128]{1,0:T(8,128)(2,1)S(1)} %collective-permute-done.refs_1_.refs_9_) | copy-start | bytes 786436
  34.0 10.6 %collective-permute-start.3 = (bf16[1024,128]{1,0:T(8,128)(2,1)S(1)}, bf16[1024,128]{1,0:T(8,128)(2,1)S(1)}, u32[]{:S(2)}, u32[]{:S(2)}) collective-permute-start(bf16[1024,128]{1,0:T(8,128)(2,1)S(1)} %collective-permute-done.1.refs_2_.refs_10_), channel_id=1, source_target_pairs={{0,6},{1,7},{2,0},{3,1},{4,2},{5,3},{6,4},{7,5},{8,14},{9,15},{10,... | collective-permute-start | bytes 786440 | tf_op jit(solution)/shard_map/ppermute | solution.py:80
  37.5 9.0 %copy-start.14 = (bf16[1024,128]{1,0:T(8,128)(2,1)}, bf16[1024,128]{1,0:T(8,128)(2,1)S(1)}, u32[]{:S(2)}) copy-start(bf16[1024,128]{1,0:T(8,128)(2,1)S(1)} %collective-permute-done.10.refs_14_.refs_22_) | copy-start | bytes 786436
  37.5 7.2 %collective-permute-start.11 = (bf16[1024,128]{1,0:T(8,128)(2,1)S(1)}, bf16[1024,128]{1,0:T(8,128)(2,1)S(1)}, u32[]{:S(2)}, u32[]{:S(2)}) collective-permute-start(bf16[1024,128]{1,0:T(8,128)(2,1)S(1)} %collective-permute-done.10.refs_14_.refs_22_), channel_id=1, source_target_pairs={{0,2},{1,3},{2,4},{3,5},{4,6},{5,7},{6,0},{7,1},{8,10},{9,11},{10,... | collective-permute-start | bytes 786440 | tf_op jit(solution)/shard_map/ppermute | solution.py:80
  39.3 7.2 %copy-start.15 = (bf16[1024,128]{1,0:T(8,128)(2,1)}, bf16[1024,128]{1,0:T(8,128)(2,1)S(1)}, u32[]{:S(2)}) copy-start(bf16[1024,128]{1,0:T(8,128)(2,1)S(1)} %collective-permute-done.8.refs_10_.refs_18_) | copy-start | bytes 786436
  39.3 5.8 %collective-permute-start.2 = (bf16[1024,128]{1,0:T(8,128)(2,1)S(1)}, bf16[1024,128]{1,0:T(8,128)(2,1)S(1)}, u32[]{:S(2)}, u32[]{:S(2)}) collective-permute-start(bf16[1024,128]{1,0:T(8,128)(2,1)S(1)} %collective-permute-done.1.refs_2_.refs_10_), channel_id=1, source_target_pairs={{0,1},{1,0},{2,3},{3,2},{4,5},{5,4},{6,7},{7,6},{8,9},{9,8},{10,11... | collective-permute-start | bytes 786440 | tf_op jit(solution)/shard_map/ppermute | solution.py:80
  39.3 7.2 %copy-start.16 = (bf16[1024,128]{1,0:T(8,128)(2,1)}, bf16[1024,128]{1,0:T(8,128)(2,1)S(1)}, u32[]{:S(2)}) copy-start(bf16[1024,128]{1,0:T(8,128)(2,1)S(1)} %collective-permute-done.7.refs_9_.refs_17_) | copy-start | bytes 786436
  39.3 5.8 %collective-permute-start.13 = (bf16[1024,128]{1,0:T(8,128)(2,1)S(1)}, bf16[1024,128]{1,0:T(8,128)(2,1)S(1)}, u32[]{:S(2)}, u32[]{:S(2)}) collective-permute-start(bf16[1024,128]{1,0:T(8,128)(2,1)S(1)} %collective-permute-done.10.refs_14_.refs_22_), channel_id=1, source_target_pairs={{0,1},{1,0},{2,3},{3,2},{4,5},{5,4},{6,7},{7,6},{8,9},{9,8},{10,11... | collective-permute-start | bytes 786440 | tf_op jit(solution)/shard_map/ppermute | solution.py:80
  39.8 6.7 %copy-start.17 = (bf16[1024,128]{1,0:T(8,128)(2,1)}, bf16[1024,128]{1,0:T(8,128)(2,1)S(1)}, u32[]{:S(2)}) copy-start(bf16[1024,128]{1,0:T(8,128)(2,1)S(1)} %collective-permute-done.6.refs_7_.refs_15_) | copy-start | bytes 786436
  39.8 5.3 %collective-permute-start.9 = (bf16[1024,128]{1,0:T(8,128)(2,1)S(1)}, bf16[1024,128]{1,0:T(8,128)(2,1)S(1)}, u32[]{:S(2)}, u32[]{:S(2)}) collective-permute-start(bf16[1024,128]{1,0:T(8,128)(2,1)S(1)} %collective-permute-done.8.refs_10_.refs_18_), channel_id=1, source_target_pairs={{0,1},{1,0},{2,3},{3,2},{4,5},{5,4},{6,7},{7,6},{8,9},{9,8},{10,11... | collective-permute-start | bytes 786440 | tf_op jit(solution)/shard_map/ppermute | solution.py:80
  44.6 2.0 %copy-start.18 = (bf16[1024,128]{1,0:T(8,128)(2,1)}, bf16[1024,128]{1,0:T(8,128)(2,1)S(1)}, u32[]{:S(2)}) copy-start(bf16[1024,128]{1,0:T(8,128)(2,1)S(1)} %collective-permute-done.3.refs_4_.refs_12_) | copy-start | bytes 786436
  44.6 1.5 %collective-permute-start.4 = (bf16[1024,128]{1,0:T(8,128)(2,1)S(1)}, bf16[1024,128]{1,0:T(8,128)(2,1)S(1)}, u32[]{:S(2)}, u32[]{:S(2)}) collective-permute-start(bf16[1024,128]{1,0:T(8,128)(2,1)S(1)} %collective-permute-done.3.refs_4_.refs_12_), channel_id=1, source_target_pairs={{0,1},{1,0},{2,3},{3,2},{4,5},{5,4},{6,7},{7,6},{8,9},{9,8},{10,11... | collective-permute-start | bytes 786440 | tf_op jit(solution)/shard_map/ppermute | solution.py:80
  44.7 1.8 %copy-start.19 = (bf16[1024,128]{1,0:T(8,128)(2,1)}, bf16[1024,128]{1,0:T(8,128)(2,1)S(1)}, u32[]{:S(2)}) copy-start(bf16[1024,128]{1,0:T(8,128)(2,1)S(1)} %collective-permute-done.11.refs_12_.refs_20_) | copy-start | bytes 786436
  44.7 1.7 %collective-permute-start.12 = (bf16[1024,128]{1,0:T(8,128)(2,1)S(1)}, bf16[1024,128]{1,0:T(8,128)(2,1)S(1)}, u32[]{:S(2)}, u32[]{:S(2)}) collective-permute-start(bf16[1024,128]{1,0:T(8,128)(2,1)S(1)} %collective-permute-done.11.refs_12_.refs_20_), channel_id=1, source_target_pairs={{0,1},{1,0},{2,3},{3,2},{4,5},{5,4},{6,7},{7,6},{8,9},{9,8},{10,11... | collective-permute-start | bytes 786440 | tf_op jit(solution)/shard_map/ppermute | solution.py:80
  45.1 1.5 %copy-start.21 = (bf16[1024,128]{1,0:T(8,128)(2,1)}, bf16[1024,128]{1,0:T(8,128)(2,1)S(1)}, u32[]{:S(2)}) copy-start(bf16[1024,128]{1,0:T(8,128)(2,1)S(1)} %collective-permute-done.13.refs_15_.refs_23_) | copy-start | bytes 786436
  55.7 5.4 %collective-permute-start.16 = (f32[8,1024]{1,0:T(8,128)}, f32[8,1024]{1,0:T(8,128)S(1)}, u32[]{:S(2)}, u32[]{:S(2)}) collective-permute-start(f32[8,1024]{1,0:T(8,128)} %get-tuple-element.34.refs_0_), channel_id=1, source_target_pairs={{0,6},{1,7},{2,0},{3,1},{4,2},{5,3},{6,4},{7,5},{8,14},{9,15},{10,... | collective-permute-start | bytes 98312 | tf_op jit(solution)/shard_map/ppermute | solution.py:80
  56.1 5.1 %collective-permute-start.15 = (f32[8,1024]{1,0:T(8,128)}, f32[8,1024]{1,0:T(8,128)S(1)}, u32[]{:S(2)}, u32[]{:S(2)}) collective-permute-start(f32[8,1024]{1,0:T(8,128)} %get-tuple-element.34.refs_0_), channel_id=1, source_target_pairs={{0,2},{1,3},{2,4},{3,5},{4,6},{5,7},{6,0},{7,1},{8,10},{9,11},{10,... | collective-permute-start | bytes 98312 | tf_op jit(solution)/shard_map/ppermute | solution.py:80
  59.1 5.6 %collective-permute-start.14 = (f32[8,1024]{1,0:T(8,128)}, f32[8,1024]{1,0:T(8,128)S(1)}, u32[]{:S(2)}, u32[]{:S(2)}) collective-permute-start(f32[8,1024]{1,0:T(8,128)} %get-tuple-element.34.refs_0_), channel_id=1, source_target_pairs={{0,4},{1,5},{2,6},{3,7},{4,0},{5,1},{6,2},{7,3},{8,12},{9,13},{10,... | collective-permute-start | bytes 98312 | tf_op jit(solution)/shard_map/ppermute | solution.py:80
  60.5 4.3 %collective-permute-start.17 = (f32[8,1024]{1,0:T(8,128)}, f32[8,1024]{1,0:T(8,128)S(1)}, u32[]{:S(2)}, u32[]{:S(2)}) collective-permute-start(f32[8,1024]{1,0:T(8,128)} %get-tuple-element.34.refs_0_), channel_id=1, source_target_pairs={{0,1},{1,0},{2,3},{3,2},{4,5},{5,4},{6,7},{7,6},{8,9},{9,8},{10,11... | collective-permute-start | bytes 98312 | tf_op jit(solution)/shard_map/ppermute | solution.py:80
  61.1 3.6 %collective-permute-start.20 = (f32[8,1024]{1,0:T(8,128)S(1)}, f32[8,1024]{1,0:T(8,128)S(1)}, u32[]{:S(2)}, u32[]{:S(2)}) collective-permute-start(f32[8,1024]{1,0:T(8,128)S(1)} %collective-permute-done.16.refs_3_), channel_id=1, source_target_pairs={{0,1},{1,0},{2,3},{3,2},{4,5},{5,4},{6,7},{7,6},{8,9},{9,8},{10,11... | collective-permute-start | bytes 98312 | tf_op jit(solution)/shard_map/ppermute | solution.py:80
  61.1 3.6 %collective-permute-start.19 = (f32[8,1024]{1,0:T(8,128)S(1)}, f32[8,1024]{1,0:T(8,128)S(1)}, u32[]{:S(2)}, u32[]{:S(2)}) collective-permute-start(f32[8,1024]{1,0:T(8,128)S(1)} %collective-permute-done.15.refs_2_), channel_id=1, source_target_pairs={{0,1},{1,0},{2,3},{3,2},{4,5},{5,4},{6,7},{7,6},{8,9},{9,8},{10,11... | collective-permute-start | bytes 98312 | tf_op jit(solution)/shard_map/ppermute | solution.py:80
  64.7 1.2 collective-permute-start.18
  77.4 3.9 %copy-start.26 = (bf16[1280,128]{1,0:T(8,128)(2,1)S(1)}, bf16[1280,128]{1,0:T(8,128)(2,1)}, u32[]{:S(2)}) copy-start(bf16[1280,128]{1,0:T(8,128)(2,1)} %get-tuple-element.37) | copy-start | bytes 983044
  77.5 5.9 %copy-start.25 = (bf16[1280,128]{1,0:T(8,128)(2,1)S(1)}, bf16[1280,128]{1,0:T(8,128)(2,1)}, u32[]{:S(2)}) copy-start(bf16[1280,128]{1,0:T(8,128)(2,1)} %get-tuple-element.38) | copy-start | bytes 983044
  77.5 6.0 %copy-start.29 = (bf16[640,128]{1,0:T(8,128)(2,1)S(1)}, bf16[640,128]{1,0:T(8,128)(2,1)}, u32[]{:S(2)}) copy-start(bf16[640,128]{1,0:T(8,128)(2,1)} %get-tuple-element.39) | copy-start | bytes 491524
  77.5 9.1 %copy-start.28 = (bf16[640,128]{1,0:T(8,128)(2,1)S(1)}, bf16[640,128]{1,0:T(8,128)(2,1)}, u32[]{:S(2)}) copy-start(bf16[640,128]{1,0:T(8,128)(2,1)} %get-tuple-element.40) | copy-start | bytes 491524
  77.5 24.1 %copy-start.27 = (bf16[640,128]{1,0:T(8,128)(2,1)S(1)}, bf16[640,128]{1,0:T(8,128)(2,1)}, u32[]{:S(2)}) copy-start(bf16[640,128]{1,0:T(8,128)(2,1)} %get-tuple-element.36) | copy-start | bytes 491524
  77.5 27.8 %copy-start.6 = (bf16[640,128]{1,0:T(8,128)(2,1)S(1)}, bf16[640,128]{1,0:T(8,128)(2,1)}, u32[]{:S(2)}) copy-start(bf16[640,128]{1,0:T(8,128)(2,1)} %get-tuple-element.35.refs_0_) | copy-start | bytes 491524
  77.5 34.6 %all-to-all-start.2 = ((bf16[16,80,512]{2,1,0:T(8,128)(2,1)}), bf16[16,80,512]{2,1,0:T(8,128)(2,1)S(1)}, u32[]{:S(2)}, u32[]{:S(2)}) async-start(bf16[16,80,512]{2,1,0:T(8,128)(2,1)} %get-tuple-element.43), calls=%async_computation.2 | async-start | bytes 2621440 | tf_op jit(solution)/shard_map/all_to_all | solution.py:431
  81.4 19.7 %collective-permute-start.22 = (bf16[1280,128]{1,0:T(8,128)(2,1)S(1)}, bf16[1280,128]{1,0:T(8,128)(2,1)S(1)}, u32[]{:S(2)}, u32[]{:S(2)}) collective-permute-start(bf16[1280,128]{1,0:T(8,128)(2,1)S(1)} %copy-done.26), channel_id=1, source_target_pairs={{0,2},{1,3},{2,4},{3,5},{4,6},{5,7},{6,0},{7,1},{8,10},{9,11},{10,... | collective-permute-start | bytes 983048 | tf_op jit(solution)/shard_map/ppermute | solution.py:80
  83.4 17.7 %collective-permute-start.24 = (bf16[1280,128]{1,0:T(8,128)(2,1)S(1)}, bf16[1280,128]{1,0:T(8,128)(2,1)S(1)}, u32[]{:S(2)}, u32[]{:S(2)}) collective-permute-start(bf16[1280,128]{1,0:T(8,128)(2,1)S(1)} %copy-done.25), channel_id=1, source_target_pairs={{0,6},{1,7},{2,0},{3,1},{4,2},{5,3},{6,4},{7,5},{8,14},{9,15},{10,... | collective-permute-start | bytes 983048 | tf_op jit(solution)/shard_map/ppermute | solution.py:80
  83.5 13.7 %collective-permute-start.26 = (bf16[640,128]{1,0:T(8,128)(2,1)S(1)}, bf16[640,128]{1,0:T(8,128)(2,1)S(1)}, u32[]{:S(2)}, u32[]{:S(2)}) collective-permute-start(bf16[640,128]{1,0:T(8,128)(2,1)S(1)} %copy-done.29), channel_id=1, source_target_pairs={{0,2},{1,3},{2,4},{3,5},{4,6},{5,7},{6,0},{7,1},{8,10},{9,11},{10,... | collective-permute-start | bytes 491528 | tf_op jit(solution)/shard_map/ppermute | solution.py:80
  86.6 15.0 %collective-permute-start.29 = (bf16[640,128]{1,0:T(8,128)(2,1)S(1)}, bf16[640,128]{1,0:T(8,128)(2,1)S(1)}, u32[]{:S(2)}, u32[]{:S(2)}) collective-permute-start(bf16[640,128]{1,0:T(8,128)(2,1)S(1)} %copy-done.28), channel_id=1, source_target_pairs={{0,4},{1,5},{2,6},{3,7},{4,0},{5,1},{6,2},{7,3},{8,12},{9,13},{10,... | collective-permute-start | bytes 491528 | tf_op jit(solution)/shard_map/ppermute | solution.py:80
  97.2 6.7 %collective-permute-start.27 = (bf16[640,128]{1,0:T(8,128)(2,1)S(1)}, bf16[640,128]{1,0:T(8,128)(2,1)S(1)}, u32[]{:S(2)}, u32[]{:S(2)}) collective-permute-start(bf16[640,128]{1,0:T(8,128)(2,1)S(1)} %collective-permute-done.26), channel_id=1, source_target_pairs={{0,2},{1,3},{2,4},{3,5},{4,6},{5,7},{6,0},{7,1},{8,10},{9,11},{10,... | collective-permute-start | bytes 491528 | tf_op jit(solution)/shard_map/ppermute | solution.py:80
  101.0 4.2 %collective-permute-start.23 = (bf16[1280,128]{1,0:T(8,128)(2,1)S(1)}, bf16[1280,128]{1,0:T(8,128)(2,1)S(1)}, u32[]{:S(2)}, u32[]{:S(2)}) collective-permute-start(bf16[1280,128]{1,0:T(8,128)(2,1)S(1)} %collective-permute-done.22.refs_2_), channel_id=1, source_target_pairs={{0,1},{1,0},{2,3},{3,2},{4,5},{5,4},{6,7},{7,6},{8,9},{9,8},{10,11... | collective-permute-start | bytes 983048 | tf_op jit(solution)/shard_map/ppermute | solution.py:80
  101.1 4.2 %collective-permute-start.25 = (bf16[1280,128]{1,0:T(8,128)(2,1)S(1)}, bf16[1280,128]{1,0:T(8,128)(2,1)S(1)}, u32[]{:S(2)}, u32[]{:S(2)}) collective-permute-start(bf16[1280,128]{1,0:T(8,128)(2,1)S(1)} %collective-permute-done.24.refs_4_), channel_id=1, source_target_pairs={{0,1},{1,0},{2,3},{3,2},{4,5},{5,4},{6,7},{7,6},{8,9},{9,8},{10,11... | collective-permute-start | bytes 983048 | tf_op jit(solution)/shard_map/ppermute | solution.py:80
  101.6 2.3 %collective-permute-start.21 = (bf16[640,128]{1,0:T(8,128)(2,1)S(1)}, bf16[640,128]{1,0:T(8,128)(2,1)S(1)}, u32[]{:S(2)}, u32[]{:S(2)}) collective-permute-start(bf16[640,128]{1,0:T(8,128)(2,1)S(1)} %copy-done.27), channel_id=1, source_target_pairs={{0,1},{1,0},{2,3},{3,2},{4,5},{5,4},{6,7},{7,6},{8,9},{9,8},{10,11... | collective-permute-start | bytes 491528 | tf_op jit(solution)/shard_map/ppermute | solution.py:80
  101.7 2.2 %collective-permute-start.30 = (bf16[640,128]{1,0:T(8,128)(2,1)S(1)}, bf16[640,128]{1,0:T(8,128)(2,1)S(1)}, u32[]{:S(2)}, u32[]{:S(2)}) collective-permute-start(bf16[640,128]{1,0:T(8,128)(2,1)S(1)} %collective-permute-done.29.refs_8_), channel_id=1, source_target_pairs={{0,1},{1,0},{2,3},{3,2},{4,5},{5,4},{6,7},{7,6},{8,9},{9,8},{10,11... | collective-permute-start | bytes 491528 | tf_op jit(solution)/shard_map/ppermute | solution.py:80
  103.9 1.4 %collective-permute-start.28 = (bf16[640,128]{1,0:T(8,128)(2,1)S(1)}, bf16[640,128]{1,0:T(8,128)(2,1)S(1)}, u32[]{:S(2)}, u32[]{:S(2)}) collective-permute-start(bf16[640,128]{1,0:T(8,128)(2,1)S(1)} %collective-permute-done.27.refs_6_), channel_id=1, source_target_pairs={{0,1},{1,0},{2,3},{3,2},{4,5},{5,4},{6,7},{7,6},{8,9},{9,8},{10,11... | collective-permute-start | bytes 491528 | tf_op jit(solution)/shard_map/ppermute | solution.py:80
  112.1 23.3 %copy-start.4 = (bf16[128,1024]{1,0:T(8,128)(2,1)S(1)}, bf16[128,1024]{1,0:T(8,128)(2,1)}, u32[]{:S(2)}) copy-start(bf16[128,1024]{1,0:T(8,128)(2,1)} %hist.3) | copy-start | bytes 786436
  112.1 23.3 %copy-start.5 = (bf16[128,1024]{1,0:T(8,128)(2,1)S(1)}, bf16[128,1024]{1,0:T(8,128)(2,1)}, u32[]{:S(2)}) copy-start(bf16[128,1024]{1,0:T(8,128)(2,1)} %gout.3) | copy-start | bytes 786436
  112.1 23.3 %all-to-all-start.1 = ((bf16[16,16,1024]{2,1,0:T(8,128)(2,1)}), bf16[16,16,1024]{2,1,0:T(8,128)(2,1)S(1)}, u32[]{:S(2)}, u32[]{:S(2)}) async-start(bf16[16,16,1024]{2,1,0:T(8,128)(2,1)} %bitcast.7), calls=%async_computation.1 | async-start | bytes 1048576 | tf_op jit(solution)/shard_map/all_to_all | solution.py:431
  120.7 11.4 %collective-permute-start.33 = (f32[16,512]{1,0:T(8,128)}, f32[16,512]{1,0:T(8,128)S(1)}, u32[]{:S(2)}, u32[]{:S(2)}) collective-permute-start(f32[16,512]{1,0:T(8,128)} %get-tuple-element.47), channel_id=1, source_target_pairs={{0,2},{1,3},{2,4},{3,5},{4,6},{5,7},{6,0},{7,1},{8,10},{9,11},{10,... | collective-permute-start | bytes 98312 | tf_op jit(solution)/shard_map/ppermute | solution.py:80
  124.4 10.3 %collective-permute-start.35 = (f32[16,512]{1,0:T(8,128)}, f32[16,512]{1,0:T(8,128)S(1)}, u32[]{:S(2)}, u32[]{:S(2)}) collective-permute-start(f32[16,512]{1,0:T(8,128)} %get-tuple-element.48), channel_id=1, source_target_pairs={{0,4},{1,5},{2,6},{3,7},{4,0},{5,1},{6,2},{7,3},{8,12},{9,13},{10,... | collective-permute-start | bytes 98312 | tf_op jit(solution)/shard_map/ppermute | solution.py:80
  124.4 10.4 %collective-permute-start.37 = (f32[16,512]{1,0:T(8,128)}, f32[16,512]{1,0:T(8,128)S(1)}, u32[]{:S(2)}, u32[]{:S(2)}) collective-permute-start(f32[16,512]{1,0:T(8,128)} %get-tuple-element.49), channel_id=1, source_target_pairs={{0,6},{1,7},{2,0},{3,1},{4,2},{5,3},{6,4},{7,5},{8,14},{9,15},{10,... | collective-permute-start | bytes 98312 | tf_op jit(solution)/shard_map/ppermute | solution.py:80
  125.3 12.0 %collective-permute-start.31 = (f32[8,1024]{1,0:T(8,128)}, f32[8,1024]{1,0:T(8,128)S(1)}, u32[]{:S(2)}, u32[]{:S(2)}) collective-permute-start(f32[8,1024]{1,0:T(8,128)} %get-tuple-element.44), channel_id=1, source_target_pairs={{0,0},{1,16},{2,32},{3,48},{4,64},{5,80},{6,96},{7,112},{8,1},{9,1... | collective-permute-start | bytes 98312 | tf_op jit(solution)/shard_map/ppermute | solution.py:517
  132.1 5.2 %collective-permute-start.34 = (f32[16,512]{1,0:T(8,128)S(1)}, f32[16,512]{1,0:T(8,128)S(1)}, u32[]{:S(2)}, u32[]{:S(2)}) collective-permute-start(f32[16,512]{1,0:T(8,128)S(1)} %collective-permute-done.33.refs_2_), channel_id=1, source_target_pairs={{0,1},{1,0},{2,3},{3,2},{4,5},{5,4},{6,7},{7,6},{8,9},{9,8},{10,11... | collective-permute-start | bytes 98312 | tf_op jit(solution)/shard_map/ppermute | solution.py:80
  134.7 2.6 %collective-permute-start.36 = (f32[16,512]{1,0:T(8,128)S(1)}, f32[16,512]{1,0:T(8,128)S(1)}, u32[]{:S(2)}, u32[]{:S(2)}) collective-permute-start(f32[16,512]{1,0:T(8,128)S(1)} %collective-permute-done.35.refs_4_), channel_id=1, source_target_pairs={{0,1},{1,0},{2,3},{3,2},{4,5},{5,4},{6,7},{7,6},{8,9},{9,8},{10,11... | collective-permute-start | bytes 98312 | tf_op jit(solution)/shard_map/ppermute | solution.py:80
  134.8 2.5 %collective-permute-start.38 = (f32[16,512]{1,0:T(8,128)S(1)}, f32[16,512]{1,0:T(8,128)S(1)}, u32[]{:S(2)}, u32[]{:S(2)}) collective-permute-start(f32[16,512]{1,0:T(8,128)S(1)} %collective-permute-done.37.refs_6_), channel_id=1, source_target_pairs={{0,1},{1,0},{2,3},{3,2},{4,5},{5,4},{6,7},{7,6},{8,9},{9,8},{10,11... | collective-permute-start | bytes 98312 | tf_op jit(solution)/shard_map/ppermute | solution.py:80
  135.3 2.0 %collective-permute-start.32 = (f32[8,512]{1,0:T(8,128)}, f32[8,512]{1,0:T(8,128)S(1)}, u32[]{:S(2)}, u32[]{:S(2)}) collective-permute-start(f32[8,512]{1,0:T(8,128)} %get-tuple-element.46), channel_id=1, source_target_pairs={{0,1},{1,0},{2,3},{3,2},{4,5},{5,4},{6,7},{7,6},{8,9},{9,8},{10,11... | collective-permute-start | bytes 49160 | tf_op jit(solution)/shard_map/ppermute | solution.py:80
  (8 other events, 8.1 us)

commit v6 on v5

--- a/solution.py
+++ b/solution.py
@@ -91,7 +91,7 @@
 
 
 def relay(own, other, near, far):
-    far = [send(send(far[0], 1, 0), 1, 0), send(far[1], 2, 0)]
+    far = [send(send(far[0], 1, 0), 1, 0), send(send(far[1], 3, 0), 3, 0)]
     near = [send(near[0], 1, 0), send(near[1], 3, 0)]
     got = [own, send(other, 0, 1)]
     for v in near + far:

time: 141 us -> 140 us (level)
  starting transfers between devices: 57 us -> 54 us
  waiting for transfers between devices: 38 us -> 39.5 us
    ppermute x38 -> x39, starting transfers between devices: 31.6 us -> 28 us  [send(): return lax.ppermute(x, 'ctx', pairs)]
    ppermute x38 -> x39, waiting for transfers between devices: 31.8 us -> 33.4 us  [send(): return lax.ppermute(x, 'ctx', pairs)]
  transfers between devices with their start and end apart: 42 -> 43, of which waited for: 15 -> 16; matrix products, arithmetic and copies ran while one was open for 0% -> 0% of each run, Pallas kernels for 11% -> 11%
where the time goes in v6:
time: 140 us; the launch traced here: 137 us
  starting transfers between devices  54 us (39%)
  waiting for transfers between devices  39.5 us (28%)
  Pallas kernels  38 us (27%)
  local copies, waits for them, and re-layouts  4.77 us (3%)
    ppermute x39, waiting for transfers between devices, send(): return lax.ppermute(x, 'ctx', pairs)  33.4 us
    ppermute x39, starting transfers between devices, send(): return lax.ppermute(x, 'ctx', pairs)  28 us
    pallas_call x7, Pallas kernels, call(): pl.pallas_call(skip(body, len(args), len(late)), out_shape=[pltpu.HBM(s,...  25.8 us
    all_to_all x3, starting transfers between devices, across(): return lax.all_to_all(x, axis, split_axis=0, concat_axis=0, tiled=True)  18.9 us
    ppermute x1, starting transfers between devices, local(): mixing = lax.ppermute(mixing, ('dp', 'ctx'), owners)  7.15 us
    pallas_call x1, Pallas kernels, rows_back(): pl.pallas_call(rows_kernel, grid=(D // cols,), in_specs=[pl.BlockSpec(mem...  6.8 us
    all_to_all x3, waiting for transfers between devices, across(): return lax.all_to_all(x, axis, split_axis=0, concat_axis=0, tiled=True)  6.16 us
    unnamed x60, local copies, waits for them, and re-layouts  4.77 us
  transfers between devices with their start and end apart: 43, of which 16 were waited for; matrix products, arithmetic and copies ran while one was open for 0% of the time, Pallas kernels for 11%

profile of v6, /device:TPU:6, one launch (start us, length us, event | category | flops | bytes accessed | tf_op | source)
XLA Modules:
  0.0 137.3 jit_solution(6334384910879699687)
XLA Ops:
  0.6 2.4 %shard_map.104 = bf16[256,1024]{1,0:T(8,128)(2,1)} custom-call(bf16[128,1024]{1,0:T(8,128)(2,1)} %hist.3, bf16[128,1024]{1,0:T(8,128)(2,1)} %gout.3, s32[1,128]{1,0:T(1,128)} %bitcast.13), custom_call_target="tpu_custom_call" | custom-call | tf_op jit(solution)/shard_map/pallas_call | solution.py:59
  3.0 8.0 %all-to-all-start = ((bf16[16,16,1024]{2,1,0:T(8,128)(2,1)}), bf16[16,16,1024]{2,1,0:T(8,128)(2,1)S(1)}, u32[]{:S(2)}, u32[]{:S(2)}) async-start(bf16[16,16,1024]{2,1,0:T(8,128)(2,1)} %bitcast.12), calls=%async_computation | async-start | bytes 1048576 | tf_op jit(solution)/shard_map/all_to_all | solution.py:431
  11.1 1.7 %shard_map.103.refs_3_.w_out = bf16[128,1024]{1,0:T(8,128)(2,1)} custom-call(s32[1]{0:T(128)} %bitcast.ctx.refs_0_, bf16[1024,1024]{1,0:T(8,128)(2,1)} %w_out.1), custom_call_target="tpu_custom_call" | custom-call | tf_op jit(solution)/shard_map/pallas_call | solution.py:397
  12.7 3.7 %shard_map.102.refs_2_.wt = bf16[512,1024]{1,0:T(8,128)(2,1)} custom-call(s32[1]{0:T(128)} %bitcast.ctx.refs_0_, bf16[1024,4096]{1,0:T(8,128)(2,1)} %w.3), custom_call_target="tpu_custom_call" | custom-call | tf_op jit(solution)/shard_map/pallas_call | solution.py:383
  16.4 6.2 %all-to-all-done = bf16[16,16,1024]{2,1,0:T(8,128)(2,1)S(1)} async-done(((bf16[16,16,1024]{2,1,0:T(8,128)(2,1)}), bf16[16,16,1024]{2,1,0:T(8,128)(2,1)S(1)}, u32[]{:S(2)}, u32[]{:S(2)}) %all-to-all-start) | async-done | bytes 524320 | tf_op jit(solution)/shard_map/all_to_all | solution.py:431
  22.6 1.2 copy-done
  23.8 1.1 shard_map.105
  25.0 0.5 collective-permute-start.5
  25.4 1.5 %collective-permute-start.1 = (bf16[1024,128]{1,0:T(8,128)(2,1)}, bf16[1024,128]{1,0:T(8,128)(2,1)S(1)}, u32[]{:S(2)}, u32[]{:S(2)}) collective-permute-start(bf16[1024,128]{1,0:T(8,128)(2,1)} %get-tuple-element.28.refs_0_.refs_8_), channel_id=1, source_target_pairs={{0,6},{1,7},{2,0},{3,1},{4,2},{5,3},{6,4},{7,5},{8,14},{9,15},{10,... | collective-permute-start | bytes 786440 | tf_op jit(solution)/shard_map/ppermute | solution.py:80
  27.0 1.7 %collective-permute-start.10 = (bf16[1024,128]{1,0:T(8,128)(2,1)}, bf16[1024,128]{1,0:T(8,128)(2,1)S(1)}, u32[]{:S(2)}, u32[]{:S(2)}) collective-permute-start(bf16[1024,128]{1,0:T(8,128)(2,1)} %get-tuple-element.29.refs_8_.refs_16_), channel_id=1, source_target_pairs={{0,2},{1,3},{2,4},{3,5},{4,6},{5,7},{6,0},{7,1},{8,10},{9,11},{10,... | collective-permute-start | bytes 786440 | tf_op jit(solution)/shard_map/ppermute | solution.py:80
  28.7 0.3 collective-permute-start.8
  29.0 4.4 %collective-permute-done.5.refs_6_.refs_14_ = bf16[1024,128]{1,0:T(8,128)(2,1)S(1)} collective-permute-done((bf16[1024,128]{1,0:T(8,128)(2,1)}, bf16[1024,128]{1,0:T(8,128)(2,1)S(1)}, u32[]{:S(2)}, u32[]{:S(2)}) %collective-permute-start.5) | collective-permute-done | bytes 262176 | tf_op jit(solution)/shard_map/ppermute | solution.py:80
  33.5 0.2 collective-permute-done.1.refs_2_.refs_10_
  33.7 0.3 collective-permute-start.6
  34.0 1.3 collective-permute-start.3
  35.3 2.2 %collective-permute-done.10.refs_14_.refs_22_ = bf16[1024,128]{1,0:T(8,128)(2,1)S(1)} collective-permute-done((bf16[1024,128]{1,0:T(8,128)(2,1)}, bf16[1024,128]{1,0:T(8,128)(2,1)S(1)}, u32[]{:S(2)}, u32[]{:S(2)}) %collective-permute-start.10) | collective-permute-done | bytes 262176 | tf_op jit(solution)/shard_map/ppermute | solution.py:80
  37.5 1.7 %collective-permute-start.11 = (bf16[1024,128]{1,0:T(8,128)(2,1)S(1)}, bf16[1024,128]{1,0:T(8,128)(2,1)S(1)}, u32[]{:S(2)}, u32[]{:S(2)}) collective-permute-start(bf16[1024,128]{1,0:T(8,128)(2,1)S(1)} %collective-permute-done.10.refs_14_.refs_22_), channel_id=1, source_target_pairs={{0,2},{1,3},{2,4},{3,5},{4,6},{5,7},{6,0},{7,1},{8,10},{9,11},{10,... | collective-permute-start | bytes 786440 | tf_op jit(solution)/shard_map/ppermute | solution.py:80
  39.2 0.1 collective-permute-done.8.refs_10_.refs_18_
  39.3 0.5 collective-permute-start.13
  39.8 0.1 collective-permute-start.9
  39.9 4.7 %collective-permute-done.3.refs_4_.refs_12_ = bf16[1024,128]{1,0:T(8,128)(2,1)S(1)} collective-permute-done((bf16[1024,128]{1,0:T(8,128)(2,1)S(1)}, bf16[1024,128]{1,0:T(8,128)(2,1)S(1)}, u32[]{:S(2)}, u32[]{:S(2)}) %collective-permute-start.3) | collective-permute-done | bytes 262176 | tf_op jit(solution)/shard_map/ppermute | solution.py:80
  44.6 0.2 collective-permute-done.11.refs_12_.refs_20_
  44.7 0.3 collective-permute-start.12
  45.1 1.0 collective-permute-done.4.refs_5_.refs_13_
  46.1 0.4 collective-permute-done.12.refs_13_.refs_21_
  46.6 0.2 copy-done.23
  46.8 0.7 copy-done.24
  47.5 8.1 %shard_map.106 = (bf16[512,1024]{1,0:T(8,128)(2,1)}, bf16[512,1024]{1,0:T(8,128)(2,1)}, f32[128,1024]{1,0:T(8,128)}, f32[128,1024]{1,0:T(8,128)}, f32[8,1024]{1,0:T(8,128)}) custom-call(s32[1,4]{1,0:T(1,128)S(1)} %copy-done.9, s32[1]{0:T(128)} %bitcast.ctx.refs_0_, bf16[512,1024]{1,0:T(8,128)(2,1)S(1)} %copy-done.1, bf16[128,1024]{1,0:T(8,128)(2,1)S(1)} %copy-done.3, ...), custom_call_target="tpu_custom_call" | custom-call | tf_op jit(solution)/shard_map/pallas_call | solution.py:59
  55.6 0.4 collective-permute-start.16
  56.1 3.0 %collective-permute-start.15 = (f32[8,1024]{1,0:T(8,128)}, f32[8,1024]{1,0:T(8,128)S(1)}, u32[]{:S(2)}, u32[]{:S(2)}) collective-permute-start(f32[8,1024]{1,0:T(8,128)} %get-tuple-element.34.refs_0_), channel_id=1, source_target_pairs={{0,2},{1,3},{2,4},{3,5},{4,6},{5,7},{6,0},{7,1},{8,10},{9,11},{10,... | collective-permute-start | bytes 98312 | tf_op jit(solution)/shard_map/ppermute | solution.py:80
  59.1 1.4 %collective-permute-start.14 = (f32[8,1024]{1,0:T(8,128)}, f32[8,1024]{1,0:T(8,128)S(1)}, u32[]{:S(2)}, u32[]{:S(2)}) collective-permute-start(f32[8,1024]{1,0:T(8,128)} %get-tuple-element.34.refs_0_), channel_id=1, source_target_pairs={{0,4},{1,5},{2,6},{3,7},{4,0},{5,1},{6,2},{7,3},{8,12},{9,13},{10,... | collective-permute-start | bytes 98312 | tf_op jit(solution)/shard_map/ppermute | solution.py:80
  60.5 0.6 collective-permute-done.16.refs_3_
  61.1 0.5 collective-permute-start.19
  61.6 3.1 %collective-permute-done.14.refs_1_ = f32[8,1024]{1,0:T(8,128)S(1)} collective-permute-done((f32[8,1024]{1,0:T(8,128)}, f32[8,1024]{1,0:T(8,128)S(1)}, u32[]{:S(2)}, u32[]{:S(2)}) %collective-permute-start.14) | collective-permute-done | bytes 32800 | tf_op jit(solution)/shard_map/ppermute | solution.py:80
  64.7 1.2 collective-permute-done.18.refs_5_
  65.9 0.8 copy-done.7
  66.7 10.8 %shard_map.107 = (bf16[640,128]{1,0:T(8,128)(2,1)}, bf16[640,128]{1,0:T(8,128)(2,1)}, bf16[1280,128]{1,0:T(8,128)(2,1)}, bf16[1280,128]{1,0:T(8,128)(2,1)}, bf16...) custom-call(s32[1,4]{1,0:T(1,128)S(1)} %copy-done.9, s32[1]{0:T(128)} %bitcast.ctx.refs_0_, ...), custom_call_target="tpu_custom_call" | custom-call | tf_op jit(solution)/shard_map/pallas_call | solution.py:59
  77.5 3.8 %all-to-all-start.2 = ((bf16[16,80,512]{2,1,0:T(8,128)(2,1)}), bf16[16,80,512]{2,1,0:T(8,128)(2,1)S(1)}, u32[]{:S(2)}, u32[]{:S(2)}) async-start(bf16[16,80,512]{2,1,0:T(8,128)(2,1)} %get-tuple-element.43), calls=%async_computation.2 | async-start | bytes 2621440 | tf_op jit(solution)/shard_map/all_to_all | solution.py:431
  81.4 2.0 %collective-permute-start.22 = (bf16[1280,128]{1,0:T(8,128)(2,1)S(1)}, bf16[1280,128]{1,0:T(8,128)(2,1)S(1)}, u32[]{:S(2)}, u32[]{:S(2)}) collective-permute-start(bf16[1280,128]{1,0:T(8,128)(2,1)S(1)} %copy-done.26), channel_id=1, source_target_pairs={{0,2},{1,3},{2,4},{3,5},{4,6},{5,7},{6,0},{7,1},{8,10},{9,11},{10,... | collective-permute-start | bytes 983048 | tf_op jit(solution)/shard_map/ppermute | solution.py:80
  83.4 0.1 collective-permute-start.24
  83.5 3.1 %collective-permute-start.26 = (bf16[640,128]{1,0:T(8,128)(2,1)S(1)}, bf16[640,128]{1,0:T(8,128)(2,1)S(1)}, u32[]{:S(2)}, u32[]{:S(2)}) collective-permute-start(bf16[640,128]{1,0:T(8,128)(2,1)S(1)} %copy-done.29), channel_id=1, source_target_pairs={{0,2},{1,3},{2,4},{3,5},{4,6},{5,7},{6,0},{7,1},{8,10},{9,11},{10,... | collective-permute-start | bytes 491528 | tf_op jit(solution)/shard_map/ppermute | solution.py:80
  86.6 8.1 %collective-permute-done.26 = bf16[640,128]{1,0:T(8,128)(2,1)S(1)} collective-permute-done((bf16[640,128]{1,0:T(8,128)(2,1)S(1)}, bf16[640,128]{1,0:T(8,128)(2,1)S(1)}, u32[]{:S(2)}, u32[]{:S(2)}) %collective-permute-start.26) | collective-permute-done | bytes 163872 | tf_op jit(solution)/shard_map/ppermute | solution.py:80
  94.7 3.2 %collective-permute-start.27 = (bf16[640,128]{1,0:T(8,128)(2,1)S(1)}, bf16[640,128]{1,0:T(8,128)(2,1)S(1)}, u32[]{:S(2)}, u32[]{:S(2)}) collective-permute-start(bf16[640,128]{1,0:T(8,128)(2,1)S(1)} %collective-permute-done.26), channel_id=1, source_target_pairs={{0,2},{1,3},{2,4},{3,5},{4,6},{5,7},{6,0},{7,1},{8,10},{9,11},{10,... | collective-permute-start | bytes 491528 | tf_op jit(solution)/shard_map/ppermute | solution.py:80
  97.9 0.1 collective-permute-start.23
  98.0 0.5 collective-permute-start.25
  98.5 0.1 collective-permute-start.21
  98.6 2.2 %collective-permute-done.27.refs_6_ = bf16[640,128]{1,0:T(8,128)(2,1)S(1)} collective-permute-done((bf16[640,128]{1,0:T(8,128)(2,1)S(1)}, bf16[640,128]{1,0:T(8,128)(2,1)S(1)}, u32[]{:S(2)}, u32[]{:S(2)}) %collective-permute-start.27) | collective-permute-done | bytes 163872 | tf_op jit(solution)/shard_map/ppermute | solution.py:80
  100.8 3.6 %collective-permute-done.30.refs_8_ = bf16[640,128]{1,0:T(8,128)(2,1)S(1)} collective-permute-done((bf16[640,128]{1,0:T(8,128)(2,1)S(1)}, bf16[640,128]{1,0:T(8,128)(2,1)S(1)}, u32[]{:S(2)}, u32[]{:S(2)}) %collective-permute-start.30) | collective-permute-done | bytes 163872 | tf_op jit(solution)/shard_map/ppermute | solution.py:80
  104.4 1.4 %collective-permute-done.31.refs_9_ = bf16[640,128]{1,0:T(8,128)(2,1)S(1)} collective-permute-done((bf16[640,128]{1,0:T(8,128)(2,1)S(1)}, bf16[640,128]{1,0:T(8,128)(2,1)S(1)}, u32[]{:S(2)}, u32[]{:S(2)}) %collective-permute-start.31) | collective-permute-done | bytes 163872 | tf_op jit(solution)/shard_map/ppermute | solution.py:80
  105.8 6.8 %shard_map.108.refs_2_ = bf16[256,1024]{1,0:T(8,128)(2,1)} custom-call(s32[1]{0:T(128)} %bitcast.ctx.refs_0_, s32[1,128]{1,0:T(1,128)S(1)} %bitcast.11, bf16[1024,4096]{1,0:T(8,128)(2,1)} %w.3, bf16[1024,1024]{1,0:T(8,128)(2,1)} %w_out.1, bf16[640,128]{1,0:T(8,128)(2,1)S(1)} %copy-done.6, bf16[640,128]{1,0:T(8,128)(2,1)S(1)} %collective-permute-done.21.refs_1_, ...), custom_call_target="tpu_custom_call" | custom-call | tf_op jit(solution)/shard_map/pallas_call | solution.py:413
  112.6 7.0 %all-to-all-start.1 = ((bf16[16,16,1024]{2,1,0:T(8,128)(2,1)}), bf16[16,16,1024]{2,1,0:T(8,128)(2,1)S(1)}, u32[]{:S(2)}, u32[]{:S(2)}) async-start(bf16[16,16,1024]{2,1,0:T(8,128)(2,1)} %bitcast.7), calls=%async_computation.1 | async-start | bytes 1048576 | tf_op jit(solution)/shard_map/all_to_all | solution.py:431
  119.7 1.1 copy-done.2
  120.7 0.8 shard_map.110
  121.6 0.2 collective-permute-start.34
  121.8 0.6 collective-permute-start.36
  122.4 1.2 collective-permute-start.38
  123.6 7.1 %collective-permute-start.32 = (f32[8,1024]{1,0:T(8,128)}, f32[8,1024]{1,0:T(8,128)S(1)}, u32[]{:S(2)}, u32[]{:S(2)}) collective-permute-start(f32[8,1024]{1,0:T(8,128)} %get-tuple-element.44), channel_id=1, source_target_pairs={{0,0},{1,16},{2,32},{3,48},{4,64},{5,80},{6,96},{7,112},{8,1},{9,1... | collective-permute-start | bytes 98312 | tf_op jit(solution)/shard_map/ppermute | solution.py:517
  130.8 2.6 %collective-permute-start.35 = (f32[16,512]{1,0:T(8,128)S(1)}, f32[16,512]{1,0:T(8,128)S(1)}, u32[]{:S(2)}, u32[]{:S(2)}) collective-permute-start(f32[16,512]{1,0:T(8,128)S(1)} %collective-permute-done.34.refs_2_), channel_id=1, source_target_pairs={{0,1},{1,0},{2,3},{3,2},{4,5},{5,4},{6,7},{7,6},{8,9},{9,8},{10,11... | collective-permute-start | bytes 98312 | tf_op jit(solution)/shard_map/ppermute | solution.py:80
  133.4 0.1 collective-permute-start.37
  133.5 0.4 collective-permute-start.39
  133.9 0.1 collective-permute-start.33
  134.0 1.9 %shard_map.109 = (bf16[128,1024]{1,0:T(8,128)(2,1)}, bf16[128,1024]{1,0:T(8,128)(2,1)}) custom-call(bf16[256,1024]{1,0:T(8,128)(2,1)S(1)} %bitcast.8, bf16[128,1024]{1,0:T(8,128)(2,1)S(1)} %copy-done.4, bf16[128,1024]{1,0:T(8,128)(2,1)S(1)} %copy-done.5, s32[1,128]{1,0:T(1,128)} %bitcast.14), custom_call_target="tpu_custom_call" | custom-call | tf_op jit(solution)/shard_map/pallas_call | solution.py:59
  135.9 0.7 copy-done.8
  136.7 0.7 shard_map.111
  (92 shorter events, 0.2 us)
Async XLA Ops:
  3.0 19.6 %all-to-all-start = ((bf16[16,16,1024]{2,1,0:T(8,128)(2,1)}), bf16[16,16,1024]{2,1,0:T(8,128)(2,1)S(1)}, u32[]{:S(2)}, u32[]{:S(2)}) async-start(bf16[16,16,1024]{2,1,0:T(8,128)(2,1)} %bitcast.12), calls=%async_computation | async-start | bytes 1048576 | tf_op jit(solution)/shard_map/all_to_all | solution.py:431
  12.7 9.9 %copy-start.3 = (bf16[128,1024]{1,0:T(8,128)(2,1)S(1)}, bf16[128,1024]{1,0:T(8,128)(2,1)}, u32[]{:S(2)}) copy-start(bf16[128,1024]{1,0:T(8,128)(2,1)} %shard_map.103.refs_3_.w_out) | copy-start | bytes 786436
  12.7 9.9 %copy-start.10 = (s32[128]{0:T(128)S(1)}, s32[128]{0:T(128)}, u32[]{:S(2)}) copy-start(s32[128]{0:T(128)} %param.11) | copy-start | bytes 1540
  12.7 34.8 %copy-start.9 = (s32[1,4]{1,0:T(1,128)S(1)}, s32[1,4]{1,0:T(1,128)}, u32[]{:S(2)}) copy-start(s32[1,4]{1,0:T(1,128)} %lengths.3) | copy-start | bytes 52
  23.8 23.7 %copy-start.1 = (bf16[512,1024]{1,0:T(8,128)(2,1)S(1)}, bf16[512,1024]{1,0:T(8,128)(2,1)}, u32[]{:S(2)}) copy-start(bf16[512,1024]{1,0:T(8,128)(2,1)} %shard_map.102.refs_2_.wt) | copy-start | bytes 3145732
  25.0 8.5 %collective-permute-start.5 = (bf16[1024,128]{1,0:T(8,128)(2,1)}, bf16[1024,128]{1,0:T(8,128)(2,1)S(1)}, u32[]{:S(2)}, u32[]{:S(2)}) collective-permute-start(bf16[1024,128]{1,0:T(8,128)(2,1)} %get-tuple-element.28.refs_0_.refs_8_), channel_id=1, source_target_pairs={{0,2},{1,3},{2,4},{3,5},{4,6},{5,7},{6,0},{7,1},{8,10},{9,11},{10,... | collective-permute-start | bytes 786440 | tf_op jit(solution)/shard_map/ppermute | solution.py:80
  25.4 8.2 %collective-permute-start.1 = (bf16[1024,128]{1,0:T(8,128)(2,1)}, bf16[1024,128]{1,0:T(8,128)(2,1)S(1)}, u32[]{:S(2)}, u32[]{:S(2)}) collective-permute-start(bf16[1024,128]{1,0:T(8,128)(2,1)} %get-tuple-element.28.refs_0_.refs_8_), channel_id=1, source_target_pairs={{0,6},{1,7},{2,0},{3,1},{4,2},{5,3},{6,4},{7,5},{8,14},{9,15},{10,... | collective-permute-start | bytes 786440 | tf_op jit(solution)/shard_map/ppermute | solution.py:80
  27.0 7.0 %collective-permute-start = (bf16[1024,128]{1,0:T(8,128)(2,1)}, bf16[1024,128]{1,0:T(8,128)(2,1)S(1)}, u32[]{:S(2)}, u32[]{:S(2)}) collective-permute-start(bf16[1024,128]{1,0:T(8,128)(2,1)} %get-tuple-element.28.refs_0_.refs_8_), channel_id=1, source_target_pairs={{0,1},{1,0},{2,3},{3,2},{4,5},{5,4},{6,7},{7,6},{8,9},{9,8},{10,11... | collective-permute-start | bytes 786440 | tf_op jit(solution)/shard_map/ppermute | solution.py:80
  27.0 10.5 %collective-permute-start.10 = (bf16[1024,128]{1,0:T(8,128)(2,1)}, bf16[1024,128]{1,0:T(8,128)(2,1)S(1)}, u32[]{:S(2)}, u32[]{:S(2)}) collective-permute-start(bf16[1024,128]{1,0:T(8,128)(2,1)} %get-tuple-element.29.refs_8_.refs_16_), channel_id=1, source_target_pairs={{0,2},{1,3},{2,4},{3,5},{4,6},{5,7},{6,0},{7,1},{8,10},{9,11},{10,... | collective-permute-start | bytes 786440 | tf_op jit(solution)/shard_map/ppermute | solution.py:80
  28.7 10.6 %collective-permute-start.8 = (bf16[1024,128]{1,0:T(8,128)(2,1)}, bf16[1024,128]{1,0:T(8,128)(2,1)S(1)}, u32[]{:S(2)}, u32[]{:S(2)}) collective-permute-start(bf16[1024,128]{1,0:T(8,128)(2,1)} %get-tuple-element.29.refs_8_.refs_16_), channel_id=1, source_target_pairs={{0,6},{1,7},{2,0},{3,1},{4,2},{5,3},{6,4},{7,5},{8,14},{9,15},{10,... | collective-permute-start | bytes 786440 | tf_op jit(solution)/shard_map/ppermute | solution.py:80
  33.5 13.0 %copy-start.11 = (bf16[1024,128]{1,0:T(8,128)(2,1)}, bf16[1024,128]{1,0:T(8,128)(2,1)S(1)}, u32[]{:S(2)}) copy-start(bf16[1024,128]{1,0:T(8,128)(2,1)S(1)} %collective-permute-done.5.refs_6_.refs_14_) | copy-start | bytes 786436
  33.5 5.8 %collective-permute-start.7 = (bf16[1024,128]{1,0:T(8,128)(2,1)}, bf16[1024,128]{1,0:T(8,128)(2,1)S(1)}, u32[]{:S(2)}, u32[]{:S(2)}) collective-permute-start(bf16[1024,128]{1,0:T(8,128)(2,1)} %get-tuple-element.29.refs_8_.refs_16_), channel_id=1, source_target_pairs={{0,1},{1,0},{2,3},{3,2},{4,5},{5,4},{6,7},{7,6},{8,9},{9,8},{10,11... | collective-permute-start | bytes 786440 | tf_op jit(solution)/shard_map/ppermute | solution.py:80
  33.7 12.8 %copy-start.12 = (bf16[1024,128]{1,0:T(8,128)(2,1)}, bf16[1024,128]{1,0:T(8,128)(2,1)S(1)}, u32[]{:S(2)}) copy-start(bf16[1024,128]{1,0:T(8,128)(2,1)S(1)} %collective-permute-done.1.refs_2_.refs_10_) | copy-start | bytes 786436
  33.7 6.1 %collective-permute-start.6 = (bf16[1024,128]{1,0:T(8,128)(2,1)S(1)}, bf16[1024,128]{1,0:T(8,128)(2,1)S(1)}, u32[]{:S(2)}, u32[]{:S(2)}) collective-permute-start(bf16[1024,128]{1,0:T(8,128)(2,1)S(1)} %collective-permute-done.5.refs_6_.refs_14_), channel_id=1, source_target_pairs={{0,1},{1,0},{2,3},{3,2},{4,5},{5,4},{6,7},{7,6},{8,9},{9,8},{10,11... | collective-permute-start | bytes 786440 | tf_op jit(solution)/shard_map/ppermute | solution.py:80
  34.0 12.5 %copy-start.13 = (bf16[1024,128]{1,0:T(8,128)(2,1)}, bf16[1024,128]{1,0:T(8,128)(2,1)S(1)}, u32[]{:S(2)}) copy-start(bf16[1024,128]{1,0:T(8,128)(2,1)S(1)} %collective-permute-done.refs_1_.refs_9_) | copy-start | bytes 786436
  34.0 10.6 %collective-permute-start.3 = (bf16[1024,128]{1,0:T(8,128)(2,1)S(1)}, bf16[1024,128]{1,0:T(8,128)(2,1)S(1)}, u32[]{:S(2)}, u32[]{:S(2)}) collective-permute-start(bf16[1024,128]{1,0:T(8,128)(2,1)S(1)} %collective-permute-done.1.refs_2_.refs_10_), channel_id=1, source_target_pairs={{0,6},{1,7},{2,0},{3,1},{4,2},{5,3},{6,4},{7,5},{8,14},{9,15},{10,... | collective-permute-start | bytes 786440 | tf_op jit(solution)/shard_map/ppermute | solution.py:80
  37.5 9.0 %copy-start.14 = (bf16[1024,128]{1,0:T(8,128)(2,1)}, bf16[1024,128]{1,0:T(8,128)(2,1)S(1)}, u32[]{:S(2)}) copy-start(bf16[1024,128]{1,0:T(8,128)(2,1)S(1)} %collective-permute-done.10.refs_14_.refs_22_) | copy-start | bytes 786436
  37.5 7.2 %collective-permute-start.11 = (bf16[1024,128]{1,0:T(8,128)(2,1)S(1)}, bf16[1024,128]{1,0:T(8,128)(2,1)S(1)}, u32[]{:S(2)}, u32[]{:S(2)}) collective-permute-start(bf16[1024,128]{1,0:T(8,128)(2,1)S(1)} %collective-permute-done.10.refs_14_.refs_22_), channel_id=1, source_target_pairs={{0,2},{1,3},{2,4},{3,5},{4,6},{5,7},{6,0},{7,1},{8,10},{9,11},{10,... | collective-permute-start | bytes 786440 | tf_op jit(solution)/shard_map/ppermute | solution.py:80
  39.3 7.2 %copy-start.15 = (bf16[1024,128]{1,0:T(8,128)(2,1)}, bf16[1024,128]{1,0:T(8,128)(2,1)S(1)}, u32[]{:S(2)}) copy-start(bf16[1024,128]{1,0:T(8,128)(2,1)S(1)} %collective-permute-done.8.refs_10_.refs_18_) | copy-start | bytes 786436
  39.3 5.8 %collective-permute-start.2 = (bf16[1024,128]{1,0:T(8,128)(2,1)S(1)}, bf16[1024,128]{1,0:T(8,128)(2,1)S(1)}, u32[]{:S(2)}, u32[]{:S(2)}) collective-permute-start(bf16[1024,128]{1,0:T(8,128)(2,1)S(1)} %collective-permute-done.1.refs_2_.refs_10_), channel_id=1, source_target_pairs={{0,1},{1,0},{2,3},{3,2},{4,5},{5,4},{6,7},{7,6},{8,9},{9,8},{10,11... | collective-permute-start | bytes 786440 | tf_op jit(solution)/shard_map/ppermute | solution.py:80
  39.3 7.2 %copy-start.16 = (bf16[1024,128]{1,0:T(8,128)(2,1)}, bf16[1024,128]{1,0:T(8,128)(2,1)S(1)}, u32[]{:S(2)}) copy-start(bf16[1024,128]{1,0:T(8,128)(2,1)S(1)} %collective-permute-done.7.refs_9_.refs_17_) | copy-start | bytes 786436
  39.3 5.8 %collective-permute-start.13 = (bf16[1024,128]{1,0:T(8,128)(2,1)S(1)}, bf16[1024,128]{1,0:T(8,128)(2,1)S(1)}, u32[]{:S(2)}, u32[]{:S(2)}) collective-permute-start(bf16[1024,128]{1,0:T(8,128)(2,1)S(1)} %collective-permute-done.10.refs_14_.refs_22_), channel_id=1, source_target_pairs={{0,1},{1,0},{2,3},{3,2},{4,5},{5,4},{6,7},{7,6},{8,9},{9,8},{10,11... | collective-permute-start | bytes 786440 | tf_op jit(solution)/shard_map/ppermute | solution.py:80
  39.8 6.7 %copy-start.17 = (bf16[1024,128]{1,0:T(8,128)(2,1)}, bf16[1024,128]{1,0:T(8,128)(2,1)S(1)}, u32[]{:S(2)}) copy-start(bf16[1024,128]{1,0:T(8,128)(2,1)S(1)} %collective-permute-done.6.refs_7_.refs_15_) | copy-start | bytes 786436
  39.8 5.3 %collective-permute-start.9 = (bf16[1024,128]{1,0:T(8,128)(2,1)S(1)}, bf16[1024,128]{1,0:T(8,128)(2,1)S(1)}, u32[]{:S(2)}, u32[]{:S(2)}) collective-permute-start(bf16[1024,128]{1,0:T(8,128)(2,1)S(1)} %collective-permute-done.8.refs_10_.refs_18_), channel_id=1, source_target_pairs={{0,1},{1,0},{2,3},{3,2},{4,5},{5,4},{6,7},{7,6},{8,9},{9,8},{10,11... | collective-permute-start | bytes 786440 | tf_op jit(solution)/shard_map/ppermute | solution.py:80
  44.6 2.0 %copy-start.18 = (bf16[1024,128]{1,0:T(8,128)(2,1)}, bf16[1024,128]{1,0:T(8,128)(2,1)S(1)}, u32[]{:S(2)}) copy-start(bf16[1024,128]{1,0:T(8,128)(2,1)S(1)} %collective-permute-done.3.refs_4_.refs_12_) | copy-start | bytes 786436
  44.6 1.5 %collective-permute-start.4 = (bf16[1024,128]{1,0:T(8,128)(2,1)S(1)}, bf16[1024,128]{1,0:T(8,128)(2,1)S(1)}, u32[]{:S(2)}, u32[]{:S(2)}) collective-permute-start(bf16[1024,128]{1,0:T(8,128)(2,1)S(1)} %collective-permute-done.3.refs_4_.refs_12_), channel_id=1, source_target_pairs={{0,1},{1,0},{2,3},{3,2},{4,5},{5,4},{6,7},{7,6},{8,9},{9,8},{10,11... | collective-permute-start | bytes 786440 | tf_op jit(solution)/shard_map/ppermute | solution.py:80
  44.7 1.8 %copy-start.19 = (bf16[1024,128]{1,0:T(8,128)(2,1)}, bf16[1024,128]{1,0:T(8,128)(2,1)S(1)}, u32[]{:S(2)}) copy-start(bf16[1024,128]{1,0:T(8,128)(2,1)S(1)} %collective-permute-done.11.refs_12_.refs_20_) | copy-start | bytes 786436
  44.7 1.7 %collective-permute-start.12 = (bf16[1024,128]{1,0:T(8,128)(2,1)S(1)}, bf16[1024,128]{1,0:T(8,128)(2,1)S(1)}, u32[]{:S(2)}, u32[]{:S(2)}) collective-permute-start(bf16[1024,128]{1,0:T(8,128)(2,1)S(1)} %collective-permute-done.11.refs_12_.refs_20_), channel_id=1, source_target_pairs={{0,1},{1,0},{2,3},{3,2},{4,5},{5,4},{6,7},{7,6},{8,9},{9,8},{10,11... | collective-permute-start | bytes 786440 | tf_op jit(solution)/shard_map/ppermute | solution.py:80
  55.6 5.5 %collective-permute-start.16 = (f32[8,1024]{1,0:T(8,128)}, f32[8,1024]{1,0:T(8,128)S(1)}, u32[]{:S(2)}, u32[]{:S(2)}) collective-permute-start(f32[8,1024]{1,0:T(8,128)} %get-tuple-element.34.refs_0_), channel_id=1, source_target_pairs={{0,6},{1,7},{2,0},{3,1},{4,2},{5,3},{6,4},{7,5},{8,14},{9,15},{10,... | collective-permute-start | bytes 98312 | tf_op jit(solution)/shard_map/ppermute | solution.py:80
  56.1 5.1 %collective-permute-start.15 = (f32[8,1024]{1,0:T(8,128)}, f32[8,1024]{1,0:T(8,128)S(1)}, u32[]{:S(2)}, u32[]{:S(2)}) collective-permute-start(f32[8,1024]{1,0:T(8,128)} %get-tuple-element.34.refs_0_), channel_id=1, source_target_pairs={{0,2},{1,3},{2,4},{3,5},{4,6},{5,7},{6,0},{7,1},{8,10},{9,11},{10,... | collective-permute-start | bytes 98312 | tf_op jit(solution)/shard_map/ppermute | solution.py:80
  59.1 5.6 %collective-permute-start.14 = (f32[8,1024]{1,0:T(8,128)}, f32[8,1024]{1,0:T(8,128)S(1)}, u32[]{:S(2)}, u32[]{:S(2)}) collective-permute-start(f32[8,1024]{1,0:T(8,128)} %get-tuple-element.34.refs_0_), channel_id=1, source_target_pairs={{0,4},{1,5},{2,6},{3,7},{4,0},{5,1},{6,2},{7,3},{8,12},{9,13},{10,... | collective-permute-start | bytes 98312 | tf_op jit(solution)/shard_map/ppermute | solution.py:80
  60.5 4.3 %collective-permute-start.17 = (f32[8,1024]{1,0:T(8,128)}, f32[8,1024]{1,0:T(8,128)S(1)}, u32[]{:S(2)}, u32[]{:S(2)}) collective-permute-start(f32[8,1024]{1,0:T(8,128)} %get-tuple-element.34.refs_0_), channel_id=1, source_target_pairs={{0,1},{1,0},{2,3},{3,2},{4,5},{5,4},{6,7},{7,6},{8,9},{9,8},{10,11... | collective-permute-start | bytes 98312 | tf_op jit(solution)/shard_map/ppermute | solution.py:80
  61.1 3.6 %collective-permute-start.20 = (f32[8,1024]{1,0:T(8,128)S(1)}, f32[8,1024]{1,0:T(8,128)S(1)}, u32[]{:S(2)}, u32[]{:S(2)}) collective-permute-start(f32[8,1024]{1,0:T(8,128)S(1)} %collective-permute-done.16.refs_3_), channel_id=1, source_target_pairs={{0,1},{1,0},{2,3},{3,2},{4,5},{5,4},{6,7},{7,6},{8,9},{9,8},{10,11... | collective-permute-start | bytes 98312 | tf_op jit(solution)/shard_map/ppermute | solution.py:80
  61.1 3.6 %collective-permute-start.19 = (f32[8,1024]{1,0:T(8,128)S(1)}, f32[8,1024]{1,0:T(8,128)S(1)}, u32[]{:S(2)}, u32[]{:S(2)}) collective-permute-start(f32[8,1024]{1,0:T(8,128)S(1)} %collective-permute-done.15.refs_2_), channel_id=1, source_target_pairs={{0,1},{1,0},{2,3},{3,2},{4,5},{5,4},{6,7},{7,6},{8,9},{9,8},{10,11... | collective-permute-start | bytes 98312 | tf_op jit(solution)/shard_map/ppermute | solution.py:80
  64.7 1.2 collective-permute-start.18
  77.4 3.9 %copy-start.26 = (bf16[1280,128]{1,0:T(8,128)(2,1)S(1)}, bf16[1280,128]{1,0:T(8,128)(2,1)}, u32[]{:S(2)}) copy-start(bf16[1280,128]{1,0:T(8,128)(2,1)} %get-tuple-element.37) | copy-start | bytes 983044
  77.5 5.9 %copy-start.25 = (bf16[1280,128]{1,0:T(8,128)(2,1)S(1)}, bf16[1280,128]{1,0:T(8,128)(2,1)}, u32[]{:S(2)}) copy-start(bf16[1280,128]{1,0:T(8,128)(2,1)} %get-tuple-element.38) | copy-start | bytes 983044
  77.5 6.0 %copy-start.29 = (bf16[640,128]{1,0:T(8,128)(2,1)S(1)}, bf16[640,128]{1,0:T(8,128)(2,1)}, u32[]{:S(2)}) copy-start(bf16[640,128]{1,0:T(8,128)(2,1)} %get-tuple-element.39) | copy-start | bytes 491524
  77.5 9.1 %copy-start.28 = (bf16[640,128]{1,0:T(8,128)(2,1)S(1)}, bf16[640,128]{1,0:T(8,128)(2,1)}, u32[]{:S(2)}) copy-start(bf16[640,128]{1,0:T(8,128)(2,1)} %get-tuple-element.40) | copy-start | bytes 491524
  77.5 21.0 %copy-start.27 = (bf16[640,128]{1,0:T(8,128)(2,1)S(1)}, bf16[640,128]{1,0:T(8,128)(2,1)}, u32[]{:S(2)}) copy-start(bf16[640,128]{1,0:T(8,128)(2,1)} %get-tuple-element.36) | copy-start | bytes 491524
  77.5 28.3 %copy-start.6 = (bf16[640,128]{1,0:T(8,128)(2,1)S(1)}, bf16[640,128]{1,0:T(8,128)(2,1)}, u32[]{:S(2)}) copy-start(bf16[640,128]{1,0:T(8,128)(2,1)} %get-tuple-element.35.refs_0_) | copy-start | bytes 491524
  77.5 35.1 %all-to-all-start.2 = ((bf16[16,80,512]{2,1,0:T(8,128)(2,1)}), bf16[16,80,512]{2,1,0:T(8,128)(2,1)S(1)}, u32[]{:S(2)}, u32[]{:S(2)}) async-start(bf16[16,80,512]{2,1,0:T(8,128)(2,1)} %get-tuple-element.43), calls=%async_computation.2 | async-start | bytes 2621440 | tf_op jit(solution)/shard_map/all_to_all | solution.py:431
  81.4 16.5 %collective-permute-start.22 = (bf16[1280,128]{1,0:T(8,128)(2,1)S(1)}, bf16[1280,128]{1,0:T(8,128)(2,1)S(1)}, u32[]{:S(2)}, u32[]{:S(2)}) collective-permute-start(bf16[1280,128]{1,0:T(8,128)(2,1)S(1)} %copy-done.26), channel_id=1, source_target_pairs={{0,2},{1,3},{2,4},{3,5},{4,6},{5,7},{6,0},{7,1},{8,10},{9,11},{10,... | collective-permute-start | bytes 983048 | tf_op jit(solution)/shard_map/ppermute | solution.py:80
  83.4 14.6 %collective-permute-start.24 = (bf16[1280,128]{1,0:T(8,128)(2,1)S(1)}, bf16[1280,128]{1,0:T(8,128)(2,1)S(1)}, u32[]{:S(2)}, u32[]{:S(2)}) collective-permute-start(bf16[1280,128]{1,0:T(8,128)(2,1)S(1)} %copy-done.25), channel_id=1, source_target_pairs={{0,6},{1,7},{2,0},{3,1},{4,2},{5,3},{6,4},{7,5},{8,14},{9,15},{10,... | collective-permute-start | bytes 983048 | tf_op jit(solution)/shard_map/ppermute | solution.py:80
  83.5 11.2 %collective-permute-start.26 = (bf16[640,128]{1,0:T(8,128)(2,1)S(1)}, bf16[640,128]{1,0:T(8,128)(2,1)S(1)}, u32[]{:S(2)}, u32[]{:S(2)}) collective-permute-start(bf16[640,128]{1,0:T(8,128)(2,1)S(1)} %copy-done.29), channel_id=1, source_target_pairs={{0,2},{1,3},{2,4},{3,5},{4,6},{5,7},{6,0},{7,1},{8,10},{9,11},{10,... | collective-permute-start | bytes 491528 | tf_op jit(solution)/shard_map/ppermute | solution.py:80
  86.6 11.3 %collective-permute-start.29 = (bf16[640,128]{1,0:T(8,128)(2,1)S(1)}, bf16[640,128]{1,0:T(8,128)(2,1)S(1)}, u32[]{:S(2)}, u32[]{:S(2)}) collective-permute-start(bf16[640,128]{1,0:T(8,128)(2,1)S(1)} %copy-done.28), channel_id=1, source_target_pairs={{0,6},{1,7},{2,0},{3,1},{4,2},{5,3},{6,4},{7,5},{8,14},{9,15},{10,... | collective-permute-start | bytes 491528 | tf_op jit(solution)/shard_map/ppermute | solution.py:80
  94.7 6.1 %collective-permute-start.27 = (bf16[640,128]{1,0:T(8,128)(2,1)S(1)}, bf16[640,128]{1,0:T(8,128)(2,1)S(1)}, u32[]{:S(2)}, u32[]{:S(2)}) collective-permute-start(bf16[640,128]{1,0:T(8,128)(2,1)S(1)} %collective-permute-done.26), channel_id=1, source_target_pairs={{0,2},{1,3},{2,4},{3,5},{4,6},{5,7},{6,0},{7,1},{8,10},{9,11},{10,... | collective-permute-start | bytes 491528 | tf_op jit(solution)/shard_map/ppermute | solution.py:80
  97.9 6.5 %collective-permute-start.30 = (bf16[640,128]{1,0:T(8,128)(2,1)S(1)}, bf16[640,128]{1,0:T(8,128)(2,1)S(1)}, u32[]{:S(2)}, u32[]{:S(2)}) collective-permute-start(bf16[640,128]{1,0:T(8,128)(2,1)S(1)} %collective-permute-done.29), channel_id=1, source_target_pairs={{0,6},{1,7},{2,0},{3,1},{4,2},{5,3},{6,4},{7,5},{8,14},{9,15},{10,... | collective-permute-start | bytes 491528 | tf_op jit(solution)/shard_map/ppermute | solution.py:80
  97.9 7.9 %collective-permute-start.23 = (bf16[1280,128]{1,0:T(8,128)(2,1)S(1)}, bf16[1280,128]{1,0:T(8,128)(2,1)S(1)}, u32[]{:S(2)}, u32[]{:S(2)}) collective-permute-start(bf16[1280,128]{1,0:T(8,128)(2,1)S(1)} %collective-permute-done.22.refs_2_), channel_id=1, source_target_pairs={{0,1},{1,0},{2,3},{3,2},{4,5},{5,4},{6,7},{7,6},{8,9},{9,8},{10,11... | collective-permute-start | bytes 983048 | tf_op jit(solution)/shard_map/ppermute | solution.py:80
  98.0 7.8 %collective-permute-start.25 = (bf16[1280,128]{1,0:T(8,128)(2,1)S(1)}, bf16[1280,128]{1,0:T(8,128)(2,1)S(1)}, u32[]{:S(2)}, u32[]{:S(2)}) collective-permute-start(bf16[1280,128]{1,0:T(8,128)(2,1)S(1)} %collective-permute-done.24.refs_4_), channel_id=1, source_target_pairs={{0,1},{1,0},{2,3},{3,2},{4,5},{5,4},{6,7},{7,6},{8,9},{9,8},{10,11... | collective-permute-start | bytes 983048 | tf_op jit(solution)/shard_map/ppermute | solution.py:80
  98.5 5.9 %collective-permute-start.21 = (bf16[640,128]{1,0:T(8,128)(2,1)S(1)}, bf16[640,128]{1,0:T(8,128)(2,1)S(1)}, u32[]{:S(2)}, u32[]{:S(2)}) collective-permute-start(bf16[640,128]{1,0:T(8,128)(2,1)S(1)} %copy-done.27), channel_id=1, source_target_pairs={{0,1},{1,0},{2,3},{3,2},{4,5},{5,4},{6,7},{7,6},{8,9},{9,8},{10,11... | collective-permute-start | bytes 491528 | tf_op jit(solution)/shard_map/ppermute | solution.py:80
  100.8 3.6 %collective-permute-start.28 = (bf16[640,128]{1,0:T(8,128)(2,1)S(1)}, bf16[640,128]{1,0:T(8,128)(2,1)S(1)}, u32[]{:S(2)}, u32[]{:S(2)}) collective-permute-start(bf16[640,128]{1,0:T(8,128)(2,1)S(1)} %collective-permute-done.27.refs_6_), channel_id=1, source_target_pairs={{0,1},{1,0},{2,3},{3,2},{4,5},{5,4},{6,7},{7,6},{8,9},{9,8},{10,11... | collective-permute-start | bytes 491528 | tf_op jit(solution)/shard_map/ppermute | solution.py:80
  104.4 1.4 %collective-permute-start.31 = (bf16[640,128]{1,0:T(8,128)(2,1)S(1)}, bf16[640,128]{1,0:T(8,128)(2,1)S(1)}, u32[]{:S(2)}, u32[]{:S(2)}) collective-permute-start(bf16[640,128]{1,0:T(8,128)(2,1)S(1)} %collective-permute-done.30.refs_8_), channel_id=1, source_target_pairs={{0,1},{1,0},{2,3},{3,2},{4,5},{5,4},{6,7},{7,6},{8,9},{9,8},{10,11... | collective-permute-start | bytes 491528 | tf_op jit(solution)/shard_map/ppermute | solution.py:80
  112.6 21.4 %copy-start.4 = (bf16[128,1024]{1,0:T(8,128)(2,1)S(1)}, bf16[128,1024]{1,0:T(8,128)(2,1)}, u32[]{:S(2)}) copy-start(bf16[128,1024]{1,0:T(8,128)(2,1)} %hist.3) | copy-start | bytes 786436
  112.6 21.4 %copy-start.5 = (bf16[128,1024]{1,0:T(8,128)(2,1)S(1)}, bf16[128,1024]{1,0:T(8,128)(2,1)}, u32[]{:S(2)}) copy-start(bf16[128,1024]{1,0:T(8,128)(2,1)} %gout.3) | copy-start | bytes 786436
  112.6 21.3 %all-to-all-start.1 = ((bf16[16,16,1024]{2,1,0:T(8,128)(2,1)}), bf16[16,16,1024]{2,1,0:T(8,128)(2,1)S(1)}, u32[]{:S(2)}, u32[]{:S(2)}) async-start(bf16[16,16,1024]{2,1,0:T(8,128)(2,1)} %bitcast.7), calls=%async_computation.1 | async-start | bytes 1048576 | tf_op jit(solution)/shard_map/all_to_all | solution.py:431
  121.6 9.2 %collective-permute-start.34 = (f32[16,512]{1,0:T(8,128)}, f32[16,512]{1,0:T(8,128)S(1)}, u32[]{:S(2)}, u32[]{:S(2)}) collective-permute-start(f32[16,512]{1,0:T(8,128)} %get-tuple-element.47), channel_id=1, source_target_pairs={{0,2},{1,3},{2,4},{3,5},{4,6},{5,7},{6,0},{7,1},{8,10},{9,11},{10,... | collective-permute-start | bytes 98312 | tf_op jit(solution)/shard_map/ppermute | solution.py:80
  121.8 11.6 %collective-permute-start.36 = (f32[16,512]{1,0:T(8,128)}, f32[16,512]{1,0:T(8,128)S(1)}, u32[]{:S(2)}, u32[]{:S(2)}) collective-permute-start(f32[16,512]{1,0:T(8,128)} %get-tuple-element.48), channel_id=1, source_target_pairs={{0,4},{1,5},{2,6},{3,7},{4,0},{5,1},{6,2},{7,3},{8,12},{9,13},{10,... | collective-permute-start | bytes 98312 | tf_op jit(solution)/shard_map/ppermute | solution.py:80
  122.4 11.0 %collective-permute-start.38 = (f32[16,512]{1,0:T(8,128)}, f32[16,512]{1,0:T(8,128)S(1)}, u32[]{:S(2)}, u32[]{:S(2)}) collective-permute-start(f32[16,512]{1,0:T(8,128)} %get-tuple-element.49), channel_id=1, source_target_pairs={{0,6},{1,7},{2,0},{3,1},{4,2},{5,3},{6,4},{7,5},{8,14},{9,15},{10,... | collective-permute-start | bytes 98312 | tf_op jit(solution)/shard_map/ppermute | solution.py:80
  123.6 12.3 %collective-permute-start.32 = (f32[8,1024]{1,0:T(8,128)}, f32[8,1024]{1,0:T(8,128)S(1)}, u32[]{:S(2)}, u32[]{:S(2)}) collective-permute-start(f32[8,1024]{1,0:T(8,128)} %get-tuple-element.44), channel_id=1, source_target_pairs={{0,0},{1,16},{2,32},{3,48},{4,64},{5,80},{6,96},{7,112},{8,1},{9,1... | collective-permute-start | bytes 98312 | tf_op jit(solution)/shard_map/ppermute | solution.py:517
  130.8 5.2 %collective-permute-start.35 = (f32[16,512]{1,0:T(8,128)S(1)}, f32[16,512]{1,0:T(8,128)S(1)}, u32[]{:S(2)}, u32[]{:S(2)}) collective-permute-start(f32[16,512]{1,0:T(8,128)S(1)} %collective-permute-done.34.refs_2_), channel_id=1, source_target_pairs={{0,1},{1,0},{2,3},{3,2},{4,5},{5,4},{6,7},{7,6},{8,9},{9,8},{10,11... | collective-permute-start | bytes 98312 | tf_op jit(solution)/shard_map/ppermute | solution.py:80
  133.4 2.6 %collective-permute-start.37 = (f32[16,512]{1,0:T(8,128)S(1)}, f32[16,512]{1,0:T(8,128)S(1)}, u32[]{:S(2)}, u32[]{:S(2)}) collective-permute-start(f32[16,512]{1,0:T(8,128)S(1)} %collective-permute-done.36.refs_4_), channel_id=1, source_target_pairs={{0,1},{1,0},{2,3},{3,2},{4,5},{5,4},{6,7},{7,6},{8,9},{9,8},{10,11... | collective-permute-start | bytes 98312 | tf_op jit(solution)/shard_map/ppermute | solution.py:80
  133.5 2.5 %collective-permute-start.39 = (f32[16,512]{1,0:T(8,128)S(1)}, f32[16,512]{1,0:T(8,128)S(1)}, u32[]{:S(2)}, u32[]{:S(2)}) collective-permute-start(f32[16,512]{1,0:T(8,128)S(1)} %collective-permute-done.38.refs_6_), channel_id=1, source_target_pairs={{0,1},{1,0},{2,3},{3,2},{4,5},{5,4},{6,7},{7,6},{8,9},{9,8},{10,11... | collective-permute-start | bytes 98312 | tf_op jit(solution)/shard_map/ppermute | solution.py:80
  133.9 2.0 %collective-permute-start.33 = (f32[8,512]{1,0:T(8,128)}, f32[8,512]{1,0:T(8,128)S(1)}, u32[]{:S(2)}, u32[]{:S(2)}) collective-permute-start(f32[8,512]{1,0:T(8,128)} %get-tuple-element.46), channel_id=1, source_target_pairs={{0,1},{1,0},{2,3},{3,2},{4,5},{5,4},{6,7},{7,6},{8,9},{9,8},{10,11... | collective-permute-start | bytes 49160 | tf_op jit(solution)/shard_map/ppermute | solution.py:80
  (9 other events, 9.6 us)
